TPU v7x, 256 devices: a whole 4x4x8 slice. The times are simulated.
256 devices in a mesh: seq: 64 (over y, x, z_hi, core), chan: 4 (over z_lo).
Axes of the slice: x: 4, y: 4, z: 8 (z_hi: 2, z_lo: 4; z = z_hi * 4 + z_lo), core: 2. Of those that a mesh axis runs over, the one named last changes fastest.
Arguments:
- signal: float32 [1024, 32768], P('chan', 'seq'), may hold values from -6 to 6
- gate: float32 [1024, 32768], P('chan', 'seq'), may hold values from -6 to 6
- filter_taps: float32 [1024, 32768], P('chan', 'seq'), may hold values from -2.5 to 2.5
- skip_weight: float32 [1024], P('chan'), may hold values from -1 to 1
- out_weight: bfloat16 [1024, 8192], P('chan'), may hold values from -0.1875 to 0.1875
Outputs:
- mixed: float32 [1024, 32768], P('chan', 'seq')
- projected: bfloat16 [32768, 8192], P(('seq', 'chan'))
All inputs are finite; a program needn't handle non-finite values.
Results may differ from a plain program's by a relative error of at most 0.023.
Values may be sent and summed in bfloat16 or wider, within the bound.
No kernel may reach another device: no remote copies, remote signals or barrier semaphores. Data moves between devices by JAX's collectives and lax.ppermute only.
A program may use at most 128 MiB of HBM per device.

v0:
```python
import jax
import jax.numpy as jnp
from jax import lax
from jax.sharding import PartitionSpec as P

exact_mode = lax.Precision.HIGHEST


def shortened(value):

    def short(part):
        return part.astype(jnp.bfloat16) if part.dtype == jnp.float32 else part

    return jax.tree.map(short, value)


def contract(form, left_arr, right_arr):
    return jnp.einsum(form, left_arr, right_arr, precision=exact_mode)


def phase_table(left_index, right_index, period):
    product = left_index[:, None] * right_index[None, :] % period
    phases = product.astype(jnp.float32) * (2.0 * jnp.pi / period)
    return (jnp.cos(phases), jnp.sin(phases))


def sequence_convolution(signal, filter_taps):
    shards = lax.axis_size("seq")
    channels, shard_len = signal.shape
    sub_block = shard_len // shards
    doubled = 2 * shards
    padded_len = doubled * shard_len
    my_index = lax.axis_index("seq")
    lay_signal = signal.T.reshape(1, shards, sub_block, channels)
    lay_filter = filter_taps.T.reshape(1, shards, sub_block, channels)
    cos_one, sin_one = phase_table(
        jnp.arange(shards, dtype=jnp.int32), jnp.arange(doubled, dtype=jnp.int32), doubled
    )
    cos_two, sin_two = phase_table(
        jnp.arange(shard_len, dtype=jnp.int32), jnp.arange(shard_len, dtype=jnp.int32), shard_len
    )
    signal_cols = lax.all_to_all(
        lay_signal.astype(jnp.bfloat16), "seq", split_axis=1, concat_axis=0, tiled=True
    ).astype(lay_signal.dtype)[:, 0]
    filter_cols = lax.all_to_all(
        lay_filter.astype(jnp.bfloat16), "seq", split_axis=1, concat_axis=0, tiled=True
    ).astype(lay_filter.dtype)[:, 0]
    local_pos = my_index * sub_block + jnp.arange(sub_block, dtype=jnp.int32)
    twiddle_cos, twiddle_sin = phase_table(
        jnp.arange(doubled, dtype=jnp.int32), local_pos, padded_len
    )
    twiddle_cos = twiddle_cos[:, :, None]
    twiddle_sin = twiddle_sin[:, :, None]

    def first_section(columns):
        real_one = contract("nmc,nf->fmc", columns, cos_one)
        imag_one = -contract("nmc,nf->fmc", columns, sin_one)
        return (
            real_one * twiddle_cos + imag_one * twiddle_sin,
            imag_one * twiddle_cos - real_one * twiddle_sin,
        )

    def second_section(real_in, imag_in):
        real_out = contract("fnc,ng->fgc", real_in, cos_two) + contract(
            "fnc,ng->fgc", imag_in, sin_two
        )
        imag_out = contract("fnc,ng->fgc", imag_in, cos_two) - contract(
            "fnc,ng->fgc", real_in, sin_two
        )
        return (real_out, imag_out)

    signal_real, signal_imag = first_section(signal_cols)
    filter_real, filter_imag = first_section(filter_cols)
    signal_real, signal_imag, filter_real, filter_imag = (
        lax.all_to_all(
            shortened(signal_real), "seq", split_axis=0, concat_axis=1, tiled=True
        ).astype(signal_real.dtype),
        lax.all_to_all(
            shortened(signal_imag), "seq", split_axis=0, concat_axis=1, tiled=True
        ).astype(signal_imag.dtype),
        lax.all_to_all(
            shortened(filter_real), "seq", split_axis=0, concat_axis=1, tiled=True
        ).astype(filter_real.dtype),
        lax.all_to_all(
            shortened(filter_imag), "seq", split_axis=0, concat_axis=1, tiled=True
        ).astype(filter_imag.dtype),
    )
    signal_real, signal_imag = second_section(signal_real, signal_imag)
    filter_real, filter_imag = second_section(filter_real, filter_imag)
    product_real = signal_real * filter_real - signal_imag * filter_imag
    product_imag = signal_real * filter_imag + signal_imag * filter_real
    back_real = contract("fgc,ng->fnc", product_real, cos_two) - contract(
        "fgc,ng->fnc", product_imag, sin_two
    )
    back_imag = contract("fgc,ng->fnc", product_imag, cos_two) + contract(
        "fgc,ng->fnc", product_real, sin_two
    )
    back_real, back_imag = (
        lax.all_to_all(shortened(back_real), "seq", split_axis=1, concat_axis=0, tiled=True).astype(
            back_real.dtype
        ),
        lax.all_to_all(shortened(back_imag), "seq", split_axis=1, concat_axis=0, tiled=True).astype(
            back_imag.dtype
        ),
    )
    turn_real = back_real * twiddle_cos - back_imag * twiddle_sin
    turn_imag = back_imag * twiddle_cos + back_real * twiddle_sin
    values = (
        contract("fmc,nf->nmc", turn_real, cos_one) - contract("fmc,nf->nmc", turn_imag, sin_one)
    ) / padded_len
    result = lax.all_to_all(
        shortened(values[:, None]), "seq", split_axis=0, concat_axis=2, tiled=True
    )
    return result[0, 0].T


def body(signal, gate, filter_taps, skip_weight, out_weight):
    convolved = sequence_convolution(signal, filter_taps)
    mixed = gate * (convolved + skip_weight[:, None] * signal)
    rounded = mixed.astype(jnp.bfloat16)
    projected = lax.psum_scatter(
        jnp.einsum("ct,cm->tm", rounded, out_weight, preferred_element_type=jnp.float32).astype(
            jnp.bfloat16
        ),
        "chan",
        scatter_dimension=0,
        tiled=True,
    )
    return (mixed, projected)


def solution(mesh):
    in_specs = (P("chan", "seq"), P("chan", "seq"), P("chan", "seq"), P("chan"), P("chan", None))
    out_specs = (P("chan", "seq"), P(("seq", "chan"), None))
    return jax.shard_map(body, mesh=mesh, in_specs=in_specs, out_specs=out_specs, check_vma=False)
```

profile of v0, /device:TPU:1, one launch (start us, length us, event | category | flops | bytes accessed | tf_op | source)
XLA Modules:
  0.0 436.3 jit_solution(8917469081325675415)
XLA Ops:
  7.2 1.2 copy.43
  9.1 15.6 %all-to-all-start = ((bf16[1,64,8,256]{3,2,0,1:T(8,128)(2,1)}), bf16[1,64,8,256]{3,2,0,1:T(8,128)(2,1)S(1)}, u32[]{:S(2)}, u32[]{:S(2)}) async-start(bf16[1,64,8,256]{3,2,0,1:T(8,128)(2,1)} %convert_bitcast_fusion.2), calls=%async_computation | async-start | bytes 524288 | tf_op jit(solution)/shard_map/all_to_all | solution.py:42
  24.8 1.9 copy.52
  26.7 12.1 %all-to-all-done = bf16[1,64,8,256]{3,2,0,1:T(8,128)(2,1)S(1)} async-done(((bf16[1,64,8,256]{3,2,0,1:T(8,128)(2,1)}), bf16[1,64,8,256]{3,2,0,1:T(8,128)(2,1)S(1)}, u32[]{:S(2)}, u32[]{:S(2)}) %all-to-all-start) | async-done | bytes 262176 | tf_op jit(solution)/shard_map/all_to_all | solution.py:42
  38.8 4.6 %all-to-all-start.3 = ((bf16[1,64,8,256]{3,2,0,1:T(8,128)(2,1)}), bf16[1,64,8,256]{3,2,0,1:T(8,128)(2,1)S(1)}, u32[]{:S(2)}, u32[]{:S(2)}) async-start(bf16[1,64,8,256]{3,2,0,1:T(8,128)(2,1)} %bitcast.141), calls=%async_computation.3 | async-start | bytes 524288 | tf_op jit(solution)/shard_map/all_to_all | solution.py:45
  43.5 0.8 convolution_negate_fusion.1
  45.0 12.5 %all-to-all-done.3 = bf16[1,64,8,256]{3,2,0,1:T(8,128)(2,1)S(1)} async-done(((bf16[1,64,8,256]{3,2,0,1:T(8,128)(2,1)}), bf16[1,64,8,256]{3,2,0,1:T(8,128)(2,1)S(1)}, u32[]{:S(2)}, u32[]{:S(2)}) %all-to-all-start.3) | async-done | bytes 262176 | tf_op jit(solution)/shard_map/all_to_all | solution.py:45
  57.5 0.8 convolution_negate_fusion
  58.3 2.3 subtract_convert_fusion
  60.5 1.1 copy.55
  61.6 4.5 %all-to-all-start.4 = ((bf16[128,8,256]{2,1,0:T(8,128)(2,1)}), bf16[128,8,256]{2,1,0:T(8,128)(2,1)S(1)}, u32[]{:S(2)}, u32[]{:S(2)}) async-start(bf16[128,8,256]{2,1,0:T(8,128)(2,1)} %copy.55), calls=%async_computation.4 | async-start | bytes 1048576 | tf_op jit(solution)/shard_map/all_to_all | solution.py:81
  66.1 2.2 copy.49
  68.3 14.8 %all-to-all-done.4 = bf16[128,8,256]{2,1,0:T(8,128)(2,1)S(1)} async-done(((bf16[128,8,256]{2,1,0:T(8,128)(2,1)}), bf16[128,8,256]{2,1,0:T(8,128)(2,1)S(1)}, u32[]{:S(2)}, u32[]{:S(2)}) %all-to-all-start.4) | async-done | bytes 524320 | tf_op jit(solution)/shard_map/all_to_all | solution.py:81
  83.0 5.8 %all-to-all-start.2 = ((bf16[128,8,256]{2,1,0:T(8,128)(2,1)}), bf16[128,8,256]{2,1,0:T(8,128)(2,1)S(1)}, u32[]{:S(2)}, u32[]{:S(2)}) async-start(bf16[128,8,256]{2,1,0:T(8,128)(2,1)} %copy.49), calls=%async_computation.2 | async-start | bytes 1048576 | tf_op jit(solution)/shard_map/all_to_all | solution.py:78
  88.9 1.1 copy.46
  90.0 15.7 %all-to-all-done.2 = bf16[128,8,256]{2,1,0:T(8,128)(2,1)S(1)} async-done(((bf16[128,8,256]{2,1,0:T(8,128)(2,1)}), bf16[128,8,256]{2,1,0:T(8,128)(2,1)S(1)}, u32[]{:S(2)}, u32[]{:S(2)}) %all-to-all-start.2) | async-done | bytes 524320 | tf_op jit(solution)/shard_map/all_to_all | solution.py:78
  105.7 5.9 %all-to-all-start.1 = ((bf16[128,8,256]{2,1,0:T(8,128)(2,1)}), bf16[128,8,256]{2,1,0:T(8,128)(2,1)S(1)}, u32[]{:S(2)}, u32[]{:S(2)}) async-start(bf16[128,8,256]{2,1,0:T(8,128)(2,1)} %copy.46), calls=%async_computation.1 | async-start | bytes 1048576 | tf_op jit(solution)/shard_map/all_to_all | solution.py:75
  111.6 1.1 copy.58
  112.7 15.7 %all-to-all-done.1 = bf16[128,8,256]{2,1,0:T(8,128)(2,1)S(1)} async-done(((bf16[128,8,256]{2,1,0:T(8,128)(2,1)}), bf16[128,8,256]{2,1,0:T(8,128)(2,1)S(1)}, u32[]{:S(2)}, u32[]{:S(2)}) %all-to-all-start.1) | async-done | bytes 524320 | tf_op jit(solution)/shard_map/all_to_all | solution.py:75
  128.4 6.5 %all-to-all-start.5 = ((bf16[128,8,256]{2,1,0:T(8,128)(2,1)}), bf16[128,8,256]{2,1,0:T(8,128)(2,1)S(1)}, u32[]{:S(2)}, u32[]{:S(2)}) async-start(bf16[128,8,256]{2,1,0:T(8,128)(2,1)} %copy.58), calls=%async_computation.5 | async-start | bytes 1048576 | tf_op jit(solution)/shard_map/all_to_all | solution.py:84
  134.9 4.8 %fusion.28 = f32[512,2,256]{2,0,1:T(8,128)S(1)} fusion(bf16[64,2,8,256]{3,2,1,0:T(8,128)(2,1)S(1)} %bitcast.155), kind=kOutput, calls=%fused_computation.41 | convolution fusion | flops 1614282752 | bytes 1572864 | tf_op jit(solution)/shard_map/fnc,ng->fgc/dot_general | solution.py:18
  139.7 5.8 %fusion.24 = f32[512,2,256]{2,0,1:T(8,128)} fusion(bf16[64,2,8,256]{3,2,1,0:T(8,128)(2,1)S(1)} %bitcast.157), kind=kOutput, calls=%fused_computation.37 | convolution fusion | flops 1614282752 | bytes 1572864 | tf_op jit(solution)/shard_map/fnc,ng->fgc/dot_general | solution.py:18
  145.5 5.8 %fusion.26 = f32[512,2,256]{2,0,1:T(8,128)} fusion(bf16[64,2,8,256]{3,2,1,0:T(8,128)(2,1)S(1)} %bitcast.153), kind=kOutput, calls=%fused_computation.39 | convolution fusion | flops 1614282752 | bytes 1572864 | tf_op jit(solution)/shard_map/fnc,ng->fgc/dot_general | solution.py:18
  151.3 6.0 %convolution_add_fusion.2 = f32[512,2,256]{2,0,1:T(8,128)} fusion(f32[512,2,256]{2,0,1:T(8,128)S(1)} %fusion.28, bf16[64,2,8,256]{3,2,1,0:T(8,128)(2,1)S(1)} %bitcast.158), kind=kOutput, calls=%fused_computation.10 | convolution fusion | flops 1614544896 | bytes 2621440 | tf_op jit(solution)/shard_map/fnc,ng->fgc/dot_general | solution.py:18
  157.3 4.8 %fusion.22 = f32[512,2,256]{2,0,1:T(8,128)S(1)} fusion(bf16[64,2,8,256]{3,2,1,0:T(8,128)(2,1)S(1)} %bitcast.159), kind=kOutput, calls=%fused_computation.35 | convolution fusion | flops 1614282752 | bytes 1572864 | tf_op jit(solution)/shard_map/fnc,ng->fgc/dot_general | solution.py:18
  162.1 4.8 %convolution_add_fusion.1 = f32[512,2,256]{2,0,1:T(8,128)S(1)} fusion(f32[512,2,256]{2,0,1:T(8,128)S(1)} %copy-done.9, bf16[64,2,8,256]{3,2,1,0:T(8,128)(2,1)S(1)} %bitcast.160), kind=kOutput, calls=%fused_computation.8 | convolution fusion | flops 1614544896 | bytes 2621440 | tf_op jit(solution)/shard_map/fnc,ng->fgc/dot_general | solution.py:18
  166.9 5.2 %convolution_subtract_fusion.1 = f32[512,2,256]{2,0,1:T(8,128)S(1)} fusion(f32[512,2,256]{2,0,1:T(8,128)S(1)} %fusion.22, bf16[64,2,8,256]{3,2,1,0:T(8,128)(2,1)S(1)} %bitcast.154), kind=kOutput, calls=%fused_computation.6 | convolution fusion | flops 1614544896 | bytes 2621440 | tf_op jit(solution)/shard_map/fnc,ng->fgc/dot_general | solution.py:18
  172.1 5.0 %multiply_subtract_fusion = (f32[512,2,256]{2,0,1:T(8,128)S(1)}, f32[512,2,256]{2,0,1:T(8,128)S(1)}) fusion(f32[512,2,256]{2,0,1:T(8,128)S(1)} %convolution_subtract_fusion.1, f32[512,2,256]{2,0,1:T(8,128)S(1)} %copy-done.5, f32[512,2,256]{2,0,1:T(8,128)S(1)} %convolution_add_fusion.1, f32[512,2,256]{2,0,1:T(8,128)S(1)} %copy-done.4, ...), kind=kOutput, calls=%fused_computation.55 | convolution fusion | flops 1616117760 | bytes 6815744 | tf_op jit(solution)/shard_map/fnc,ng->fgc/dot_general | solution.py:18
  177.1 5.9 %fusion.10 = f32[512,2,256]{2,0,1:T(8,128)S(1)} fusion(f32[512,2,256]{2,0,1:T(8,128)S(1)} %get-tuple-element.7), kind=kOutput, calls=%fused_computation.23 | convolution fusion | flops 1614282752 | bytes 2097152 | tf_op jit(solution)/shard_map/fgc,ng->fnc/dot_general | solution.py:18
  183.0 6.1 %fusion.2 = bf16[2,512,256]{2,1,0:T(8,128)(2,1)S(1)} fusion(f32[512,2,256]{2,0,1:T(8,128)S(1)} %fusion.10, f32[512,2,256]{2,0,1:T(8,128)S(1)} %get-tuple-element.6), kind=kOutput, calls=%fused_computation.14 | convolution fusion | flops 1614807040 | bytes 2621440 | tf_op jit(solution)/shard_map/fgc,ng->fnc/dot_general | solution.py:18
  189.1 1.3 copy.67
  190.5 12.7 %all-to-all-start.7 = ((bf16[2,512,256]{2,0,1:T(2,128)(2,1)}), bf16[2,512,256]{2,0,1:T(2,128)(2,1)S(1)}, u32[]{:S(2)}, u32[]{:S(2)}) async-start(bf16[2,512,256]{2,0,1:T(2,128)(2,1)} %copy.67), calls=%async_computation.7 | async-start | bytes 1048576 | tf_op jit(solution)/shard_map/all_to_all | solution.py:102
  203.2 6.9 %fusion.14 = f32[512,2,256]{2,0,1:T(8,128)S(1)} fusion(f32[512,2,256]{2,0,1:T(8,128)} %copy-done.8), kind=kOutput, calls=%fused_computation.27 | convolution fusion | flops 1614282752 | bytes 2097152 | tf_op jit(solution)/shard_map/fgc,ng->fnc/dot_general | solution.py:18
  210.2 6.1 %fusion.3 = bf16[2,512,256]{2,1,0:T(8,128)(2,1)S(1)} fusion(f32[512,2,256]{2,0,1:T(8,128)S(1)} %fusion.14, f32[512,2,256]{2,0,1:T(8,128)S(1)} %copy-done.7), kind=kOutput, calls=%fused_computation.15 | convolution fusion | flops 1614807040 | bytes 2621440 | tf_op jit(solution)/shard_map/fgc,ng->fnc/dot_general | solution.py:18
  216.3 1.3 copy.65
  217.6 2.4 all-to-all-done.7
  220.0 10.6 %all-to-all-start.6 = ((bf16[2,512,256]{2,0,1:T(2,128)(2,1)}), bf16[2,512,256]{2,0,1:T(2,128)(2,1)S(1)}, u32[]{:S(2)}, u32[]{:S(2)}) async-start(bf16[2,512,256]{2,0,1:T(2,128)(2,1)} %copy.65), calls=%async_computation.6 | async-start | bytes 1048576 | tf_op jit(solution)/shard_map/all_to_all | solution.py:99
  231.8 15.6 %all-to-all-done.6 = bf16[2,512,256]{2,0,1:T(2,128)(2,1)S(1)} async-done(((bf16[2,512,256]{2,0,1:T(2,128)(2,1)}), bf16[2,512,256]{2,0,1:T(2,128)(2,1)S(1)}, u32[]{:S(2)}, u32[]{:S(2)}) %all-to-all-start.6) | async-done | bytes 524320 | tf_op jit(solution)/shard_map/all_to_all | solution.py:99
  247.3 1.4 copy_bitcast_fusion.1
  248.7 2.0 reshape.111
  250.7 1.0 fusion.35
  251.7 1.0 fusion.6
  252.7 0.9 copy.69
  253.5 5.9 %all-to-all-start.8 = ((bf16[64,1,8,256]{3,2,1,0:T(8,128)(2,1)}), bf16[64,1,8,256]{3,2,1,0:T(8,128)(2,1)S(1)}, u32[]{:S(2)}, u32[]{:S(2)}) async-start(bf16[64,1,8,256]{3,2,1,0:T(8,128)(2,1)} %copy.69), calls=%async_computation.8 | async-start | bytes 524288 | tf_op jit(solution)/shard_map/all_to_all | solution.py:111
  259.7 13.6 %all-to-all-done.8 = bf16[64,1,8,256]{3,2,1,0:T(8,128)(2,1)S(1)} async-done(((bf16[64,1,8,256]{3,2,1,0:T(8,128)(2,1)}), bf16[64,1,8,256]{3,2,1,0:T(8,128)(2,1)S(1)}, u32[]{:S(2)}, u32[]{:S(2)}) %all-to-all-start.8) | async-done | bytes 262176 | tf_op jit(solution)/shard_map/all_to_all | solution.py:111
  273.5 7.8 %convolution_convert_fusion = bf16[512,8192]{1,0:T(8,128)(2,1)} fusion(bf16[256,8192]{1,0:T(8,128)(2,1)} %param.9, f32[256,512]{0,1:T(8,128)S(1)} %fusion.43), kind=kOutput, calls=%fused_computation | convolution fusion | flops 2151809024 | bytes 13107200 | tf_op jit(solution)/shard_map/ct,cm->tm/dot_general | solution.py:122
  281.3 1.0 copy.73
  282.3 147.0 %reduce-scatter.2.cloned.1.call-done = bf16[128,8192]{1,0:T(8,128)(2,1)} async-done(((bf16[512,8192]{1,0:T(8,128)(2,1)}), bf16[128,8192]{1,0:T(8,128)(2,1)}) %reduce-scatter.2.cloned.1.call-update) | async-done | bytes 2097168 | tf_op jit(solution)/shard_map/reduce_scatter | solution.py:121
  (31 shorter events, 3.1 us)
Async XLA Ops:
  9.1 29.6 %all-to-all-start = ((bf16[1,64,8,256]{3,2,0,1:T(8,128)(2,1)}), bf16[1,64,8,256]{3,2,0,1:T(8,128)(2,1)S(1)}, u32[]{:S(2)}, u32[]{:S(2)}) async-start(bf16[1,64,8,256]{3,2,0,1:T(8,128)(2,1)} %convert_bitcast_fusion.2), calls=%async_computation | async-start | bytes 524288 | tf_op jit(solution)/shard_map/all_to_all | solution.py:42
  38.8 18.7 %all-to-all-start.3 = ((bf16[1,64,8,256]{3,2,0,1:T(8,128)(2,1)}), bf16[1,64,8,256]{3,2,0,1:T(8,128)(2,1)S(1)}, u32[]{:S(2)}, u32[]{:S(2)}) async-start(bf16[1,64,8,256]{3,2,0,1:T(8,128)(2,1)} %bitcast.141), calls=%async_computation.3 | async-start | bytes 524288 | tf_op jit(solution)/shard_map/all_to_all | solution.py:45
  60.5 28.4 %copy-start.1 = (bf16[128,8,256]{2,0,1:T(8,128)(2,1)S(1)}, bf16[128,8,256]{2,0,1:T(8,128)(2,1)}, u32[]{:S(2)}) copy-start(bf16[128,8,256]{2,0,1:T(8,128)(2,1)} %get-tuple-element.13) | copy-start | bytes 1572868
  60.5 51.1 %copy-start = (bf16[128,8,256]{2,0,1:T(8,128)(2,1)S(1)}, bf16[128,8,256]{2,0,1:T(8,128)(2,1)}, u32[]{:S(2)}) copy-start(bf16[128,8,256]{2,0,1:T(8,128)(2,1)} %get-tuple-element.8) | copy-start | bytes 1572868
  61.6 21.4 %all-to-all-start.4 = ((bf16[128,8,256]{2,1,0:T(8,128)(2,1)}), bf16[128,8,256]{2,1,0:T(8,128)(2,1)S(1)}, u32[]{:S(2)}, u32[]{:S(2)}) async-start(bf16[128,8,256]{2,1,0:T(8,128)(2,1)} %copy.55), calls=%async_computation.4 | async-start | bytes 1048576 | tf_op jit(solution)/shard_map/all_to_all | solution.py:81
  83.0 22.6 %all-to-all-start.2 = ((bf16[128,8,256]{2,1,0:T(8,128)(2,1)}), bf16[128,8,256]{2,1,0:T(8,128)(2,1)S(1)}, u32[]{:S(2)}, u32[]{:S(2)}) async-start(bf16[128,8,256]{2,1,0:T(8,128)(2,1)} %copy.49), calls=%async_computation.2 | async-start | bytes 1048576 | tf_op jit(solution)/shard_map/all_to_all | solution.py:78
  105.7 22.7 %all-to-all-start.1 = ((bf16[128,8,256]{2,1,0:T(8,128)(2,1)}), bf16[128,8,256]{2,1,0:T(8,128)(2,1)S(1)}, u32[]{:S(2)}, u32[]{:S(2)}) async-start(bf16[128,8,256]{2,1,0:T(8,128)(2,1)} %copy.46), calls=%async_computation.1 | async-start | bytes 1048576 | tf_op jit(solution)/shard_map/all_to_all | solution.py:75
  128.4 28.9 %all-to-all-start.5 = ((bf16[128,8,256]{2,1,0:T(8,128)(2,1)}), bf16[128,8,256]{2,1,0:T(8,128)(2,1)S(1)}, u32[]{:S(2)}, u32[]{:S(2)}) async-start(bf16[128,8,256]{2,1,0:T(8,128)(2,1)} %copy.58), calls=%async_computation.5 | async-start | bytes 1048576 | tf_op jit(solution)/shard_map/all_to_all | solution.py:84
  157.3 4.8 %copy-start.9 = (f32[512,2,256]{2,0,1:T(8,128)S(1)}, f32[512,2,256]{2,0,1:T(8,128)}, u32[]{:S(2)}) copy-start(f32[512,2,256]{2,0,1:T(8,128)} %fusion.26) | copy-start | bytes 3145732
  166.9 5.2 %copy-start.4 = (f32[512,2,256]{2,0,1:T(8,128)S(1)}, f32[512,2,256]{2,0,1:T(8,128)}, u32[]{:S(2)}) copy-start(f32[512,2,256]{2,0,1:T(8,128)} %fusion.24) | copy-start | bytes 3145732
  166.9 5.2 %copy-start.5 = (f32[512,2,256]{2,0,1:T(8,128)S(1)}, f32[512,2,256]{2,0,1:T(8,128)}, u32[]{:S(2)}) copy-start(f32[512,2,256]{2,0,1:T(8,128)} %convolution_add_fusion.2) | copy-start | bytes 3145732
  177.1 5.9 %copy-start.6 = (f32[512,2,256]{2,0,1:T(8,128)}, f32[512,2,256]{2,0,1:T(8,128)S(1)}, u32[]{:S(2)}) copy-start(f32[512,2,256]{2,0,1:T(8,128)S(1)} %get-tuple-element.7) | copy-start | bytes 3145732
  177.1 5.9 %copy-start.8 = (f32[512,2,256]{2,0,1:T(8,128)}, f32[512,2,256]{2,0,1:T(8,128)S(1)}, u32[]{:S(2)}) copy-start(f32[512,2,256]{2,0,1:T(8,128)S(1)} %get-tuple-element.6) | copy-start | bytes 3145732
  189.1 21.0 %copy-start.7 = (f32[512,2,256]{2,0,1:T(8,128)S(1)}, f32[512,2,256]{2,0,1:T(8,128)}, u32[]{:S(2)}) copy-start(f32[512,2,256]{2,0,1:T(8,128)} %copy-done.6) | copy-start | bytes 3145732
  190.5 29.5 %all-to-all-start.7 = ((bf16[2,512,256]{2,0,1:T(2,128)(2,1)}), bf16[2,512,256]{2,0,1:T(2,128)(2,1)S(1)}, u32[]{:S(2)}, u32[]{:S(2)}) async-start(bf16[2,512,256]{2,0,1:T(2,128)(2,1)} %copy.67), calls=%async_computation.7 | async-start | bytes 1048576 | tf_op jit(solution)/shard_map/all_to_all | solution.py:102
  220.0 27.3 %all-to-all-start.6 = ((bf16[2,512,256]{2,0,1:T(2,128)(2,1)}), bf16[2,512,256]{2,0,1:T(2,128)(2,1)S(1)}, u32[]{:S(2)}, u32[]{:S(2)}) async-start(bf16[2,512,256]{2,0,1:T(2,128)(2,1)} %copy.65), calls=%async_computation.6 | async-start | bytes 1048576 | tf_op jit(solution)/shard_map/all_to_all | solution.py:99
  248.7 10.8 %copy-start.2 = (f32[256,512]{1,0:T(8,128)S(1)}, f32[256,512]{1,0:T(8,128)}, u32[]{:S(2)}) copy-start(f32[256,512]{1,0:T(8,128)} %param.6) | copy-start | bytes 1572868
  250.7 22.7 %copy-start.3 = (f32[256]{0:T(256)S(1)}, f32[256]{0:T(256)}, u32[]{:S(2)}) copy-start(f32[256]{0:T(256)} %param.8) | copy-start | bytes 3076
  253.5 19.8 %all-to-all-start.8 = ((bf16[64,1,8,256]{3,2,1,0:T(8,128)(2,1)}), bf16[64,1,8,256]{3,2,1,0:T(8,128)(2,1)S(1)}, u32[]{:S(2)}, u32[]{:S(2)}) async-start(bf16[64,1,8,256]{3,2,1,0:T(8,128)(2,1)} %copy.69), calls=%async_computation.8 | async-start | bytes 524288 | tf_op jit(solution)/shard_map/all_to_all | solution.py:111
  259.5 169.8 %reduce-scatter.2.cloned.1.call-start = ((), (), s32[]{:S(2)}) async-start(), calls=%async_computation.10 | async-start | bytes 10485760 | tf_op jit(solution)/shard_map/reduce_scatter | solution.py:121
Sparse Core Ops, SparseCore 0:
  281.4 147.8 reduce-scatter.1
where the time goes:
time: 445 us; the launch traced here: 436 us
  waiting for transfers between devices  249 us (56%)
  matrix products  81.3 us (18%)
  starting transfers between devices  72.3 us (16%)
  local copies, waits for them, and re-layouts  16 us (4%)
  between operations  14.6 us (3%)
    reduce_scatter x1, waiting for transfers between devices, body(): lax.psum_scatter(jnp.einsum('ct,cm->tm', rounded, out_weight, preferred_e...  147 us
    dot_general x18, matrix products, contract(): return jnp.einsum(form, left_arr, right_arr, precision=exact_mode)  73.5 us
    all_to_all x1, waiting for transfers between devices, sequence_convolution(): lax.all_to_all(shortened(signal_imag), 'seq', split_axis=0, concat_axis=1...  15.7 us
    all_to_all x1, waiting for transfers between devices, sequence_convolution(): lax.all_to_all(shortened(signal_real), 'seq', split_axis=0, concat_axis=1...  15.7 us
    all_to_all x1, starting transfers between devices, sequence_convolution(): lax.all_to_all(lay_signal.astype(jnp.bfloat16), 'seq', split_axis=1, conc...  15.6 us
    all_to_all x1, waiting for transfers between devices, sequence_convolution(): lax.all_to_all(shortened(back_real), 'seq', split_axis=1, concat_axis=0,...  15.6 us
    all_to_all x1, waiting for transfers between devices, sequence_convolution(): lax.all_to_all(shortened(filter_real), 'seq', split_axis=0, concat_axis=1...  14.8 us
    all_to_all x1, waiting for transfers between devices, sequence_convolution(): lax.all_to_all(shortened(values[:, None]), 'seq', split_axis=0, concat_ax...  13.6 us
  transfers between devices with their start and end apart: 10, of which 9 were waited for; matrix products, arithmetic and copies ran while one was open for 11% of the time, Pallas kernels for 0%

commit v1 on v0

v1 whole, which is shorter than its diff:
```python
import functools

import jax
import jax.numpy as jnp
import ml_dtypes
import numpy as np
from jax import lax
from jax.experimental import pallas as pl
from jax.experimental.pallas import tpu as pltpu
from jax.sharding import Mesh
from jax.sharding import PartitionSpec as P

AXES = ("y", "x", "zh", "core")
SEQ_DEVICES = 64
ROWS = 256
LANES = 128
POSITIONS = ROWS * LANES
OWN_CHANNELS = 4
PIECES = 4


def transform_tables():
    n1 = (np.arange(SEQ_DEVICES)[None, :] * PIECES + np.arange(PIECES)[:, None]).reshape(-1)
    k1 = np.arange(ROWS) + 0.25
    first = np.exp(-2j * np.pi * np.outer(k1, n1) / ROWS)
    n2 = np.arange(LANES)
    turn = np.exp(-2j * np.pi * np.outer(k1, n2) / POSITIONS)
    second = np.exp(-2j * np.pi * np.outer(n2, n2) / LANES)
    forward_one = np.concatenate([first.real, first.imag], 0)
    forward_two = np.block([[second.real, second.imag], [-second.imag, second.real]])
    back_two = np.block([[second.real, -second.imag], [second.imag, second.real]])
    back_one = np.concatenate([first.real.T, first.imag.T], 1)

    def narrow(table):
        return table.astype(np.float32).astype(ml_dtypes.bfloat16)

    return (
        narrow(forward_one),
        narrow(forward_two),
        narrow(back_two),
        narrow(back_one),
        turn.real.astype(np.float32),
        turn.imag.astype(np.float32),
    )


def pack_kernel(signal_ref, filter_ref, out_ref, wide):
    for which, source in enumerate((signal_ref, filter_ref)):
        for own in range(OWN_CHANNELS):
            for piece in range(PIECES):
                row = which * 16 + own * PIECES + piece
                wide[pl.ds(row, SEQ_DEVICES, stride=32), :] = source[
                    own * SEQ_DEVICES : (own + 1) * SEQ_DEVICES,
                    piece * LANES : (piece + 1) * LANES,
                ]
    out_ref[...] = wide[...].astype(jnp.bfloat16)


def matmul(left, right):
    return jnp.dot(left, right, preferred_element_type=jnp.float32)


def convolve_kernel(
    data_ref, one_ref, two_ref, back_two_ref, back_one_ref, cos_ref, sin_ref, out_ref, wide, result
):
    wide[...] = data_ref[...].astype(jnp.float32)
    columns = []
    for which in range(2):
        for own in range(OWN_CHANNELS):
            pieces = [
                wide[pl.ds(which * 16 + own * PIECES + piece, SEQ_DEVICES, stride=32), :]
                for piece in range(PIECES)
            ]
            columns.append(jnp.concatenate(pieces, axis=0).astype(jnp.bfloat16))
    turn_cos, turn_sin = cos_ref[...], sin_ref[...]

    def spectrum(column):
        part = matmul(one_ref[...], column)
        real, imag = part[:ROWS], part[ROWS:]
        turned = jnp.concatenate(
            [real * turn_cos - imag * turn_sin, real * turn_sin + imag * turn_cos], axis=1
        )
        both = matmul(turned.astype(jnp.bfloat16), two_ref[...])
        return both[:, :LANES], both[:, LANES:]

    for own in range(OWN_CHANNELS):
        signal_real, signal_imag = spectrum(columns[own])
        filter_real, filter_imag = spectrum(columns[OWN_CHANNELS + own])
        product = jnp.concatenate(
            [
                signal_real * filter_real - signal_imag * filter_imag,
                signal_real * filter_imag + signal_imag * filter_real,
            ],
            axis=1,
        )
        back = matmul(product.astype(jnp.bfloat16), back_two_ref[...])
        real, imag = back[:, :LANES], back[:, LANES:]
        turned = jnp.concatenate(
            [real * turn_cos + imag * turn_sin, imag * turn_cos - real * turn_sin], axis=0
        )
        values = matmul(back_one_ref[...], turned.astype(jnp.bfloat16)) * (1.0 / POSITIONS)
        for piece in range(PIECES):
            result[pl.ds(own * PIECES + piece, SEQ_DEVICES, stride=16), :] = values[
                piece * SEQ_DEVICES : (piece + 1) * SEQ_DEVICES
            ]
    out_ref[...] = result[...].astype(jnp.bfloat16)


def mix_kernel(conv_ref, signal_ref, gate_ref, skip_ref, mixed_ref, rounded_ref, wide):
    wide[...] = conv_ref[...].astype(jnp.float32)
    for own in range(OWN_CHANNELS):
        rows = slice(own * SEQ_DEVICES, (own + 1) * SEQ_DEVICES)
        skip = skip_ref[rows, :]
        for piece in range(PIECES):
            lanes = slice(piece * LANES, (piece + 1) * LANES)
            conv = wide[pl.ds(own * PIECES + piece, SEQ_DEVICES, stride=16), :]
            mixed = gate_ref[rows, lanes] * (conv + skip * signal_ref[rows, lanes])
            mixed_ref[rows, lanes] = mixed
            rounded_ref[piece, rows, :] = mixed.astype(jnp.bfloat16)


def call(kernel, out_shape, scratch, cost=None):
    return pl.pallas_call(
        kernel, out_shape=out_shape, scratch_shapes=scratch, cost_estimate=cost
    )


def gathered_weights(out_weight):
    half = out_weight.shape[1] // 2
    piece = half // 16
    place = lax.axis_index("y") * 4 + lax.axis_index("x")
    start = lax.axis_index("core") * half + place * piece
    mine = lax.dynamic_slice_in_dim(out_weight, start, piece, 1)
    depth = lax.all_gather(mine, "chan", axis=0, tiled=True)
    return lax.all_gather(depth, ("y", "x"), axis=0, tiled=False)


def body(signal, gate, filter_taps, skip_weight, out_weight):
    weights = gathered_weights(out_weight)
    tables = transform_tables()
    packed = call(
        pack_kernel,
        jax.ShapeDtypeStruct((SEQ_DEVICES * 32, LANES), jnp.bfloat16),
        [pltpu.VMEM((SEQ_DEVICES * 32, LANES), jnp.float32)],
    )(signal, filter_taps)
    arrived = lax.all_to_all(
        packed.reshape(SEQ_DEVICES, 32, LANES), AXES, split_axis=0, concat_axis=0, tiled=True
    )
    convolved = call(
        convolve_kernel,
        jax.ShapeDtypeStruct((SEQ_DEVICES * 16, LANES), jnp.bfloat16),
        [
            pltpu.VMEM((SEQ_DEVICES * 32, LANES), jnp.float32),
            pltpu.VMEM((SEQ_DEVICES * 16, LANES), jnp.float32),
        ],
    )(arrived.reshape(SEQ_DEVICES * 32, LANES), *tables)
    returned = lax.all_to_all(
        convolved.reshape(SEQ_DEVICES, 16, LANES), AXES, split_axis=0, concat_axis=0, tiled=True
    )
    channels, shard_len = signal.shape
    mixed, rounded = call(
        mix_kernel,
        (
            jax.ShapeDtypeStruct((channels, shard_len), jnp.float32),
            jax.ShapeDtypeStruct((PIECES, channels, LANES), jnp.bfloat16),
        ),
        [pltpu.VMEM((SEQ_DEVICES * 16, LANES), jnp.float32)],
    )(returned.reshape(SEQ_DEVICES * 16, LANES), signal, gate, skip_weight[:, None])
    mine = lax.all_to_all(rounded, "chan", split_axis=0, concat_axis=0, tiled=True)
    mine = mine.reshape(4 * channels, LANES)
    pair = [(0, 1), (1, 0)]
    theirs = lax.ppermute(mine, "core", pair)

    def project(columns):
        return (
            jnp.einsum("ct,gcm->tgm", columns, weights, preferred_element_type=jnp.float32)
            .astype(jnp.bfloat16)
            .reshape(LANES, -1)
        )

    for_them = project(theirs)
    from_them = lax.ppermute(for_them, "core", pair)
    own = project(mine)
    first_core = lax.axis_index("core") == 0
    projected = jnp.concatenate(
        [jnp.where(first_core, own, from_them), jnp.where(first_core, from_them, own)], axis=1
    )
    return mixed, projected


def solution(mesh):
    fine = Mesh(mesh.devices.reshape(4, 4, 2, 2, 4), (*AXES, "chan"))
    slab = P("chan", AXES)
    in_specs = (slab, slab, slab, P("chan"), P("chan", None))
    out_specs = (slab, P((*AXES, "chan"), None))
    return jax.shard_map(body, mesh=fine, in_specs=in_specs, out_specs=out_specs, check_vma=False)
```

time: 445 us -> 134 us (0.30); the launches traced: 436 us -> 134 us
  waiting for transfers between devices: 249 us -> 18.6 us
  matrix products: 81.3 us -> 9.32 us
  starting transfers between devices: 72.3 us -> 8.53 us
  blocking collectives: 0 us -> 63.7 us
  Pallas kernels: 0 us -> 11.4 us
  local copies, waits for them, and re-layouts: 16 us -> 7.44 us
    reduce_scatter x1 -> x0, waiting for transfers between devices: 147 us -> none  [body(): lax.psum_scatter(jnp.einsum('ct,cm->tm', rounded, out_weight, preferred_e...]
    all_to_all x9 -> x1, waiting for transfers between devices: 102 us -> 13.2 us  [body(): lax.all_to_all(convolved.reshape(SEQ_DEVICES, 16, LANES), AXES, split_axi...]
    dot_general x19 -> x2, matrix products: 81.3 us -> 9.32 us  [project(): jnp.einsum('ct,gcm->tgm', columns, weights, preferred_element_type=jnp.fl...]
    all_to_all x9 -> x1, starting transfers between devices: 72.3 us -> 5.04 us  [body(): lax.all_to_all(convolved.reshape(SEQ_DEVICES, 16, LANES), AXES, split_axi...]
    all_to_all x0 -> x2, blocking collectives: none -> 47 us  [the longest x1 33.8 us: body(): lax.all_to_all(packed.reshape(SEQ_DEVICES, 32, LANES), AXES, split_axis=0...]
    all_gather x0 -> x1, blocking collectives: none -> 16.7 us  [gathered_weights(): depth = lax.all_gather(mine, 'chan', axis=0, tiled=True)]
    pallas_call x0 -> x3, Pallas kernels: none -> 11.4 us  [the longest x1 5.91 us: body(): call(convolve_kernel, jax.ShapeDtypeStruct((SEQ_DEVICES * 16, LANES), jnp...]
    convert_element_type x9 -> x2, local copies, waits for them, and re-layouts: 11.7 us -> 1.97 us  [project(): return jnp.einsum('ct,gcm->tgm', columns, weights, preferred_element_type...]
  transfers between devices with their start and end apart: 10 -> 4, of which waited for: 9 -> 3; matrix products, arithmetic and copies ran while one was open for 11% -> 5% of each run, Pallas kernels for 0% -> 9%
where the time goes in v1:
time: 134 us
  blocking collectives  63.7 us (48%)
  waiting for transfers between devices  18.6 us (14%)
  between operations  14.1 us (11%)
  Pallas kernels  11.4 us (9%)
  matrix products  9.32 us (7%)
  starting transfers between devices  8.53 us (6%)
  local copies, waits for them, and re-layouts  7.44 us (6%)
    all_to_all x1, blocking collectives, body(): lax.all_to_all(packed.reshape(SEQ_DEVICES, 32, LANES), AXES, split_axis=0...  33.8 us
    all_gather x1, blocking collectives, gathered_weights(): depth = lax.all_gather(mine, 'chan', axis=0, tiled=True)  16.7 us
    all_to_all x1, blocking collectives, body(): lax.all_to_all(rounded, 'chan', split_axis=0, concat_axis=0, tiled=True)  13.2 us
    all_to_all x1, waiting for transfers between devices, body(): lax.all_to_all(convolved.reshape(SEQ_DEVICES, 16, LANES), AXES, split_axi...  13.2 us
    dot_general x2, matrix products, project(): jnp.einsum('ct,gcm->tgm', columns, weights, preferred_element_type=jnp.fl...  9.32 us
    pallas_call x1, Pallas kernels, body(): call(convolve_kernel, jax.ShapeDtypeStruct((SEQ_DEVICES * 16, LANES), jnp...  5.91 us
    all_to_all x1, starting transfers between devices, body(): lax.all_to_all(convolved.reshape(SEQ_DEVICES, 16, LANES), AXES, split_axi...  5.04 us
    all_gather x1, waiting for transfers between devices, gathered_weights(): return lax.all_gather(depth, ('y', 'x'), axis=0, tiled=False)  4.26 us
  transfers between devices with their start and end apart: 4, of which 3 were waited for; matrix products, arithmetic and copies ran while one was open for 5% of the time, Pallas kernels for 9%

profile of v1, /device:TPU:1, one launch (start us, length us, event | category | flops | bytes accessed | tf_op | source)
XLA Modules:
  0.0 133.5 jit_solution(469981785633922657)
XLA Ops:
  7.2 0.0 copy-start.1
  7.2 0.0 all-gather.3.cloned.1.call-start
  7.2 0.9 constant_dynamic-slice_fusion
  8.2 16.7 %all_gather.9 = bf16[1024,256]{1,0:T(8,128)(2,1)} all-gather(bf16[256,256]{1,0:T(8,128)(2,1)S(1)} %constant_dynamic-slice_fusion), channel_id=1, replica_groups=mesh['y'=4,'x'=4,'zh'=2,'core'=2,'chan'=4] {'chan'}, dimensions={0}, use_global_device_ids=true | all-gather | bytes 655360 | tf_op jit(solution)/shard_map/all_gather | solution.py:134
  24.9 0.0 all-gather.3.cloned.1.call-update
  24.9 3.1 %shard_map.122 = bf16[2048,128]{1,0:T(8,128)(2,1)} custom-call(f32[256,512]{1,0:T(8,128)} %signal_ref.3, f32[256,512]{1,0:T(8,128)} %filter_ref.1), custom_call_target="tpu_custom_call" | custom-call | tf_op jit(solution)/shard_map/pallas_call | solution.py:141
  28.0 33.8 %all_to_all.15 = bf16[64,32,128]{2,1,0:T(8,128)(2,1)} all-to-all(bf16[64,32,128]{2,1,0:T(8,128)(2,1)} %bitcast.24), channel_id=1, replica_groups=mesh['y'=4,'x'=4,'zh'=2,'core'=2,'chan'=4] {'y','x','zh','core'}, dimensions={0} | all-to-all | bytes 1048576 | tf_op jit(solution)/shard_map/all_to_all | solution.py:146
  61.8 5.9 %shard_map.123 = bf16[1024,128]{1,0:T(8,128)(2,1)} custom-call(bf16[2048,128]{1,0:T(8,128)(2,1)} %bitcast.23, bf16[512,256]{1,0:T(8,128)(2,1)} %constant.37.clone.one_ref, bf16[256,256]{1,0:T(8,128)(2,1)} %constant.38.clone.two_ref, bf16[256,256]{1,0:T(8,128)(2,1)} %constant.39.clone.back_two_ref, bf16[256,512]{1,0:T(8,128)(2,1)} %constant.40.clone.back_one_ref, ...), custom_call_target="tpu_custom_call" | custom-call | tf_op jit(solution)/shard_map/pallas_call | solution.py:149
  67.7 5.0 %all-to-all-start.1 = ((bf16[64,16,128]{2,1,0:T(8,128)(2,1)}), bf16[64,16,128]{2,1,0:T(8,128)(2,1)S(1)}, u32[]{:S(2)}, u32[]{:S(2)}) async-start(bf16[64,16,128]{2,1,0:T(8,128)(2,1)} %bitcast.25), calls=%async_computation.1 | async-start | bytes 524288 | tf_op jit(solution)/shard_map/all_to_all | solution.py:157
  72.7 0.0 copy-done.1
  72.7 0.8 copy.15.skip_ref
  73.5 13.2 %all-to-all-done.1 = bf16[64,16,128]{2,1,0:T(8,128)(2,1)S(1)} async-done(((bf16[64,16,128]{2,1,0:T(8,128)(2,1)}), bf16[64,16,128]{2,1,0:T(8,128)(2,1)S(1)}, u32[]{:S(2)}, u32[]{:S(2)}) %all-to-all-start.1) | async-done | bytes 262176 | tf_op jit(solution)/shard_map/all_to_all | solution.py:157
  86.7 0.0 copy-start
  86.7 0.7 copy-done
  87.4 2.4 %shard_map.124 = (f32[256,512]{1,0:T(8,128)}, bf16[4,256,128]{2,1,0:T(8,128)(2,1)}) custom-call(bf16[1024,128]{1,0:T(8,128)(2,1)} %bitcast.26, f32[256,512]{1,0:T(8,128)} %signal_ref.3, f32[256,512]{1,0:T(8,128)} %gate_ref.1, f32[256,1]{1,0:T(8,128)} %copy.15.skip_ref), custom_call_target="tpu_custom_call" | custom-call | tf_op jit(solution)/shard_map/pallas_call | solution.py:161
  89.9 13.2 %all_to_all.16 = bf16[4,256,128]{2,1,0:T(8,128)(2,1)S(1)} all-to-all(bf16[4,256,128]{2,1,0:T(8,128)(2,1)} %get-tuple-element.5), channel_id=1, replica_groups=mesh['y'=4,'x'=4,'zh'=2,'core'=2,'chan'=4] {'chan'}, dimensions={0} | all-to-all | bytes 524288 | tf_op jit(solution)/shard_map/all_to_all | solution.py:169
  103.1 0.1 copy.18
  103.2 2.8 %collective-permute-start = (bf16[1024,128]{0,1:T(8,128)(2,1)S(1)}, bf16[1024,128]{0,1:T(8,128)(2,1)S(1)}, u32[]{:S(2)}, u32[]{:S(2)}) collective-permute-start(bf16[1024,128]{0,1:T(8,128)(2,1)S(1)} %copy.18), channel_id=1, source_target_pairs={{0,4},{4,0},{1,5},{5,1},{2,6},{6,2},{3,7},{7,3},{8,12},{12,8},{9,1... | collective-permute-start | bytes 786440 | tf_op jit(solution)/shard_map/ppermute | solution.py:172
  106.0 1.2 collective-permute-done
  107.1 4.3 %all-gather.3.cloned.1.call-done = bf16[16384,256]{1,0:T(8,128)(2,1)} async-done(((bf16[1024,256]{1,0:T(8,128)(2,1)}), bf16[16384,256]{1,0:T(8,128)(2,1)}) %all-gather.3.cloned.1.call-update) | async-done | bytes 8388624 | tf_op jit(solution)/shard_map/all_gather | solution.py:135
  111.4 4.6 %convolution_convert_fusion = bf16[128,16,256]{2,0,1:T(8,128)(2,1)S(1)} fusion(bf16[16,1024,256]{2,1,0:T(8,128)(2,1)} %bitcast.19, bf16[1024,128]{0,1:T(8,128)(2,1)S(1)} %collective-permute-done), kind=kOutput, calls=%fused_computation.1 | convolution fusion | flops 1074266112 | bytes 9699328 | tf_op jit(solution)/shard_map/ct,gcm->tgm/dot_general | solution.py:176
  116.1 1.3 copy.19
  117.4 0.7 collective-permute-start.1
  118.0 4.7 %convolution_convert_fusion.1 = bf16[128,16,256]{2,0,1:T(8,128)(2,1)S(1)} fusion(bf16[1024,128,1]{1,0,2:T(8,128)(2,1)S(1)} %bitcast.22, bf16[16,1024,256]{2,1,0:T(8,128)(2,1)} %bitcast.20), kind=kOutput, calls=%fused_computation.2 | convolution fusion | flops 1074266112 | bytes 9699328 | tf_op jit(solution)/shard_map/ct,gcm->tgm/dot_general | solution.py:176
  122.7 0.7 copy.17
  123.4 0.0 collective-permute-done.1
  123.4 0.2 bitcast_select_fusion.1
  123.6 0.1 pad_maximum_fusion
  123.8 2.9 %copy.20 = bf16[128,8192]{1,0:T(8,128)(2,1)} copy(bf16[128,8192]{0,1:T(8,128)(2,1)S(1)} %pad_maximum_fusion) | data formatting | bytes 4194304
Async XLA Ops:
  7.2 65.5 %copy-start.1 = (f32[256]{0:T(256)S(1)}, f32[256]{0:T(256)}, u32[]{:S(2)}) copy-start(f32[256]{0:T(256)} %param.14) | copy-start | bytes 3076
  7.2 104.2 %all-gather.3.cloned.1.call-start = ((), (), s32[]{:S(2)}) async-start(), calls=%async_computation.3 | async-start | bytes 8912896 | tf_op jit(solution)/shard_map/all_gather | solution.py:135
  67.7 19.1 %all-to-all-start.1 = ((bf16[64,16,128]{2,1,0:T(8,128)(2,1)}), bf16[64,16,128]{2,1,0:T(8,128)(2,1)S(1)}, u32[]{:S(2)}, u32[]{:S(2)}) async-start(bf16[64,16,128]{2,1,0:T(8,128)(2,1)} %bitcast.25), calls=%async_computation.1 | async-start | bytes 524288 | tf_op jit(solution)/shard_map/all_to_all | solution.py:157
  86.7 0.7 copy-start
  103.2 3.9 %collective-permute-start = (bf16[1024,128]{0,1:T(8,128)(2,1)S(1)}, bf16[1024,128]{0,1:T(8,128)(2,1)S(1)}, u32[]{:S(2)}, u32[]{:S(2)}) collective-permute-start(bf16[1024,128]{0,1:T(8,128)(2,1)S(1)} %copy.18), channel_id=1, source_target_pairs={{0,4},{4,0},{1,5},{5,1},{2,6},{6,2},{3,7},{7,3},{8,12},{12,8},{9,1... | collective-permute-start | bytes 786440 | tf_op jit(solution)/shard_map/ppermute | solution.py:172
  117.4 6.0 %collective-permute-start.1 = (bf16[128,4096]{0,1:T(8,128)(2,1)}, bf16[128,4096]{0,1:T(8,128)(2,1)S(1)}, u32[]{:S(2)}, u32[]{:S(2)}) collective-permute-start(bf16[128,4096]{0,1:T(8,128)(2,1)} %bitcast.10), channel_id=1, source_target_pairs={{0,4},{4,0},{1,5},{5,1},{2,6},{6,2},{3,7},{7,3},{8,12},{12,8},{9,1... | collective-permute-start | bytes 3145736 | tf_op jit(solution)/shard_map/ppermute | solution.py:182
Sparse Core Ops, SparseCore 0:
  25.0 86.3 all-gather.2

commit v2 on v1

--- a/solution.py
+++ b/solution.py
@@ -1,4 +1,4 @@
-import functools
+import itertools
 
 import jax
 import jax.numpy as jnp
@@ -17,6 +17,9 @@
 POSITIONS = ROWS * LANES
 OWN_CHANNELS = 4
 PIECES = 4
+HALF = 4096
+QUARTER = 1024
+WORK = 10**11
 
 
 def transform_tables():
@@ -119,30 +122,147 @@
             rounded_ref[piece, rows, :] = mixed.astype(jnp.bfloat16)
 
 
-def call(kernel, out_shape, scratch, cost=None):
+def call(kernel, out_shape, scratch, limit=8, work=0, **options):
     return pl.pallas_call(
-        kernel, out_shape=out_shape, scratch_shapes=scratch, cost_estimate=cost
+        kernel,
+        out_shape=out_shape,
+        scratch_shapes=scratch,
+        compiler_params=pltpu.CompilerParams(vmem_limit_bytes=limit << 20),
+        cost_estimate=pl.CostEstimate(flops=work, bytes_accessed=0, transcendentals=0),
+        **options,
     )
 
 
-def gathered_weights(out_weight):
-    half = out_weight.shape[1] // 2
-    piece = half // 16
-    place = lax.axis_index("y") * 4 + lax.axis_index("x")
-    start = lax.axis_index("core") * half + place * piece
-    mine = lax.dynamic_slice_in_dim(out_weight, start, piece, 1)
-    depth = lax.all_gather(mine, "chan", axis=0, tiled=True)
-    return lax.all_gather(depth, ("y", "x"), axis=0, tiled=False)
+def device_pairs(move):
+    pairs = []
+    for y, x, z, core in itertools.product(range(4), range(4), range(8), range(2)):
+        spots = []
+        for sy, sx, sz, sc in ((y, x, z, core), move(y, x, z, core)):
+            sy, sx, sz = sy % 4, sx % 4, sz % 8
+            spots.append((((sy * 4 + sx) * 2 + sz // 4) * 2 + sc) * 4 + sz % 4)
+        pairs.append(tuple(spots))
+    return pairs
+
+
+def moved(array, move):
+    return lax.ppermute(array, (*AXES, "chan"), device_pairs(move))
+
+
+def colour():
+    return (lax.axis_index("x") + 2 * lax.axis_index("y")) % 4
+
+
+def join_kernel(below_ref, above_ref, far_ref, after_ref, out_ref, sem):
+    copies = [
+        pltpu.make_async_copy(ref, out_ref.at[pl.ds(index * ROWS, ROWS)], sem.at[index])
+        for index, ref in enumerate((below_ref, above_ref, far_ref))
+    ]
+    for copy in copies:
+        copy.start()
+    for copy in copies:
+        copy.wait()
+
+
+def keep_kernel(block_ref, after_ref, out_ref):
+    pass
+
+
+ANYWHERE = pl.BlockSpec(memory_space=pl.ANY)
+
+
+def ordered(block, after):
+    return call(
+        keep_kernel,
+        jax.ShapeDtypeStruct(block.shape, block.dtype),
+        [],
+        limit=4,
+        in_specs=[ANYWHERE] * 2,
+        out_specs=ANYWHERE,
+        input_output_aliases={0: 0},
+    )(block, after)
+
+
+def first_quarter(out_weight):
+    start = lax.axis_index("core") * HALF + colour() * QUARTER
+    mine = lax.dynamic_slice_in_dim(out_weight, start, QUARTER, 1)
+    below = moved(mine, lambda y, x, z, c: (y, x, z + 1, c))
+    above = moved(mine, lambda y, x, z, c: (y, x, z - 1, c))
+    far = moved(mine, lambda y, x, z, c: (y, x, z + 2 - 4 * c, c))
+    return below, above, far
+
+
+def other_quarters(parts, after):
+    block = call(
+        join_kernel,
+        jax.ShapeDtypeStruct((3 * ROWS, QUARTER), jnp.bfloat16),
+        [pltpu.SemaphoreType.DMA((3,))],
+        limit=4,
+        in_specs=[ANYWHERE] * 4,
+        out_specs=ANYWHERE,
+    )(*parts, after)
+    return [
+        block,
+        moved(block, lambda y, x, z, c: (y, x - 1, z, c)),
+        moved(block, lambda y, x, z, c: (y + 1 - 2 * c, x, z, c)),
+        moved(block, lambda y, x, z, c: (y, x + 1, z, c)),
+    ]
+
+
+def both_halves(blocks, after):
+    blocks = blocks[:1] + [ordered(block, after) for block in blocks[1:]]
+    return blocks + [moved(block, lambda y, x, z, c: (y, x, z, 1 - c)) for block in blocks]
+
+
+def project_kernel(columns_ref, own_ref, *refs):
+    block_refs, (out_ref, weights, results, own_sem, block_sem, out_sem) = refs[:8], refs[8:]
+    core, chan = lax.axis_index("core"), lax.axis_index("chan")
+    starts, loads = [], []
+    for index, block_ref in enumerate(block_refs):
+        half = core if index < 4 else 1 - core
+        start = pl.multiple_of(half * HALF + (colour() + index) % 4 * QUARTER, QUARTER)
+        pair = (
+            pltpu.make_async_copy(
+                own_ref.at[:, pl.ds(start, QUARTER)],
+                weights.at[index, pl.ds(0, ROWS)],
+                own_sem.at[index],
+            ),
+            pltpu.make_async_copy(
+                block_ref, weights.at[index, pl.ds(ROWS, 3 * ROWS)], block_sem.at[index]
+            ),
+        )
+        for load in pair:
+            load.start()
+        starts.append(start)
+        loads.append(pair)
+    rows = [
+        columns_ref[pl.ds(pl.multiple_of((chan + shift) % 4 * ROWS, ROWS), ROWS), :].T
+        for shift in (0, 3, 1, 2)
+    ]
+    left = jnp.concatenate(rows, axis=1)
+    stores = []
+    for index in range(8):
+        for load in loads[index]:
+            load.wait()
+        results[index] = matmul(left, weights[index]).astype(jnp.bfloat16)
+        store = pltpu.make_async_copy(
+            results.at[index], out_ref.at[:, pl.ds(starts[index], QUARTER)], out_sem.at[index]
+        )
+        store.start()
+        stores.append(store)
+    for store in stores:
+        store.wait()
 
 
 def body(signal, gate, filter_taps, skip_weight, out_weight):
-    weights = gathered_weights(out_weight)
+    parts = first_quarter(out_weight)
     tables = transform_tables()
     packed = call(
         pack_kernel,
         jax.ShapeDtypeStruct((SEQ_DEVICES * 32, LANES), jnp.bfloat16),
         [pltpu.VMEM((SEQ_DEVICES * 32, LANES), jnp.float32)],
+        work=WORK,
     )(signal, filter_taps)
+    blocks = other_quarters(parts, packed)
     arrived = lax.all_to_all(
         packed.reshape(SEQ_DEVICES, 32, LANES), AXES, split_axis=0, concat_axis=0, tiled=True
     )
@@ -153,7 +273,9 @@
             pltpu.VMEM((SEQ_DEVICES * 32, LANES), jnp.float32),
             pltpu.VMEM((SEQ_DEVICES * 16, LANES), jnp.float32),
         ],
+        work=WORK,
     )(arrived.reshape(SEQ_DEVICES * 32, LANES), *tables)
+    weights = both_halves(blocks, convolved)
     returned = lax.all_to_all(
         convolved.reshape(SEQ_DEVICES, 16, LANES), AXES, split_axis=0, concat_axis=0, tiled=True
     )
@@ -165,26 +287,24 @@
             jax.ShapeDtypeStruct((PIECES, channels, LANES), jnp.bfloat16),
         ),
         [pltpu.VMEM((SEQ_DEVICES * 16, LANES), jnp.float32)],
+        work=WORK,
     )(returned.reshape(SEQ_DEVICES * 16, LANES), signal, gate, skip_weight[:, None])
     mine = lax.all_to_all(rounded, "chan", split_axis=0, concat_axis=0, tiled=True)
-    mine = mine.reshape(4 * channels, LANES)
-    pair = [(0, 1), (1, 0)]
-    theirs = lax.ppermute(mine, "core", pair)
-
-    def project(columns):
-        return (
-            jnp.einsum("ct,gcm->tgm", columns, weights, preferred_element_type=jnp.float32)
-            .astype(jnp.bfloat16)
-            .reshape(LANES, -1)
-        )
-
-    for_them = project(theirs)
-    from_them = lax.ppermute(for_them, "core", pair)
-    own = project(mine)
-    first_core = lax.axis_index("core") == 0
-    projected = jnp.concatenate(
-        [jnp.where(first_core, own, from_them), jnp.where(first_core, from_them, own)], axis=1
-    )
+    width = out_weight.shape[1]
+    projected = call(
+        project_kernel,
+        jax.ShapeDtypeStruct((LANES, width), jnp.bfloat16),
+        [
+            pltpu.VMEM((8, 4 * ROWS, QUARTER), jnp.bfloat16),
+            pltpu.VMEM((8, LANES, QUARTER), jnp.bfloat16),
+            pltpu.SemaphoreType.DMA((8,)),
+            pltpu.SemaphoreType.DMA((8,)),
+            pltpu.SemaphoreType.DMA((8,)),
+        ],
+        limit=58,
+        in_specs=[pl.BlockSpec(memory_space=pltpu.VMEM)] + [ANYWHERE] * 9,
+        out_specs=ANYWHERE,
+    )(mine.reshape(4 * channels, LANES), out_weight, *weights)
     return mixed, projected
 
 

time: 134 us -> 125 us (0.933); the launches traced: 134 us -> 123 us
  blocking collectives: 63.7 us -> 11.4 us
  starting transfers between devices: 8.53 us -> 46.9 us
  waiting for transfers between devices: 18.6 us -> 37.5 us
  between operations: 14.1 us -> 0.94 us
  matrix products: 9.32 us -> 0 us
  Pallas kernels: 11.4 us -> 17.3 us
  local copies, waits for them, and re-layouts: 7.44 us -> 9.06 us
    ppermute x2 -> x10, waiting for transfers between devices: 1.16 us -> 36.8 us  [moved(): return lax.ppermute(array, (*AXES, 'chan'), device_pairs(move))]
    all_to_all x1 -> x0, blocking collectives: 33.8 us -> none  [body(): lax.all_to_all(packed.reshape(SEQ_DEVICES, 32, LANES), AXES, split_axis=0...]
    ppermute x2 -> x10, starting transfers between devices: 3.45 us -> 21.8 us  [moved(): return lax.ppermute(array, (*AXES, 'chan'), device_pairs(move))]
    all_gather x1 -> x0, blocking collectives: 16.7 us -> none  [gathered_weights(): depth = lax.all_gather(mine, 'chan', axis=0, tiled=True)]
    all_to_all x0 -> x1, starting transfers between devices: none -> 15.8 us  [body(): lax.all_to_all(packed.reshape(SEQ_DEVICES, 32, LANES), AXES, split_axis=0...]
    all_to_all x1, waiting for transfers between devices: 13.2 us -> 0.75 us  [body(): lax.all_to_all(convolved.reshape(SEQ_DEVICES, 16, LANES), AXES, split_axi...]
    dot_general x2 -> x0, matrix products: 9.32 us -> none  [project(): jnp.einsum('ct,gcm->tgm', columns, weights, preferred_element_type=jnp.fl...]
    pallas_call x0 -> x5, Pallas kernels: none -> 8.81 us  [the longest x1 8.67 us: body(): call(project_kernel, jax.ShapeDtypeStruct((LANES, width), jnp.bfloat16),...]
  transfers between devices with their start and end apart: 4 -> 12, of which waited for: 3 -> 4; matrix products, arithmetic and copies ran while one was open for 5% -> 1% of each run, Pallas kernels for 9% -> 5%
where the time goes in v2:
time: 125 us; the launch traced here: 123 us
  starting transfers between devices  46.9 us (38%)
  waiting for transfers between devices  37.5 us (30%)
  Pallas kernels  17.3 us (14%)
  blocking collectives  11.4 us (9%)
  local copies, waits for them, and re-layouts  9.06 us (7%)
    ppermute x10, waiting for transfers between devices, moved(): return lax.ppermute(array, (*AXES, 'chan'), device_pairs(move))  36.8 us
    ppermute x10, starting transfers between devices, moved(): return lax.ppermute(array, (*AXES, 'chan'), device_pairs(move))  21.8 us
    all_to_all x1, starting transfers between devices, body(): lax.all_to_all(packed.reshape(SEQ_DEVICES, 32, LANES), AXES, split_axis=0...  15.8 us
    all_to_all x1, blocking collectives, body(): lax.all_to_all(rounded, 'chan', split_axis=0, concat_axis=0, tiled=True)  11.4 us
    all_to_all x1, starting transfers between devices, body(): lax.all_to_all(convolved.reshape(SEQ_DEVICES, 16, LANES), AXES, split_axi...  9.3 us
    pallas_call x1, Pallas kernels, body(): call(project_kernel, jax.ShapeDtypeStruct((LANES, width), jnp.bfloat16),...  8.67 us
    unnamed x26, local copies, waits for them, and re-layouts  7.84 us
    pallas_call x1, Pallas kernels, body(): call(convolve_kernel, jax.ShapeDtypeStruct((SEQ_DEVICES * 16, LANES), jnp...  5.56 us
  transfers between devices with their start and end apart: 12, of which 4 were waited for; matrix products, arithmetic and copies ran while one was open for 1% of the time, Pallas kernels for 5%

profile of v2, /device:TPU:1, one launch (start us, length us, event | category | flops | bytes accessed | tf_op | source)
XLA Modules:
  0.0 123.1 jit_solution(13277932035975435420)
XLA Ops:
  0.6 0.0 copy-start.2
  0.6 1.0 copy-done.2
  1.7 1.0 copy-done.3
  2.7 1.9 %shard_map.122.after_ref = bf16[2048,128]{1,0:T(8,128)(2,1)} custom-call(f32[256,512]{1,0:T(8,128)S(1)} %copy-done.3, f32[256,512]{1,0:T(8,128)S(1)} %copy-done.2), custom_call_target="tpu_custom_call" | custom-call | flops 99999997952 | tf_op jit(solution)/shard_map/pallas_call | solution.py:259
  4.6 15.8 %all-to-all-start = ((bf16[64,32,128]{2,1,0:T(8,128)(2,1)}), bf16[64,32,128]{2,1,0:T(8,128)(2,1)}, u32[]{:S(2)}, u32[]{:S(2)}) async-start(bf16[64,32,128]{2,1,0:T(8,128)(2,1)} %bitcast), calls=%async_computation | async-start | bytes 1048576 | tf_op jit(solution)/shard_map/all_to_all | solution.py:266
  20.4 1.1 constant_dynamic-slice_fusion
  21.5 0.0 copy-start.6
  21.5 0.0 copy-start.8
  21.5 4.5 %collective-permute-start.2 = (bf16[256,1024]{1,0:T(8,128)(2,1)S(1)}, bf16[256,1024]{1,0:T(8,128)(2,1)S(1)}, u32[]{:S(2)}, u32[]{:S(2)}) collective-permute-start(bf16[256,1024]{1,0:T(8,128)(2,1)S(1)} %constant_dynamic-slice_fusion), channel_id=1, source_target_pairs={{0,2},{4,14},{1,3},{5,15},{2,8},{6,4},{3,9},{7,5},{8,10},{12,6},{9... | collective-permute-start | bytes 1572872 | tf_op jit(solution)/shard_map/ppermute | solution.py:148
  26.0 0.7 collective-permute-start.1
  26.8 0.7 collective-permute-start
  27.5 23.5 %collective-permute-done.2.far_ref = bf16[256,1024]{1,0:T(8,128)(2,1)S(1)} collective-permute-done((bf16[256,1024]{1,0:T(8,128)(2,1)S(1)}, bf16[256,1024]{1,0:T(8,128)(2,1)S(1)}, u32[]{:S(2)}, u32[]{:S(2)}) %collective-permute-start.2) | collective-permute-done | bytes 524320 | tf_op jit(solution)/shard_map/ppermute | solution.py:148
  51.0 4.8 %collective-permute-done.1.above_ref = bf16[256,1024]{1,0:T(8,128)(2,1)S(1)} collective-permute-done((bf16[256,1024]{1,0:T(8,128)(2,1)S(1)}, bf16[256,1024]{1,0:T(8,128)(2,1)S(1)}, u32[]{:S(2)}, u32[]{:S(2)}) %collective-permute-start.1) | collective-permute-done | bytes 524320 | tf_op jit(solution)/shard_map/ppermute | solution.py:148
  55.8 0.0 collective-permute-done.below_ref
  55.8 0.1 shard_map.125.refs_0_
  55.9 0.0 copy-start
  55.9 1.5 %collective-permute-start.5 = (bf16[768,1024]{1,0:T(8,128)(2,1)S(1)}, bf16[768,1024]{1,0:T(8,128)(2,1)}, u32[]{:S(2)}, u32[]{:S(2)}) collective-permute-start(bf16[768,1024]{1,0:T(8,128)(2,1)S(1)} %shard_map.125.refs_0_), channel_id=1, source_target_pairs={{0,16},{4,20},{1,17},{5,21},{2,18},{6,22},{3,19},{7,23},{8,24},{12... | collective-permute-start | bytes 4718600 | tf_op jit(solution)/shard_map/ppermute | solution.py:148
  57.4 2.6 %collective-permute-start.4 = (bf16[768,1024]{1,0:T(8,128)(2,1)S(1)}, bf16[768,1024]{1,0:T(8,128)(2,1)}, u32[]{:S(2)}, u32[]{:S(2)}) collective-permute-start(bf16[768,1024]{1,0:T(8,128)(2,1)S(1)} %shard_map.125.refs_0_), channel_id=1, source_target_pairs={{0,64},{4,196},{1,65},{5,197},{2,66},{6,198},{3,67},{7,199},{8,72}... | collective-permute-start | bytes 4718600 | tf_op jit(solution)/shard_map/ppermute | solution.py:148
  60.0 1.5 %collective-permute-start.3 = (bf16[768,1024]{1,0:T(8,128)(2,1)S(1)}, bf16[768,1024]{1,0:T(8,128)(2,1)S(1)}, u32[]{:S(2)}, u32[]{:S(2)}) collective-permute-start(bf16[768,1024]{1,0:T(8,128)(2,1)S(1)} %shard_map.125.refs_0_), channel_id=1, source_target_pairs={{0,48},{4,52},{1,49},{5,53},{2,50},{6,54},{3,51},{7,55},{8,56},{12... | collective-permute-start | bytes 4718600 | tf_op jit(solution)/shard_map/ppermute | solution.py:148
  61.5 0.0 all-to-all-done
  61.5 0.0 copy-done.6
  61.5 0.0 copy-done.8
  61.5 0.0 copy-start.7
  61.5 0.9 copy-done.7
  62.5 0.9 copy-done.9
  63.4 0.9 copy-done.10
  64.3 0.9 copy-done.11
  65.2 5.6 %shard_map.123.after_ref = bf16[1024,128]{1,0:T(8,128)(2,1)} custom-call(bf16[2048,128]{1,0:T(8,128)(2,1)} %bitcast.1.data_ref, bf16[512,256]{1,0:T(8,128)(2,1)S(1)} %copy-done.7, bf16[256,256]{1,0:T(8,128)(2,1)S(1)} %copy-done.11, bf16[256,256]{1,0:T(8,128)(2,1)S(1)} %copy-done.10, bf16[256,512]{1,0:T(8,128)(2,1)S(1)} %copy-done.6, ...), custom_call_target="tpu_custom_call" | custom-call | flops 99999997952 | tf_op jit(solution)/shard_map/pallas_call | solution.py:269
  70.7 9.3 %all-to-all-start.1 = ((bf16[64,16,128]{2,1,0:T(8,128)(2,1)}), bf16[64,16,128]{2,1,0:T(8,128)(2,1)S(1)}, u32[]{:S(2)}, u32[]{:S(2)}) async-start(bf16[64,16,128]{2,1,0:T(8,128)(2,1)} %bitcast.2), calls=%async_computation.1 | async-start | bytes 524288 | tf_op jit(solution)/shard_map/all_to_all | solution.py:279
  80.1 0.0 copy-done.12
  80.1 0.1 copy.16.skip_ref
  80.2 0.5 collective-permute-start.6
  80.8 8.5 %collective-permute-done.5.block_ref = bf16[768,1024]{1,0:T(8,128)(2,1)} collective-permute-done((bf16[768,1024]{1,0:T(8,128)(2,1)S(1)}, bf16[768,1024]{1,0:T(8,128)(2,1)}, u32[]{:S(2)}, u32[]{:S(2)}) %collective-permute-start.5) | collective-permute-done | bytes 1572896 | tf_op jit(solution)/shard_map/ppermute | solution.py:148
  89.2 7.0 %collective-permute-start.9 = (bf16[768,1024]{1,0:T(8,128)(2,1)}, bf16[768,1024]{1,0:T(8,128)(2,1)}, u32[]{:S(2)}, u32[]{:S(2)}) collective-permute-start(bf16[768,1024]{1,0:T(8,128)(2,1)} %shard_map.128.refs_3_), channel_id=1, source_target_pairs={{0,4},{4,0},{1,5},{5,1},{2,6},{6,2},{3,7},{7,3},{8,12},{12,8},{9,1... | collective-permute-start | bytes 4718600 | tf_op jit(solution)/shard_map/ppermute | solution.py:148
  96.2 0.0 collective-permute-done.4.block_ref
  96.2 0.1 collective-permute-start.8
  96.3 0.0 collective-permute-done.3.block_ref
  96.3 2.6 %collective-permute-start.7 = (bf16[768,1024]{1,0:T(8,128)(2,1)S(1)}, bf16[768,1024]{1,0:T(8,128)(2,1)}, u32[]{:S(2)}, u32[]{:S(2)}) collective-permute-start(bf16[768,1024]{1,0:T(8,128)(2,1)S(1)} %shard_map.126.refs_1_), channel_id=1, source_target_pairs={{0,4},{4,0},{1,5},{5,1},{2,6},{6,2},{3,7},{7,3},{8,12},{12,8},{9,1... | collective-permute-start | bytes 4718600 | tf_op jit(solution)/shard_map/ppermute | solution.py:148
  99.0 0.7 all-to-all-done.1
  99.7 1.0 copy-done.4
  100.7 1.0 copy-done.5
  101.8 1.0 shard_map.124
  102.8 11.4 %all_to_all.15 = bf16[4,256,128]{2,1,0:T(8,128)(2,1)} all-to-all(bf16[4,256,128]{2,1,0:T(8,128)(2,1)S(1)} %get-tuple-element.5), channel_id=1, replica_groups=mesh['y'=4,'x'=4,'zh'=2,'core'=2,'chan'=4] {'chan'}, dimensions={0} | all-to-all | bytes 524288 | tf_op jit(solution)/shard_map/all_to_all | solution.py:292
  114.2 0.0 collective-permute-done.6.refs_4_
  114.3 0.0 collective-permute-done.9.refs_7_
  114.3 0.0 collective-permute-done.8.refs_6_
  114.3 0.0 collective-permute-done.7.refs_5_
  114.3 8.7 %shard_map.129 = bf16[128,8192]{1,0:T(8,128)(2,1)} custom-call(bf16[1024,128]{1,0:T(8,128)(2,1)} %bitcast.7, bf16[256,8192]{1,0:T(8,128)(2,1)} %own_ref.1, bf16[768,1024]{1,0:T(8,128)(2,1)} %copy-done, bf16[768,1024]{1,0:T(8,128)(2,1)} %copy-done.1, bf16[768,1024]{1,0:T(8,128)(2,1)} %shard_map.127.refs_2_, bf16[768,1024]{1,0:T(8,128)(2,1)} %shard_map.128.refs_3_, ...), custom_call_target="tpu_custom_call" | custom-call | tf_op jit(solution)/shard_map/pallas_call | solution.py:294
  (13 shorter events, 0.0 us)
Async XLA Ops:
  0.6 1.0 copy-start.2
  1.7 1.0 copy-start.3
  4.6 56.9 %all-to-all-start = ((bf16[64,32,128]{2,1,0:T(8,128)(2,1)}), bf16[64,32,128]{2,1,0:T(8,128)(2,1)}, u32[]{:S(2)}, u32[]{:S(2)}) async-start(bf16[64,32,128]{2,1,0:T(8,128)(2,1)} %bitcast), calls=%async_computation | async-start | bytes 1048576 | tf_op jit(solution)/shard_map/all_to_all | solution.py:266
  21.5 40.0 %copy-start.6 = (bf16[256,512]{1,0:T(8,128)(2,1)S(1)}, bf16[256,512]{1,0:T(8,128)(2,1)}, u32[]{:S(2)}) copy-start(bf16[256,512]{1,0:T(8,128)(2,1)} %constant.52.clone.back_one_ref) | copy-start | bytes 786436
  21.5 40.0 %copy-start.8 = (f32[256,128]{1,0:T(8,128)S(1)}, f32[256,128]{1,0:T(8,128)}, u32[]{:S(2)}) copy-start(f32[256,128]{1,0:T(8,128)} %constant.54.clone.sin_ref) | copy-start | bytes 393220
  21.5 29.5 %collective-permute-start.2 = (bf16[256,1024]{1,0:T(8,128)(2,1)S(1)}, bf16[256,1024]{1,0:T(8,128)(2,1)S(1)}, u32[]{:S(2)}, u32[]{:S(2)}) collective-permute-start(bf16[256,1024]{1,0:T(8,128)(2,1)S(1)} %constant_dynamic-slice_fusion), channel_id=1, source_target_pairs={{0,2},{4,14},{1,3},{5,15},{2,8},{6,4},{3,9},{7,5},{8,10},{12,6},{9... | collective-permute-start | bytes 1572872 | tf_op jit(solution)/shard_map/ppermute | solution.py:148
  26.0 29.7 %collective-permute-start.1 = (bf16[256,1024]{1,0:T(8,128)(2,1)S(1)}, bf16[256,1024]{1,0:T(8,128)(2,1)S(1)}, u32[]{:S(2)}, u32[]{:S(2)}) collective-permute-start(bf16[256,1024]{1,0:T(8,128)(2,1)S(1)} %constant_dynamic-slice_fusion), channel_id=1, source_target_pairs={{0,11},{4,15},{1,0},{5,4},{2,1},{6,5},{3,2},{7,6},{8,3},{12,7},{9,... | collective-permute-start | bytes 1572872 | tf_op jit(solution)/shard_map/ppermute | solution.py:148
  26.8 29.0 %collective-permute-start = (bf16[256,1024]{1,0:T(8,128)(2,1)S(1)}, bf16[256,1024]{1,0:T(8,128)(2,1)S(1)}, u32[]{:S(2)}, u32[]{:S(2)}) collective-permute-start(bf16[256,1024]{1,0:T(8,128)(2,1)S(1)} %constant_dynamic-slice_fusion), channel_id=1, source_target_pairs={{0,1},{4,5},{1,2},{5,6},{2,3},{6,7},{3,8},{7,12},{8,9},{12,13},{9,... | collective-permute-start | bytes 1572872 | tf_op jit(solution)/shard_map/ppermute | solution.py:148
  55.9 24.3 %copy-start = (bf16[768,1024]{1,0:T(8,128)(2,1)}, bf16[768,1024]{1,0:T(8,128)(2,1)S(1)}, u32[]{:S(2)}) copy-start(bf16[768,1024]{1,0:T(8,128)(2,1)S(1)} %shard_map.125.refs_0_) | copy-start | bytes 4718596
  55.9 33.3 %collective-permute-start.5 = (bf16[768,1024]{1,0:T(8,128)(2,1)S(1)}, bf16[768,1024]{1,0:T(8,128)(2,1)}, u32[]{:S(2)}, u32[]{:S(2)}) collective-permute-start(bf16[768,1024]{1,0:T(8,128)(2,1)S(1)} %shard_map.125.refs_0_), channel_id=1, source_target_pairs={{0,16},{4,20},{1,17},{5,21},{2,18},{6,22},{3,19},{7,23},{8,24},{12... | collective-permute-start | bytes 4718600 | tf_op jit(solution)/shard_map/ppermute | solution.py:148
  57.4 38.8 %collective-permute-start.4 = (bf16[768,1024]{1,0:T(8,128)(2,1)S(1)}, bf16[768,1024]{1,0:T(8,128)(2,1)}, u32[]{:S(2)}, u32[]{:S(2)}) collective-permute-start(bf16[768,1024]{1,0:T(8,128)(2,1)S(1)} %shard_map.125.refs_0_), channel_id=1, source_target_pairs={{0,64},{4,196},{1,65},{5,197},{2,66},{6,198},{3,67},{7,199},{8,72}... | collective-permute-start | bytes 4718600 | tf_op jit(solution)/shard_map/ppermute | solution.py:148
  60.0 36.3 %collective-permute-start.3 = (bf16[768,1024]{1,0:T(8,128)(2,1)S(1)}, bf16[768,1024]{1,0:T(8,128)(2,1)S(1)}, u32[]{:S(2)}, u32[]{:S(2)}) collective-permute-start(bf16[768,1024]{1,0:T(8,128)(2,1)S(1)} %shard_map.125.refs_0_), channel_id=1, source_target_pairs={{0,48},{4,52},{1,49},{5,53},{2,50},{6,54},{3,51},{7,55},{8,56},{12... | collective-permute-start | bytes 4718600 | tf_op jit(solution)/shard_map/ppermute | solution.py:148
  61.5 1.0 copy-start.7
  62.5 0.9 copy-start.9
  63.4 0.9 copy-start.10
  64.3 0.9 copy-start.11
  65.2 14.9 %copy-start.12 = (f32[256]{0:T(256)S(1)}, f32[256]{0:T(256)}, u32[]{:S(2)}) copy-start(f32[256]{0:T(256)} %param.14) | copy-start | bytes 3076
  70.7 29.0 %all-to-all-start.1 = ((bf16[64,16,128]{2,1,0:T(8,128)(2,1)}), bf16[64,16,128]{2,1,0:T(8,128)(2,1)S(1)}, u32[]{:S(2)}, u32[]{:S(2)}) async-start(bf16[64,16,128]{2,1,0:T(8,128)(2,1)} %bitcast.2), calls=%async_computation.1 | async-start | bytes 524288 | tf_op jit(solution)/shard_map/all_to_all | solution.py:279
  80.2 34.0 %collective-permute-start.6 = (bf16[768,1024]{1,0:T(8,128)(2,1)S(1)}, bf16[768,1024]{1,0:T(8,128)(2,1)}, u32[]{:S(2)}, u32[]{:S(2)}) collective-permute-start(bf16[768,1024]{1,0:T(8,128)(2,1)S(1)} %shard_map.125.refs_0_), channel_id=1, source_target_pairs={{0,4},{4,0},{1,5},{5,1},{2,6},{6,2},{3,7},{7,3},{8,12},{12,8},{9,1... | collective-permute-start | bytes 4718600 | tf_op jit(solution)/shard_map/ppermute | solution.py:148
  89.2 25.0 %collective-permute-start.9 = (bf16[768,1024]{1,0:T(8,128)(2,1)}, bf16[768,1024]{1,0:T(8,128)(2,1)}, u32[]{:S(2)}, u32[]{:S(2)}) collective-permute-start(bf16[768,1024]{1,0:T(8,128)(2,1)} %shard_map.128.refs_3_), channel_id=1, source_target_pairs={{0,4},{4,0},{1,5},{5,1},{2,6},{6,2},{3,7},{7,3},{8,12},{12,8},{9,1... | collective-permute-start | bytes 4718600 | tf_op jit(solution)/shard_map/ppermute | solution.py:148
  96.2 18.0 %collective-permute-start.8 = (bf16[768,1024]{1,0:T(8,128)(2,1)}, bf16[768,1024]{1,0:T(8,128)(2,1)}, u32[]{:S(2)}, u32[]{:S(2)}) collective-permute-start(bf16[768,1024]{1,0:T(8,128)(2,1)} %shard_map.127.refs_2_), channel_id=1, source_target_pairs={{0,4},{4,0},{1,5},{5,1},{2,6},{6,2},{3,7},{7,3},{8,12},{12,8},{9,1... | collective-permute-start | bytes 4718600 | tf_op jit(solution)/shard_map/ppermute | solution.py:148
  96.3 6.5 %copy-start.1 = (bf16[768,1024]{1,0:T(8,128)(2,1)}, bf16[768,1024]{1,0:T(8,128)(2,1)S(1)}, u32[]{:S(2)}) copy-start(bf16[768,1024]{1,0:T(8,128)(2,1)S(1)} %shard_map.126.refs_1_) | copy-start | bytes 4718596
  96.3 17.9 %collective-permute-start.7 = (bf16[768,1024]{1,0:T(8,128)(2,1)S(1)}, bf16[768,1024]{1,0:T(8,128)(2,1)}, u32[]{:S(2)}, u32[]{:S(2)}) collective-permute-start(bf16[768,1024]{1,0:T(8,128)(2,1)S(1)} %shard_map.126.refs_1_), channel_id=1, source_target_pairs={{0,4},{4,0},{1,5},{5,1},{2,6},{6,2},{3,7},{7,3},{8,12},{12,8},{9,1... | collective-permute-start | bytes 4718600 | tf_op jit(solution)/shard_map/ppermute | solution.py:148
  99.7 1.0 copy-start.4
  100.7 1.0 copy-start.5

commit v3 on v2

--- a/solution.py
+++ b/solution.py
@@ -19,7 +19,10 @@
 PIECES = 4
 HALF = 4096
 QUARTER = 1024
+SPLIT = 384
 WORK = 10**11
+PACK_WORK = 10**10
+JOIN_WORK = 10**10
 
 
 def transform_tables():
@@ -47,7 +50,7 @@
     )
 
 
-def pack_kernel(signal_ref, filter_ref, out_ref, wide):
+def pack_kernel(signal_ref, filter_ref, after_ref, out_ref, wide):
     for which, source in enumerate((signal_ref, filter_ref)):
         for own in range(OWN_CHANNELS):
             for piece in range(PIECES):
@@ -122,7 +125,7 @@
             rounded_ref[piece, rows, :] = mixed.astype(jnp.bfloat16)
 
 
-def call(kernel, out_shape, scratch, limit=8, work=0, **options):
+def call(kernel, out_shape, scratch, limit=60, work=0, **options):
     return pl.pallas_call(
         kernel,
         out_shape=out_shape,
@@ -148,8 +151,9 @@
     return lax.ppermute(array, (*AXES, "chan"), device_pairs(move))
 
 
-def colour():
-    return (lax.axis_index("x") + 2 * lax.axis_index("y")) % 4
+def colour(core):
+    x, y = lax.axis_index("x"), lax.axis_index("y")
+    return jnp.where(core == 0, x + 2 * y, 2 * x + y) % 4
 
 
 def join_kernel(below_ref, above_ref, far_ref, after_ref, out_ref, sem):
@@ -175,7 +179,7 @@
         keep_kernel,
         jax.ShapeDtypeStruct(block.shape, block.dtype),
         [],
-        limit=4,
+        limit=2,
         in_specs=[ANYWHERE] * 2,
         out_specs=ANYWHERE,
         input_output_aliases={0: 0},
@@ -183,12 +187,13 @@
 
 
 def first_quarter(out_weight):
-    start = lax.axis_index("core") * HALF + colour() * QUARTER
+    core = lax.axis_index("core")
+    start = core * HALF + colour(core) * QUARTER
     mine = lax.dynamic_slice_in_dim(out_weight, start, QUARTER, 1)
     below = moved(mine, lambda y, x, z, c: (y, x, z + 1, c))
     above = moved(mine, lambda y, x, z, c: (y, x, z - 1, c))
     far = moved(mine, lambda y, x, z, c: (y, x, z + 2 - 4 * c, c))
-    return below, above, far
+    return mine, (below, above, far)
 
 
 def other_quarters(parts, after):
@@ -196,15 +201,18 @@
         join_kernel,
         jax.ShapeDtypeStruct((3 * ROWS, QUARTER), jnp.bfloat16),
         [pltpu.SemaphoreType.DMA((3,))],
-        limit=4,
+        limit=2,
+        work=JOIN_WORK,
         in_specs=[ANYWHERE] * 4,
         out_specs=ANYWHERE,
     )(*parts, after)
+    upper, lower = block[:SPLIT], block[SPLIT:]
     return [
         block,
-        moved(block, lambda y, x, z, c: (y, x - 1, z, c)),
-        moved(block, lambda y, x, z, c: (y + 1 - 2 * c, x, z, c)),
-        moved(block, lambda y, x, z, c: (y, x + 1, z, c)),
+        moved(block, lambda y, x, z, c: (y - c, x - 1 + c, z, c)),
+        moved(upper, lambda y, x, z, c: (y + 1 - c, x + c, z, c)),
+        moved(lower, lambda y, x, z, c: (y - 1 + c, x - c, z, c)),
+        moved(block, lambda y, x, z, c: (y + c, x + 1 - c, z, c)),
     ]
 
 
@@ -214,54 +222,45 @@
 
 
 def project_kernel(columns_ref, own_ref, *refs):
-    block_refs, (out_ref, weights, results, own_sem, block_sem, out_sem) = refs[:8], refs[8:]
+    block_refs, (out_ref, results, out_sem) = refs[:10], refs[10:]
     core, chan = lax.axis_index("core"), lax.axis_index("chan")
-    starts, loads = [], []
-    for index, block_ref in enumerate(block_refs):
-        half = core if index < 4 else 1 - core
-        start = pl.multiple_of(half * HALF + (colour() + index) % 4 * QUARTER, QUARTER)
-        pair = (
-            pltpu.make_async_copy(
-                own_ref.at[:, pl.ds(start, QUARTER)],
-                weights.at[index, pl.ds(0, ROWS)],
-                own_sem.at[index],
-            ),
-            pltpu.make_async_copy(
-                block_ref, weights.at[index, pl.ds(ROWS, 3 * ROWS)], block_sem.at[index]
-            ),
-        )
-        for load in pair:
-            load.start()
-        starts.append(start)
-        loads.append(pair)
     rows = [
         columns_ref[pl.ds(pl.multiple_of((chan + shift) % 4 * ROWS, ROWS), ROWS), :].T
         for shift in (0, 3, 1, 2)
     ]
-    left = jnp.concatenate(rows, axis=1)
+    own_columns, columns = rows[0], jnp.concatenate(rows[1:], axis=1)
     stores = []
-    for index in range(8):
-        for load in loads[index]:
-            load.wait()
-        results[index] = matmul(left, weights[index]).astype(jnp.bfloat16)
-        store = pltpu.make_async_copy(
-            results.at[index], out_ref.at[:, pl.ds(starts[index], QUARTER)], out_sem.at[index]
-        )
-        store.start()
-        stores.append(store)
+    for half in range(2):
+        owner = core if half == 0 else 1 - core
+        for step, parts in enumerate(((0,), (1,), (2, 3), (4,))):
+            index = 4 * half + step
+            start = pl.multiple_of(owner * HALF + (colour(owner) + step) % 4 * QUARTER, QUARTER)
+            total = matmul(own_columns, own_ref[:, pl.ds(start, QUARTER)])
+            row = 0
+            for part in parts:
+                block = block_refs[5 * half + part][...]
+                total += matmul(columns[:, row : row + block.shape[0]], block)
+                row += block.shape[0]
+            results[index] = total.astype(jnp.bfloat16)
+            store = pltpu.make_async_copy(
+                results.at[index], out_ref.at[:, pl.ds(start, QUARTER)], out_sem.at[index]
+            )
+            store.start()
+            stores.append(store)
     for store in stores:
         store.wait()
 
 
 def body(signal, gate, filter_taps, skip_weight, out_weight):
-    parts = first_quarter(out_weight)
+    mine, parts = first_quarter(out_weight)
     tables = transform_tables()
     packed = call(
         pack_kernel,
         jax.ShapeDtypeStruct((SEQ_DEVICES * 32, LANES), jnp.bfloat16),
         [pltpu.VMEM((SEQ_DEVICES * 32, LANES), jnp.float32)],
-        work=WORK,
-    )(signal, filter_taps)
+        work=PACK_WORK,
+        in_specs=[pl.BlockSpec(memory_space=pltpu.VMEM)] * 2 + [ANYWHERE],
+    )(signal, filter_taps, mine)
     blocks = other_quarters(parts, packed)
     arrived = lax.all_to_all(
         packed.reshape(SEQ_DEVICES, 32, LANES), AXES, split_axis=0, concat_axis=0, tiled=True
@@ -295,14 +294,11 @@
         project_kernel,
         jax.ShapeDtypeStruct((LANES, width), jnp.bfloat16),
         [
-            pltpu.VMEM((8, 4 * ROWS, QUARTER), jnp.bfloat16),
             pltpu.VMEM((8, LANES, QUARTER), jnp.bfloat16),
             pltpu.SemaphoreType.DMA((8,)),
-            pltpu.SemaphoreType.DMA((8,)),
-            pltpu.SemaphoreType.DMA((8,)),
         ],
-        limit=58,
-        in_specs=[pl.BlockSpec(memory_space=pltpu.VMEM)] + [ANYWHERE] * 9,
+        limit=30,
+        in_specs=[pl.BlockSpec(memory_space=pltpu.VMEM)] * 12,
         out_specs=ANYWHERE,
     )(mine.reshape(4 * channels, LANES), out_weight, *weights)
     return mixed, projected

time: 125 us -> 105 us (0.84)
  starting transfers between devices: 46.9 us -> 34.5 us
  waiting for transfers between devices: 37.5 us -> 30.4 us
  Pallas kernels: 17.3 us -> 18.6 us
    ppermute x10 -> x12, waiting for transfers between devices: 36.8 us -> 25.8 us  [moved(): return lax.ppermute(array, (*AXES, 'chan'), device_pairs(move))]
    ppermute x10 -> x12, starting transfers between devices: 21.8 us -> 14.5 us  [moved(): return lax.ppermute(array, (*AXES, 'chan'), device_pairs(move))]
    all_to_all x1, starting transfers between devices: 15.8 us -> 11.2 us  [body(): lax.all_to_all(packed.reshape(SEQ_DEVICES, 32, LANES), AXES, split_axis=0...]
    all_to_all x1, waiting for transfers between devices: 0.75 us -> 4.57 us  [body(): lax.all_to_all(convolved.reshape(SEQ_DEVICES, 16, LANES), AXES, split_axi...]
    unnamed x26 -> x14, local copies, waits for them, and re-layouts: 7.84 us -> 4.89 us
    pallas_call x1, Pallas kernels: 8.67 us -> 7.08 us  [body(): call(project_kernel, jax.ShapeDtypeStruct((LANES, width), jnp.bfloat16),...]
    pallas_call x1, Pallas kernels: 1.03 us -> 2.41 us  [body(): call(mix_kernel, (jax.ShapeDtypeStruct((channels, shard_len), jnp.float32...]
    slice x0 -> x1, local copies, waits for them, and re-layouts: none -> 1.26 us  [other_quarters(): upper, lower = (block[:SPLIT], block[SPLIT:])]
  transfers between devices with their start and end apart: 12 -> 14, of which waited for: 4 -> 7; matrix products, arithmetic and copies ran while one was open for 1% -> 2% of each run, Pallas kernels for 5% -> 11%
where the time goes in v3:
time: 105 us; the launch traced here: 104 us
  starting transfers between devices  34.5 us (33%)
  waiting for transfers between devices  30.4 us (29%)
  Pallas kernels  18.6 us (18%)
  blocking collectives  11.2 us (11%)
  local copies, waits for them, and re-layouts  8.03 us (8%)
    ppermute x12, waiting for transfers between devices, moved(): return lax.ppermute(array, (*AXES, 'chan'), device_pairs(move))  25.8 us
    ppermute x12, starting transfers between devices, moved(): return lax.ppermute(array, (*AXES, 'chan'), device_pairs(move))  14.5 us
    all_to_all x1, blocking collectives, body(): lax.all_to_all(rounded, 'chan', split_axis=0, concat_axis=0, tiled=True)  11.2 us
    all_to_all x1, starting transfers between devices, body(): lax.all_to_all(packed.reshape(SEQ_DEVICES, 32, LANES), AXES, split_axis=0...  11.2 us
    all_to_all x1, starting transfers between devices, body(): lax.all_to_all(convolved.reshape(SEQ_DEVICES, 16, LANES), AXES, split_axi...  8.84 us
    pallas_call x1, Pallas kernels, body(): call(project_kernel, jax.ShapeDtypeStruct((LANES, width), jnp.bfloat16),...  7.08 us
    pallas_call x1, Pallas kernels, body(): call(convolve_kernel, jax.ShapeDtypeStruct((SEQ_DEVICES * 16, LANES), jnp...  5.92 us
    unnamed x14, local copies, waits for them, and re-layouts  4.89 us
  transfers between devices with their start and end apart: 14, of which 7 were waited for; matrix products, arithmetic and copies ran while one was open for 2% of the time, Pallas kernels for 11%

profile of v3, /device:TPU:1, one launch (start us, length us, event | category | flops | bytes accessed | tf_op | source)
XLA Modules:
  0.0 103.7 jit_solution(18368608874565917715)
XLA Ops:
  0.7 1.1 %constant_dynamic-slice_fusion.after_ref = bf16[256,1024]{1,0:T(8,128)(2,1)S(1)} fusion(bf16[256,8192]{1,0:T(8,128)(2,1)} %own_ref.1, s32[]{:T(128)S(6)} %select_n.15), kind=kLoop, calls=%fused_computation | loop fusion | bytes 1048580 | tf_op jit(solution)/shard_map/dynamic_slice | solution.py:192
  1.7 0.0 copy-start.4
  1.8 6.9 %collective-permute-start.2 = (bf16[256,1024]{1,0:T(8,128)(2,1)S(1)}, bf16[256,1024]{1,0:T(8,128)(2,1)S(1)}, u32[]{:S(2)}, u32[]{:S(2)}) collective-permute-start(bf16[256,1024]{1,0:T(8,128)(2,1)S(1)} %constant_dynamic-slice_fusion.after_ref), channel_id=1, source_target_pairs={{0,2},{4,14},{1,3},{5,15},{2,8},{6,4},{3,9},{7,5},{8,10},{12,6},{9... | collective-permute-start | bytes 1572872 | tf_op jit(solution)/shard_map/ppermute | solution.py:151
  8.7 0.7 collective-permute-start.1
  9.4 0.7 collective-permute-start
  10.1 0.0 copy-done.4
  10.1 3.1 %shard_map.122.after_ref = bf16[2048,128]{1,0:T(8,128)(2,1)} custom-call(f32[256,512]{1,0:T(8,128)} %signal_ref.3, f32[256,512]{1,0:T(8,128)} %filter_ref.1, bf16[256,1024]{1,0:T(8,128)(2,1)} %copy-done.4), custom_call_target="tpu_custom_call" | custom-call | flops 10000000000 | tf_op jit(solution)/shard_map/pallas_call | solution.py:257
  13.2 11.2 %all-to-all-start = ((bf16[64,32,128]{2,1,0:T(8,128)(2,1)}), bf16[64,32,128]{2,1,0:T(8,128)(2,1)}, u32[]{:S(2)}, u32[]{:S(2)}) async-start(bf16[64,32,128]{2,1,0:T(8,128)(2,1)} %bitcast.8), calls=%async_computation | async-start | bytes 1048576 | tf_op jit(solution)/shard_map/all_to_all | solution.py:265
  24.4 0.9 collective-permute-done.2.far_ref
  25.3 17.6 %collective-permute-done.1.above_ref = bf16[256,1024]{1,0:T(8,128)(2,1)S(1)} collective-permute-done((bf16[256,1024]{1,0:T(8,128)(2,1)S(1)}, bf16[256,1024]{1,0:T(8,128)(2,1)S(1)}, u32[]{:S(2)}, u32[]{:S(2)}) %collective-permute-start.1) | collective-permute-done | bytes 524320 | tf_op jit(solution)/shard_map/ppermute | solution.py:151
  42.9 0.0 collective-permute-done.below_ref
  42.9 0.0 copy-start.3
  42.9 1.0 %copy-done.3 = bf16[2048,128]{1,0:T(8,128)(2,1)S(1)} copy-done((bf16[2048,128]{1,0:T(8,128)(2,1)S(1)}, bf16[2048,128]{1,0:T(8,128)(2,1)}, u32[]{:S(2)}) %copy-start.3) | copy-done | bytes 524312
  43.9 0.1 shard_map.125.refs_0_
  44.1 1.4 %collective-permute-start.6 = (bf16[768,1024]{1,0:T(8,128)(2,1)S(1)}, bf16[768,1024]{1,0:T(8,128)(2,1)}, u32[]{:S(2)}, u32[]{:S(2)}) collective-permute-start(bf16[768,1024]{1,0:T(8,128)(2,1)S(1)} %shard_map.125.refs_0_), channel_id=1, source_target_pairs={{0,16},{4,68},{1,17},{5,69},{2,18},{6,70},{3,19},{7,71},{8,24},{12... | collective-permute-start | bytes 4718600 | tf_op jit(solution)/shard_map/ppermute | solution.py:151
  45.5 1.5 %collective-permute-start.3 = (bf16[768,1024]{1,0:T(8,128)(2,1)S(1)}, bf16[768,1024]{1,0:T(8,128)(2,1)S(1)}, u32[]{:S(2)}, u32[]{:S(2)}) collective-permute-start(bf16[768,1024]{1,0:T(8,128)(2,1)S(1)} %shard_map.125.refs_0_), channel_id=1, source_target_pairs={{0,48},{4,196},{1,49},{5,197},{2,50},{6,198},{3,51},{7,199},{8,56}... | collective-permute-start | bytes 4718600 | tf_op jit(solution)/shard_map/ppermute | solution.py:151
  47.0 1.3 %fusion = (bf16[384,1024]{1,0:T(8,128)(2,1)}, bf16[384,1024]{1,0:T(8,128)(2,1)}) fusion(bf16[768,1024]{1,0:T(8,128)(2,1)S(1)} %shard_map.125.refs_0_), kind=kLoop, calls=%fused_computation.1 | loop fusion | bytes 3145728 | tf_op jit(solution)/shard_map/slice | solution.py:209
  48.3 2.5 %collective-permute-start.5 = (bf16[384,1024]{1,0:T(8,128)(2,1)}, bf16[384,1024]{1,0:T(8,128)(2,1)}, u32[]{:S(2)}, u32[]{:S(2)}) collective-permute-start(bf16[384,1024]{1,0:T(8,128)(2,1)} %get-tuple-element.6), channel_id=1, source_target_pairs={{0,192},{4,52},{1,193},{5,53},{2,194},{6,54},{3,195},{7,55},{8,200... | collective-permute-start | bytes 2359304 | tf_op jit(solution)/shard_map/ppermute | solution.py:151
  50.7 0.0 collective-permute-start.4
  50.7 0.0 all-to-all-done
  50.7 0.0 copy-start.6
  50.7 5.9 %shard_map.123.after_ref = bf16[1024,128]{1,0:T(8,128)(2,1)} custom-call(bf16[2048,128]{1,0:T(8,128)(2,1)} %bitcast.1.data_ref, bf16[512,256]{1,0:T(8,128)(2,1)} %constant.49.clone.one_ref, bf16[256,256]{1,0:T(8,128)(2,1)} %constant.50.clone.two_ref, bf16[256,256]{1,0:T(8,128)(2,1)} %constant.51.clone.back_two_ref, ...), custom_call_target="tpu_custom_call" | custom-call | flops 99999997952 | tf_op jit(solution)/shard_map/pallas_call | solution.py:268
  56.7 8.8 %all-to-all-start.1 = ((bf16[64,16,128]{2,1,0:T(8,128)(2,1)}), bf16[64,16,128]{2,1,0:T(8,128)(2,1)S(1)}, u32[]{:S(2)}, u32[]{:S(2)}) async-start(bf16[64,16,128]{2,1,0:T(8,128)(2,1)} %bitcast.6), calls=%async_computation.1 | async-start | bytes 524288 | tf_op jit(solution)/shard_map/all_to_all | solution.py:278
  65.5 0.0 copy-done.6
  65.5 0.8 copy.17.skip_ref
  66.3 0.5 collective-permute-start.7
  66.8 1.9 %collective-permute-done.5.block_ref = bf16[384,1024]{1,0:T(8,128)(2,1)} collective-permute-done((bf16[384,1024]{1,0:T(8,128)(2,1)}, bf16[384,1024]{1,0:T(8,128)(2,1)}, u32[]{:S(2)}, u32[]{:S(2)}) %collective-permute-start.5) | collective-permute-done | bytes 786464 | tf_op jit(solution)/shard_map/ppermute | solution.py:151
  68.6 0.9 copy-done
  69.6 0.0 collective-permute-start.10
  69.6 1.0 collective-permute-done.4.block_ref
  70.6 0.0 collective-permute-start.9
  70.6 4.2 %collective-permute-done.6.block_ref = bf16[768,1024]{1,0:T(8,128)(2,1)} collective-permute-done((bf16[768,1024]{1,0:T(8,128)(2,1)S(1)}, bf16[768,1024]{1,0:T(8,128)(2,1)}, u32[]{:S(2)}, u32[]{:S(2)}) %collective-permute-start.6) | collective-permute-done | bytes 1572896 | tf_op jit(solution)/shard_map/ppermute | solution.py:151
  74.8 0.0 copy-done.1
  74.8 0.0 collective-permute-start.11
  74.8 0.3 collective-permute-done.3.block_ref
  75.1 0.2 collective-permute-start.8
  75.3 4.6 %all-to-all-done.1 = bf16[64,16,128]{2,1,0:T(8,128)(2,1)S(1)} async-done(((bf16[64,16,128]{2,1,0:T(8,128)(2,1)}), bf16[64,16,128]{2,1,0:T(8,128)(2,1)S(1)}, u32[]{:S(2)}, u32[]{:S(2)}) %all-to-all-start.1) | async-done | bytes 262176 | tf_op jit(solution)/shard_map/all_to_all | solution.py:278
  79.9 0.7 copy-done.5
  80.6 2.4 %shard_map.124 = (f32[256,512]{1,0:T(8,128)}, bf16[4,256,128]{2,1,0:T(8,128)(2,1)}) custom-call(bf16[1024,128]{1,0:T(8,128)(2,1)} %bitcast.9, f32[256,512]{1,0:T(8,128)} %signal_ref.3, f32[256,512]{1,0:T(8,128)} %gate_ref.1, f32[256,1]{1,0:T(8,128)} %copy.17.skip_ref), custom_call_target="tpu_custom_call" | custom-call | flops 99999997952 | tf_op jit(solution)/shard_map/pallas_call | solution.py:282
  83.0 11.2 %all_to_all.15 = bf16[4,256,128]{2,1,0:T(8,128)(2,1)S(1)} all-to-all(bf16[4,256,128]{2,1,0:T(8,128)(2,1)} %get-tuple-element.5), channel_id=1, replica_groups=mesh['y'=4,'x'=4,'zh'=2,'core'=2,'chan'=4] {'chan'}, dimensions={0} | all-to-all | bytes 524288 | tf_op jit(solution)/shard_map/all_to_all | solution.py:291
  94.2 0.0 collective-permute-done.10.refs_8_
  94.2 0.0 collective-permute-done.9.refs_7_
  94.2 0.0 collective-permute-done.7.refs_5_
  94.2 0.0 collective-permute-done.11.refs_9_
  94.2 0.0 collective-permute-done.8.refs_6_
  94.3 0.0 copy-start.2
  94.3 2.2 %copy-done.2 = bf16[256,8192]{1,0:T(8,128)(2,1)S(1)} copy-done((bf16[256,8192]{1,0:T(8,128)(2,1)S(1)}, bf16[256,8192]{1,0:T(8,128)(2,1)}, u32[]{:S(2)}) %copy-start.2) | copy-done | bytes 4194328
  96.5 7.1 %shard_map.130 = bf16[128,8192]{1,0:T(8,128)(2,1)} custom-call(bf16[1024,128]{1,0:T(8,128)(2,1)S(1)} %bitcast.7, bf16[256,8192]{1,0:T(8,128)(2,1)S(1)} %copy-done.2, bf16[768,1024]{1,0:T(8,128)(2,1)S(1)} %shard_map.125.refs_0_, bf16[768,1024]{1,0:T(8,128)(2,1)S(1)} %shard_map.126.refs_1_, bf16[384,1024]{1,0:T(8,128)(2,1)} %shard_map.127.refs_2_, ...), custom_call_target="tpu_custom_call" | custom-call | tf_op jit(solution)/shard_map/pallas_call | solution.py:293
  (7 shorter events, 0.0 us)
Async XLA Ops:
  1.7 8.4 %copy-start.4 = (bf16[256,1024]{1,0:T(8,128)(2,1)}, bf16[256,1024]{1,0:T(8,128)(2,1)S(1)}, u32[]{:S(2)}) copy-start(bf16[256,1024]{1,0:T(8,128)(2,1)S(1)} %constant_dynamic-slice_fusion.after_ref) | copy-start | bytes 1572868
  1.8 23.6 %collective-permute-start.2 = (bf16[256,1024]{1,0:T(8,128)(2,1)S(1)}, bf16[256,1024]{1,0:T(8,128)(2,1)S(1)}, u32[]{:S(2)}, u32[]{:S(2)}) collective-permute-start(bf16[256,1024]{1,0:T(8,128)(2,1)S(1)} %constant_dynamic-slice_fusion.after_ref), channel_id=1, source_target_pairs={{0,2},{4,14},{1,3},{5,15},{2,8},{6,4},{3,9},{7,5},{8,10},{12,6},{9... | collective-permute-start | bytes 1572872 | tf_op jit(solution)/shard_map/ppermute | solution.py:151
  8.7 34.2 %collective-permute-start.1 = (bf16[256,1024]{1,0:T(8,128)(2,1)S(1)}, bf16[256,1024]{1,0:T(8,128)(2,1)S(1)}, u32[]{:S(2)}, u32[]{:S(2)}) collective-permute-start(bf16[256,1024]{1,0:T(8,128)(2,1)S(1)} %constant_dynamic-slice_fusion.after_ref), channel_id=1, source_target_pairs={{0,11},{4,15},{1,0},{5,4},{2,1},{6,5},{3,2},{7,6},{8,3},{12,7},{9,... | collective-permute-start | bytes 1572872 | tf_op jit(solution)/shard_map/ppermute | solution.py:151
  9.4 33.5 %collective-permute-start = (bf16[256,1024]{1,0:T(8,128)(2,1)S(1)}, bf16[256,1024]{1,0:T(8,128)(2,1)S(1)}, u32[]{:S(2)}, u32[]{:S(2)}) collective-permute-start(bf16[256,1024]{1,0:T(8,128)(2,1)S(1)} %constant_dynamic-slice_fusion.after_ref), channel_id=1, source_target_pairs={{0,1},{4,5},{1,2},{5,6},{2,3},{6,7},{3,8},{7,12},{8,9},{12,13},{9,... | collective-permute-start | bytes 1572872 | tf_op jit(solution)/shard_map/ppermute | solution.py:151
  13.2 37.5 %all-to-all-start = ((bf16[64,32,128]{2,1,0:T(8,128)(2,1)}), bf16[64,32,128]{2,1,0:T(8,128)(2,1)}, u32[]{:S(2)}, u32[]{:S(2)}) async-start(bf16[64,32,128]{2,1,0:T(8,128)(2,1)} %bitcast.8), calls=%async_computation | async-start | bytes 1048576 | tf_op jit(solution)/shard_map/all_to_all | solution.py:265
  42.9 1.0 %copy-start.3 = (bf16[2048,128]{1,0:T(8,128)(2,1)S(1)}, bf16[2048,128]{1,0:T(8,128)(2,1)}, u32[]{:S(2)}) copy-start(bf16[2048,128]{1,0:T(8,128)(2,1)} %shard_map.122.after_ref) | copy-start | bytes 1572868
  44.1 30.7 %collective-permute-start.6 = (bf16[768,1024]{1,0:T(8,128)(2,1)S(1)}, bf16[768,1024]{1,0:T(8,128)(2,1)}, u32[]{:S(2)}, u32[]{:S(2)}) collective-permute-start(bf16[768,1024]{1,0:T(8,128)(2,1)S(1)} %shard_map.125.refs_0_), channel_id=1, source_target_pairs={{0,16},{4,68},{1,17},{5,69},{2,18},{6,70},{3,19},{7,71},{8,24},{12... | collective-permute-start | bytes 4718600 | tf_op jit(solution)/shard_map/ppermute | solution.py:151
  45.5 29.6 %collective-permute-start.3 = (bf16[768,1024]{1,0:T(8,128)(2,1)S(1)}, bf16[768,1024]{1,0:T(8,128)(2,1)S(1)}, u32[]{:S(2)}, u32[]{:S(2)}) collective-permute-start(bf16[768,1024]{1,0:T(8,128)(2,1)S(1)} %shard_map.125.refs_0_), channel_id=1, source_target_pairs={{0,48},{4,196},{1,49},{5,197},{2,50},{6,198},{3,51},{7,199},{8,56}... | collective-permute-start | bytes 4718600 | tf_op jit(solution)/shard_map/ppermute | solution.py:151
  48.3 20.4 %collective-permute-start.5 = (bf16[384,1024]{1,0:T(8,128)(2,1)}, bf16[384,1024]{1,0:T(8,128)(2,1)}, u32[]{:S(2)}, u32[]{:S(2)}) collective-permute-start(bf16[384,1024]{1,0:T(8,128)(2,1)} %get-tuple-element.6), channel_id=1, source_target_pairs={{0,192},{4,52},{1,193},{5,53},{2,194},{6,54},{3,195},{7,55},{8,200... | collective-permute-start | bytes 2359304 | tf_op jit(solution)/shard_map/ppermute | solution.py:151
  50.7 19.9 %collective-permute-start.4 = (bf16[384,1024]{1,0:T(8,128)(2,1)}, bf16[384,1024]{1,0:T(8,128)(2,1)}, u32[]{:S(2)}, u32[]{:S(2)}) collective-permute-start(bf16[384,1024]{1,0:T(8,128)(2,1)} %get-tuple-element.7), channel_id=1, source_target_pairs={{0,64},{4,20},{1,65},{5,21},{2,66},{6,22},{3,67},{7,23},{8,72},{12... | collective-permute-start | bytes 2359304 | tf_op jit(solution)/shard_map/ppermute | solution.py:151
  50.7 14.8 %copy-start.6 = (f32[256]{0:T(256)S(1)}, f32[256]{0:T(256)}, u32[]{:S(2)}) copy-start(f32[256]{0:T(256)} %param.14) | copy-start | bytes 3076
  56.7 23.2 %all-to-all-start.1 = ((bf16[64,16,128]{2,1,0:T(8,128)(2,1)}), bf16[64,16,128]{2,1,0:T(8,128)(2,1)S(1)}, u32[]{:S(2)}, u32[]{:S(2)}) async-start(bf16[64,16,128]{2,1,0:T(8,128)(2,1)} %bitcast.6), calls=%async_computation.1 | async-start | bytes 524288 | tf_op jit(solution)/shard_map/all_to_all | solution.py:278
  66.3 27.9 %collective-permute-start.7 = (bf16[768,1024]{1,0:T(8,128)(2,1)S(1)}, bf16[768,1024]{1,0:T(8,128)(2,1)}, u32[]{:S(2)}, u32[]{:S(2)}) collective-permute-start(bf16[768,1024]{1,0:T(8,128)(2,1)S(1)} %shard_map.125.refs_0_), channel_id=1, source_target_pairs={{0,4},{4,0},{1,5},{5,1},{2,6},{6,2},{3,7},{7,3},{8,12},{12,8},{9,1... | collective-permute-start | bytes 4718600 | tf_op jit(solution)/shard_map/ppermute | solution.py:151
  68.6 0.9 copy-start
  69.6 5.2 %copy-start.1 = (bf16[1024,128]{1,0:T(8,128)(2,1)S(1)}, bf16[1024,128]{1,0:T(8,128)(2,1)}, u32[]{:S(2)}) copy-start(bf16[1024,128]{1,0:T(8,128)(2,1)} %shard_map.123.after_ref) | copy-start | bytes 786436
  69.6 24.6 %collective-permute-start.10 = (bf16[384,1024]{1,0:T(8,128)(2,1)}, bf16[384,1024]{1,0:T(8,128)(2,1)}, u32[]{:S(2)}, u32[]{:S(2)}) collective-permute-start(bf16[384,1024]{1,0:T(8,128)(2,1)} %shard_map.128.refs_3_), channel_id=1, source_target_pairs={{0,4},{4,0},{1,5},{5,1},{2,6},{6,2},{3,7},{7,3},{8,12},{12,8},{9,1... | collective-permute-start | bytes 2359304 | tf_op jit(solution)/shard_map/ppermute | solution.py:151
  70.6 23.7 %collective-permute-start.9 = (bf16[384,1024]{1,0:T(8,128)(2,1)}, bf16[384,1024]{1,0:T(8,128)(2,1)}, u32[]{:S(2)}, u32[]{:S(2)}) collective-permute-start(bf16[384,1024]{1,0:T(8,128)(2,1)} %shard_map.127.refs_2_), channel_id=1, source_target_pairs={{0,4},{4,0},{1,5},{5,1},{2,6},{6,2},{3,7},{7,3},{8,12},{12,8},{9,1... | collective-permute-start | bytes 2359304 | tf_op jit(solution)/shard_map/ppermute | solution.py:151
  74.8 19.4 %collective-permute-start.11 = (bf16[768,1024]{1,0:T(8,128)(2,1)}, bf16[768,1024]{1,0:T(8,128)(2,1)}, u32[]{:S(2)}, u32[]{:S(2)}) collective-permute-start(bf16[768,1024]{1,0:T(8,128)(2,1)} %shard_map.129.refs_4_), channel_id=1, source_target_pairs={{0,4},{4,0},{1,5},{5,1},{2,6},{6,2},{3,7},{7,3},{8,12},{12,8},{9,1... | collective-permute-start | bytes 4718600 | tf_op jit(solution)/shard_map/ppermute | solution.py:151
  75.1 19.2 %collective-permute-start.8 = (bf16[768,1024]{1,0:T(8,128)(2,1)S(1)}, bf16[768,1024]{1,0:T(8,128)(2,1)}, u32[]{:S(2)}, u32[]{:S(2)}) collective-permute-start(bf16[768,1024]{1,0:T(8,128)(2,1)S(1)} %shard_map.126.refs_1_), channel_id=1, source_target_pairs={{0,4},{4,0},{1,5},{5,1},{2,6},{6,2},{3,7},{7,3},{8,12},{12,8},{9,1... | collective-permute-start | bytes 4718600 | tf_op jit(solution)/shard_map/ppermute | solution.py:151
  79.9 0.7 copy-start.5
  94.3 2.2 %copy-start.2 = (bf16[256,8192]{1,0:T(8,128)(2,1)S(1)}, bf16[256,8192]{1,0:T(8,128)(2,1)}, u32[]{:S(2)}) copy-start(bf16[256,8192]{1,0:T(8,128)(2,1)} %own_ref.1) | copy-start | bytes 12582916

commit v4 on v3

--- a/solution.py
+++ b/solution.py
@@ -19,7 +19,7 @@
 PIECES = 4
 HALF = 4096
 QUARTER = 1024
-SPLIT = 384
+AHEAD = 3
 WORK = 10**11
 PACK_WORK = 10**10
 JOIN_WORK = 10**10
@@ -50,7 +50,7 @@
     )
 
 
-def pack_kernel(signal_ref, filter_ref, after_ref, out_ref, wide):
+def pack_kernel(signal_ref, filter_ref, after_ref, out_ref, token_ref, wide):
     for which, source in enumerate((signal_ref, filter_ref)):
         for own in range(OWN_CHANNELS):
             for piece in range(PIECES):
@@ -60,6 +60,7 @@
                     piece * LANES : (piece + 1) * LANES,
                 ]
     out_ref[...] = wide[...].astype(jnp.bfloat16)
+    token_ref[...] = jnp.zeros_like(token_ref)
 
 
 def matmul(left, right):
@@ -67,7 +68,17 @@
 
 
 def convolve_kernel(
-    data_ref, one_ref, two_ref, back_two_ref, back_one_ref, cos_ref, sin_ref, out_ref, wide, result
+    data_ref,
+    one_ref,
+    two_ref,
+    back_two_ref,
+    back_one_ref,
+    cos_ref,
+    sin_ref,
+    out_ref,
+    token_ref,
+    wide,
+    result,
 ):
     wide[...] = data_ref[...].astype(jnp.float32)
     columns = []
@@ -110,6 +121,7 @@
                 piece * SEQ_DEVICES : (piece + 1) * SEQ_DEVICES
             ]
     out_ref[...] = result[...].astype(jnp.bfloat16)
+    token_ref[...] = jnp.zeros_like(token_ref)
 
 
 def mix_kernel(conv_ref, signal_ref, gate_ref, skip_ref, mixed_ref, rounded_ref, wide):
@@ -172,6 +184,7 @@
 
 
 ANYWHERE = pl.BlockSpec(memory_space=pl.ANY)
+TOKEN = jax.ShapeDtypeStruct((8, LANES), jnp.float32)
 
 
 def ordered(block, after):
@@ -206,12 +219,10 @@
         in_specs=[ANYWHERE] * 4,
         out_specs=ANYWHERE,
     )(*parts, after)
-    upper, lower = block[:SPLIT], block[SPLIT:]
     return [
         block,
         moved(block, lambda y, x, z, c: (y - c, x - 1 + c, z, c)),
-        moved(upper, lambda y, x, z, c: (y + 1 - c, x + c, z, c)),
-        moved(lower, lambda y, x, z, c: (y - 1 + c, x - c, z, c)),
+        moved(block, lambda y, x, z, c: (y + 1 - c, x + c, z, c)),
         moved(block, lambda y, x, z, c: (y + c, x + 1 - c, z, c)),
     ]
 
@@ -222,31 +233,47 @@
 
 
 def project_kernel(columns_ref, own_ref, *refs):
-    block_refs, (out_ref, results, out_sem) = refs[:10], refs[10:]
+    block_refs, (out_ref, weights, results, own_sem, block_sem, out_sem) = refs[:8], refs[8:]
     core, chan = lax.axis_index("core"), lax.axis_index("chan")
+    starts, loads = [], []
+    for index, block_ref in enumerate(block_refs):
+        owner = core if index < 4 else 1 - core
+        start = pl.multiple_of(owner * HALF + (colour(owner) + index) % 4 * QUARTER, QUARTER)
+        slot = index % (AHEAD + 1)
+        starts.append(start)
+        loads.append(
+            (
+                pltpu.make_async_copy(
+                    own_ref.at[:, pl.ds(start, QUARTER)],
+                    weights.at[slot, pl.ds(0, ROWS)],
+                    own_sem.at[index],
+                ),
+                pltpu.make_async_copy(
+                    block_ref, weights.at[slot, pl.ds(ROWS, 3 * ROWS)], block_sem.at[index]
+                ),
+            )
+        )
+    for index in range(AHEAD):
+        for load in loads[index]:
+            load.start()
     rows = [
         columns_ref[pl.ds(pl.multiple_of((chan + shift) % 4 * ROWS, ROWS), ROWS), :].T
         for shift in (0, 3, 1, 2)
     ]
-    own_columns, columns = rows[0], jnp.concatenate(rows[1:], axis=1)
+    left = jnp.concatenate(rows, axis=1)
     stores = []
-    for half in range(2):
-        owner = core if half == 0 else 1 - core
-        for step, parts in enumerate(((0,), (1,), (2, 3), (4,))):
-            index = 4 * half + step
-            start = pl.multiple_of(owner * HALF + (colour(owner) + step) % 4 * QUARTER, QUARTER)
-            total = matmul(own_columns, own_ref[:, pl.ds(start, QUARTER)])
-            row = 0
-            for part in parts:
-                block = block_refs[5 * half + part][...]
-                total += matmul(columns[:, row : row + block.shape[0]], block)
-                row += block.shape[0]
-            results[index] = total.astype(jnp.bfloat16)
-            store = pltpu.make_async_copy(
-                results.at[index], out_ref.at[:, pl.ds(start, QUARTER)], out_sem.at[index]
-            )
-            store.start()
-            stores.append(store)
+    for index in range(8):
+        for load in loads[index]:
+            load.wait()
+        if index + AHEAD < 8:
+            for load in loads[index + AHEAD]:
+                load.start()
+        results[index] = matmul(left, weights[index % (AHEAD + 1)]).astype(jnp.bfloat16)
+        store = pltpu.make_async_copy(
+            results.at[index], out_ref.at[:, pl.ds(starts[index], QUARTER)], out_sem.at[index]
+        )
+        store.start()
+        stores.append(store)
     for store in stores:
         store.wait()
 
@@ -254,27 +281,27 @@
 def body(signal, gate, filter_taps, skip_weight, out_weight):
     mine, parts = first_quarter(out_weight)
     tables = transform_tables()
-    packed = call(
+    packed, packed_token = call(
         pack_kernel,
-        jax.ShapeDtypeStruct((SEQ_DEVICES * 32, LANES), jnp.bfloat16),
+        (jax.ShapeDtypeStruct((SEQ_DEVICES * 32, LANES), jnp.bfloat16), TOKEN),
         [pltpu.VMEM((SEQ_DEVICES * 32, LANES), jnp.float32)],
         work=PACK_WORK,
         in_specs=[pl.BlockSpec(memory_space=pltpu.VMEM)] * 2 + [ANYWHERE],
     )(signal, filter_taps, mine)
-    blocks = other_quarters(parts, packed)
+    blocks = other_quarters(parts, packed_token)
     arrived = lax.all_to_all(
         packed.reshape(SEQ_DEVICES, 32, LANES), AXES, split_axis=0, concat_axis=0, tiled=True
     )
-    convolved = call(
+    convolved, convolved_token = call(
         convolve_kernel,
-        jax.ShapeDtypeStruct((SEQ_DEVICES * 16, LANES), jnp.bfloat16),
+        (jax.ShapeDtypeStruct((SEQ_DEVICES * 16, LANES), jnp.bfloat16), TOKEN),
         [
             pltpu.VMEM((SEQ_DEVICES * 32, LANES), jnp.float32),
             pltpu.VMEM((SEQ_DEVICES * 16, LANES), jnp.float32),
         ],
         work=WORK,
     )(arrived.reshape(SEQ_DEVICES * 32, LANES), *tables)
-    weights = both_halves(blocks, convolved)
+    weights = both_halves(blocks, convolved_token)
     returned = lax.all_to_all(
         convolved.reshape(SEQ_DEVICES, 16, LANES), AXES, split_axis=0, concat_axis=0, tiled=True
     )
@@ -294,11 +321,13 @@
         project_kernel,
         jax.ShapeDtypeStruct((LANES, width), jnp.bfloat16),
         [
+            pltpu.VMEM((AHEAD + 1, 4 * ROWS, QUARTER), jnp.bfloat16),
             pltpu.VMEM((8, LANES, QUARTER), jnp.bfloat16),
             pltpu.SemaphoreType.DMA((8,)),
+            pltpu.SemaphoreType.DMA((8,)),
+            pltpu.SemaphoreType.DMA((8,)),
         ],
-        limit=30,
-        in_specs=[pl.BlockSpec(memory_space=pltpu.VMEM)] * 12,
+        in_specs=[pl.BlockSpec(memory_space=pltpu.VMEM)] + [ANYWHERE] * 9,
         out_specs=ANYWHERE,
     )(mine.reshape(4 * channels, LANES), out_weight, *weights)
     return mixed, projected

time: 105 us -> 111 us (1.057)
  waiting for transfers between devices: 30.4 us -> 37.1 us
  local copies, waits for them, and re-layouts: 8.03 us -> 4.63 us
  Pallas kernels: 18.6 us -> 21.5 us
  blocking collectives: 11.2 us -> 12.8 us
    ppermute x12 -> x10, waiting for transfers between devices: 25.8 us -> 37.1 us  [moved(): return lax.ppermute(array, (*AXES, 'chan'), device_pairs(move))]
    all_to_all x1, waiting for transfers between devices: 4.57 us -> 0.01 us  [body(): lax.all_to_all(convolved.reshape(SEQ_DEVICES, 16, LANES), AXES, split_axi...]
    unnamed x14, local copies, waits for them, and re-layouts: 4.89 us -> 2.76 us
    pallas_call x1, Pallas kernels: 7.08 us -> 8.92 us  [body(): call(project_kernel, jax.ShapeDtypeStruct((LANES, width), jnp.bfloat16),...]
    all_to_all x1, blocking collectives: 11.2 us -> 12.8 us  [body(): lax.all_to_all(rounded, 'chan', split_axis=0, concat_axis=0, tiled=True)]
    slice x1 -> x0, local copies, waits for them, and re-layouts: 1.26 us -> none  [other_quarters(): upper, lower = (block[:SPLIT], block[SPLIT:])]
    ppermute x12 -> x10, starting transfers between devices: 14.5 us -> 14 us  [moved(): return lax.ppermute(array, (*AXES, 'chan'), device_pairs(move))]
  transfers between devices with their start and end apart: 14 -> 12, of which waited for: 7 -> 3; matrix products, arithmetic and copies ran while one was open for 2% -> 1% of each run, Pallas kernels for 11% -> 11%
where the time goes in v4:
time: 111 us; the launch traced here: 110 us
  waiting for transfers between devices  37.1 us (33%)
  starting transfers between devices  33.5 us (30%)
  Pallas kernels  21.5 us (19%)
  blocking collectives  12.8 us (12%)
  local copies, waits for them, and re-layouts  4.63 us (4%)
    ppermute x10, waiting for transfers between devices, moved(): return lax.ppermute(array, (*AXES, 'chan'), device_pairs(move))  37.1 us
    ppermute x10, starting transfers between devices, moved(): return lax.ppermute(array, (*AXES, 'chan'), device_pairs(move))  14 us
    all_to_all x1, blocking collectives, body(): lax.all_to_all(rounded, 'chan', split_axis=0, concat_axis=0, tiled=True)  12.8 us
    all_to_all x1, starting transfers between devices, body(): lax.all_to_all(packed.reshape(SEQ_DEVICES, 32, LANES), AXES, split_axis=0...  11.2 us
    pallas_call x1, Pallas kernels, body(): call(project_kernel, jax.ShapeDtypeStruct((LANES, width), jnp.bfloat16),...  8.92 us
    all_to_all x1, starting transfers between devices, body(): lax.all_to_all(convolved.reshape(SEQ_DEVICES, 16, LANES), AXES, split_axi...  8.34 us
    pallas_call x1, Pallas kernels, body(): call(convolve_kernel, (jax.ShapeDtypeStruct((SEQ_DEVICES * 16, LANES), jn...  5.92 us
    pallas_call x1, Pallas kernels, body(): call(pack_kernel, (jax.ShapeDtypeStruct((SEQ_DEVICES * 32, LANES), jnp.bf...  3.09 us
  transfers between devices with their start and end apart: 12, of which 3 were waited for; matrix products, arithmetic and copies ran while one was open for 1% of the time, Pallas kernels for 11%

profile of v4, /device:TPU:1, one launch (start us, length us, event | category | flops | bytes accessed | tf_op | source)
XLA Modules:
  0.0 110.4 jit_solution(1314276248884031348)
XLA Ops:
  0.7 1.1 constant_dynamic-slice_fusion.after_ref
  1.7 0.0 copy-start.4
  1.8 6.9 %collective-permute-start.2 = (bf16[256,1024]{1,0:T(8,128)(2,1)S(1)}, bf16[256,1024]{1,0:T(8,128)(2,1)S(1)}, u32[]{:S(2)}, u32[]{:S(2)}) collective-permute-start(bf16[256,1024]{1,0:T(8,128)(2,1)S(1)} %constant_dynamic-slice_fusion.after_ref), channel_id=1, source_target_pairs={{0,2},{4,14},{1,3},{5,15},{2,8},{6,4},{3,9},{7,5},{8,10},{12,6},{9... | collective-permute-start | bytes 1572872 | tf_op jit(solution)/shard_map/ppermute | solution.py:163
  8.7 0.7 collective-permute-start.1
  9.4 0.7 collective-permute-start
  10.1 0.0 copy-done.4
  10.1 3.1 %shard_map.122 = (bf16[2048,128]{1,0:T(8,128)(2,1)}, f32[8,128]{1,0:T(8,128)}) custom-call(f32[256,512]{1,0:T(8,128)} %signal_ref.3, f32[256,512]{1,0:T(8,128)} %filter_ref.1, bf16[256,1024]{1,0:T(8,128)(2,1)} %copy-done.4), custom_call_target="tpu_custom_call" | custom-call | flops 10000000000 | tf_op jit(solution)/shard_map/pallas_call | solution.py:284
  13.2 11.2 %all-to-all-start = ((bf16[64,32,128]{2,1,0:T(8,128)(2,1)}), bf16[64,32,128]{2,1,0:T(8,128)(2,1)}, u32[]{:S(2)}, u32[]{:S(2)}) async-start(bf16[64,32,128]{2,1,0:T(8,128)(2,1)} %bitcast.7), calls=%async_computation | async-start | bytes 1048576 | tf_op jit(solution)/shard_map/all_to_all | solution.py:292
  24.4 0.9 collective-permute-done.2.far_ref
  25.3 17.6 %collective-permute-done.1.above_ref = bf16[256,1024]{1,0:T(8,128)(2,1)S(1)} collective-permute-done((bf16[256,1024]{1,0:T(8,128)(2,1)S(1)}, bf16[256,1024]{1,0:T(8,128)(2,1)S(1)}, u32[]{:S(2)}, u32[]{:S(2)}) %collective-permute-start.1) | collective-permute-done | bytes 524320 | tf_op jit(solution)/shard_map/ppermute | solution.py:163
  42.9 0.0 collective-permute-done.below_ref
  42.9 0.0 copy-start.3
  42.9 0.7 copy-done.3
  43.6 1.2 %shard_map.125.refs_0_ = bf16[768,1024]{1,0:T(8,128)(2,1)} custom-call(bf16[256,1024]{1,0:T(8,128)(2,1)S(1)} %collective-permute-done.below_ref, bf16[256,1024]{1,0:T(8,128)(2,1)S(1)} %collective-permute-done.1.above_ref, bf16[256,1024]{1,0:T(8,128)(2,1)S(1)} %collective-permute-done.2.far_ref, f32[8,128]{1,0:T(8,128)S(1)} %copy-done.3), custom_call_target="tpu_custom_call" | custom-call | flops 10000000000 | tf_op jit(solution)/shard_map/pallas_call | solution.py:213
  44.8 1.4 %collective-permute-start.5 = (bf16[768,1024]{1,0:T(8,128)(2,1)}, bf16[768,1024]{1,0:T(8,128)(2,1)}, u32[]{:S(2)}, u32[]{:S(2)}) collective-permute-start(bf16[768,1024]{1,0:T(8,128)(2,1)} %shard_map.125.refs_0_), channel_id=1, source_target_pairs={{0,16},{4,68},{1,17},{5,69},{2,18},{6,70},{3,19},{7,71},{8,24},{12... | collective-permute-start | bytes 4718600 | tf_op jit(solution)/shard_map/ppermute | solution.py:163
  46.1 1.2 %collective-permute-start.4 = (bf16[768,1024]{1,0:T(8,128)(2,1)}, bf16[768,1024]{1,0:T(8,128)(2,1)S(1)}, u32[]{:S(2)}, u32[]{:S(2)}) collective-permute-start(bf16[768,1024]{1,0:T(8,128)(2,1)} %shard_map.125.refs_0_), channel_id=1, source_target_pairs={{0,64},{4,20},{1,65},{5,21},{2,66},{6,22},{3,67},{7,23},{8,72},{12... | collective-permute-start | bytes 4718600 | tf_op jit(solution)/shard_map/ppermute | solution.py:163
  47.4 1.5 %collective-permute-start.3 = (bf16[768,1024]{1,0:T(8,128)(2,1)}, bf16[768,1024]{1,0:T(8,128)(2,1)S(1)}, u32[]{:S(2)}, u32[]{:S(2)}) collective-permute-start(bf16[768,1024]{1,0:T(8,128)(2,1)} %shard_map.125.refs_0_), channel_id=1, source_target_pairs={{0,48},{4,196},{1,49},{5,197},{2,50},{6,198},{3,51},{7,199},{8,56}... | collective-permute-start | bytes 4718600 | tf_op jit(solution)/shard_map/ppermute | solution.py:163
  48.9 0.0 all-to-all-done
  48.9 0.0 copy-start.6
  48.9 5.9 %shard_map.123 = (bf16[1024,128]{1,0:T(8,128)(2,1)}, f32[8,128]{1,0:T(8,128)}) custom-call(bf16[2048,128]{1,0:T(8,128)(2,1)} %bitcast.1.data_ref, bf16[512,256]{1,0:T(8,128)(2,1)} %constant.49.clone.one_ref, bf16[256,256]{1,0:T(8,128)(2,1)} %constant.50.clone.two_ref, bf16[256,256]{1,0:T(8,128)(2,1)} %constant.51.clone.back_two_ref, ...), custom_call_target="tpu_custom_call" | custom-call | flops 99999997952 | tf_op jit(solution)/shard_map/pallas_call | solution.py:295
  54.8 8.3 %all-to-all-start.1 = ((bf16[64,16,128]{2,1,0:T(8,128)(2,1)}), bf16[64,16,128]{2,1,0:T(8,128)(2,1)S(1)}, u32[]{:S(2)}, u32[]{:S(2)}) async-start(bf16[64,16,128]{2,1,0:T(8,128)(2,1)} %bitcast.8), calls=%async_computation.1 | async-start | bytes 524288 | tf_op jit(solution)/shard_map/all_to_all | solution.py:305
  63.2 0.0 copy-done.6
  63.2 0.8 copy.16.skip_ref
  64.0 0.5 collective-permute-start.6
  64.4 18.6 %collective-permute-done.5.block_ref = bf16[768,1024]{1,0:T(8,128)(2,1)} collective-permute-done((bf16[768,1024]{1,0:T(8,128)(2,1)}, bf16[768,1024]{1,0:T(8,128)(2,1)}, u32[]{:S(2)}, u32[]{:S(2)}) %collective-permute-start.5) | collective-permute-done | bytes 1572896 | tf_op jit(solution)/shard_map/ppermute | solution.py:163
  83.0 0.0 copy-start.2
  83.0 0.7 copy-done.2
  83.7 0.0 collective-permute-start.9
  83.7 0.0 collective-permute-done.4.block_ref
  83.7 0.0 copy-start.1
  83.7 0.5 collective-permute-start.8
  84.2 0.0 collective-permute-done.3.block_ref
  84.2 0.7 copy-done.1
  84.9 0.0 copy-start
  84.9 0.5 collective-permute-start.7
  85.4 0.0 all-to-all-done.1
  85.4 0.0 copy-start.5
  85.4 0.7 copy-done.5
  86.1 2.4 %shard_map.124 = (f32[256,512]{1,0:T(8,128)}, bf16[4,256,128]{2,1,0:T(8,128)(2,1)}) custom-call(bf16[1024,128]{1,0:T(8,128)(2,1)} %bitcast.9, f32[256,512]{1,0:T(8,128)} %signal_ref.3, f32[256,512]{1,0:T(8,128)} %gate_ref.1, f32[256,1]{1,0:T(8,128)} %copy.16.skip_ref), custom_call_target="tpu_custom_call" | custom-call | flops 99999997952 | tf_op jit(solution)/shard_map/pallas_call | solution.py:309
  88.5 0.0 copy-done
  88.5 12.8 %all_to_all.15 = bf16[4,256,128]{2,1,0:T(8,128)(2,1)} all-to-all(bf16[4,256,128]{2,1,0:T(8,128)(2,1)} %get-tuple-element.11), channel_id=1, replica_groups=mesh['y'=4,'x'=4,'zh'=2,'core'=2,'chan'=4] {'chan'}, dimensions={0} | all-to-all | bytes 524288 | tf_op jit(solution)/shard_map/all_to_all | solution.py:318
  101.3 0.0 collective-permute-done.6.refs_4_
  101.4 0.0 collective-permute-done.9.refs_7_
  101.4 0.0 collective-permute-done.8.refs_6_
  101.4 0.0 collective-permute-done.7.refs_5_
  101.4 8.9 %shard_map.129 = bf16[128,8192]{1,0:T(8,128)(2,1)} custom-call(bf16[1024,128]{1,0:T(8,128)(2,1)} %bitcast.6, bf16[256,8192]{1,0:T(8,128)(2,1)} %own_ref.1, bf16[768,1024]{1,0:T(8,128)(2,1)} %shard_map.125.refs_0_, bf16[768,1024]{1,0:T(8,128)(2,1)} %copy-done, bf16[768,1024]{1,0:T(8,128)(2,1)} %copy-done.1, bf16[768,1024]{1,0:T(8,128)(2,1)} %shard_map.128.refs_3_, ...), custom_call_target="tpu_custom_call" | custom-call | tf_op jit(solution)/shard_map/pallas_call | solution.py:320
  (3 shorter events, 0.0 us)
Async XLA Ops:
  1.7 8.4 %copy-start.4 = (bf16[256,1024]{1,0:T(8,128)(2,1)}, bf16[256,1024]{1,0:T(8,128)(2,1)S(1)}, u32[]{:S(2)}) copy-start(bf16[256,1024]{1,0:T(8,128)(2,1)S(1)} %constant_dynamic-slice_fusion.after_ref) | copy-start | bytes 1572868
  1.8 23.6 %collective-permute-start.2 = (bf16[256,1024]{1,0:T(8,128)(2,1)S(1)}, bf16[256,1024]{1,0:T(8,128)(2,1)S(1)}, u32[]{:S(2)}, u32[]{:S(2)}) collective-permute-start(bf16[256,1024]{1,0:T(8,128)(2,1)S(1)} %constant_dynamic-slice_fusion.after_ref), channel_id=1, source_target_pairs={{0,2},{4,14},{1,3},{5,15},{2,8},{6,4},{3,9},{7,5},{8,10},{12,6},{9... | collective-permute-start | bytes 1572872 | tf_op jit(solution)/shard_map/ppermute | solution.py:163
  8.7 34.2 %collective-permute-start.1 = (bf16[256,1024]{1,0:T(8,128)(2,1)S(1)}, bf16[256,1024]{1,0:T(8,128)(2,1)S(1)}, u32[]{:S(2)}, u32[]{:S(2)}) collective-permute-start(bf16[256,1024]{1,0:T(8,128)(2,1)S(1)} %constant_dynamic-slice_fusion.after_ref), channel_id=1, source_target_pairs={{0,11},{4,15},{1,0},{5,4},{2,1},{6,5},{3,2},{7,6},{8,3},{12,7},{9,... | collective-permute-start | bytes 1572872 | tf_op jit(solution)/shard_map/ppermute | solution.py:163
  9.4 33.5 %collective-permute-start = (bf16[256,1024]{1,0:T(8,128)(2,1)S(1)}, bf16[256,1024]{1,0:T(8,128)(2,1)S(1)}, u32[]{:S(2)}, u32[]{:S(2)}) collective-permute-start(bf16[256,1024]{1,0:T(8,128)(2,1)S(1)} %constant_dynamic-slice_fusion.after_ref), channel_id=1, source_target_pairs={{0,1},{4,5},{1,2},{5,6},{2,3},{6,7},{3,8},{7,12},{8,9},{12,13},{9,... | collective-permute-start | bytes 1572872 | tf_op jit(solution)/shard_map/ppermute | solution.py:163
  13.2 35.6 %all-to-all-start = ((bf16[64,32,128]{2,1,0:T(8,128)(2,1)}), bf16[64,32,128]{2,1,0:T(8,128)(2,1)}, u32[]{:S(2)}, u32[]{:S(2)}) async-start(bf16[64,32,128]{2,1,0:T(8,128)(2,1)} %bitcast.7), calls=%async_computation | async-start | bytes 1048576 | tf_op jit(solution)/shard_map/all_to_all | solution.py:292
  42.9 0.7 copy-start.3
  44.8 38.2 %collective-permute-start.5 = (bf16[768,1024]{1,0:T(8,128)(2,1)}, bf16[768,1024]{1,0:T(8,128)(2,1)}, u32[]{:S(2)}, u32[]{:S(2)}) collective-permute-start(bf16[768,1024]{1,0:T(8,128)(2,1)} %shard_map.125.refs_0_), channel_id=1, source_target_pairs={{0,16},{4,68},{1,17},{5,69},{2,18},{6,70},{3,19},{7,71},{8,24},{12... | collective-permute-start | bytes 4718600 | tf_op jit(solution)/shard_map/ppermute | solution.py:163
  46.1 37.6 %collective-permute-start.4 = (bf16[768,1024]{1,0:T(8,128)(2,1)}, bf16[768,1024]{1,0:T(8,128)(2,1)S(1)}, u32[]{:S(2)}, u32[]{:S(2)}) collective-permute-start(bf16[768,1024]{1,0:T(8,128)(2,1)} %shard_map.125.refs_0_), channel_id=1, source_target_pairs={{0,64},{4,20},{1,65},{5,21},{2,66},{6,22},{3,67},{7,23},{8,72},{12... | collective-permute-start | bytes 4718600 | tf_op jit(solution)/shard_map/ppermute | solution.py:163
  47.4 36.9 %collective-permute-start.3 = (bf16[768,1024]{1,0:T(8,128)(2,1)}, bf16[768,1024]{1,0:T(8,128)(2,1)S(1)}, u32[]{:S(2)}, u32[]{:S(2)}) collective-permute-start(bf16[768,1024]{1,0:T(8,128)(2,1)} %shard_map.125.refs_0_), channel_id=1, source_target_pairs={{0,48},{4,196},{1,49},{5,197},{2,50},{6,198},{3,51},{7,199},{8,56}... | collective-permute-start | bytes 4718600 | tf_op jit(solution)/shard_map/ppermute | solution.py:163
  48.9 14.3 %copy-start.6 = (f32[256]{0:T(256)S(1)}, f32[256]{0:T(256)}, u32[]{:S(2)}) copy-start(f32[256]{0:T(256)} %param.14) | copy-start | bytes 3076
  54.8 30.6 %all-to-all-start.1 = ((bf16[64,16,128]{2,1,0:T(8,128)(2,1)}), bf16[64,16,128]{2,1,0:T(8,128)(2,1)S(1)}, u32[]{:S(2)}, u32[]{:S(2)}) async-start(bf16[64,16,128]{2,1,0:T(8,128)(2,1)} %bitcast.8), calls=%async_computation.1 | async-start | bytes 524288 | tf_op jit(solution)/shard_map/all_to_all | solution.py:305
  64.0 37.4 %collective-permute-start.6 = (bf16[768,1024]{1,0:T(8,128)(2,1)}, bf16[768,1024]{1,0:T(8,128)(2,1)}, u32[]{:S(2)}, u32[]{:S(2)}) collective-permute-start(bf16[768,1024]{1,0:T(8,128)(2,1)} %shard_map.125.refs_0_), channel_id=1, source_target_pairs={{0,4},{4,0},{1,5},{5,1},{2,6},{6,2},{3,7},{7,3},{8,12},{12,8},{9,1... | collective-permute-start | bytes 4718600 | tf_op jit(solution)/shard_map/ppermute | solution.py:163
  83.0 0.7 copy-start.2
  83.7 17.7 %collective-permute-start.9 = (bf16[768,1024]{1,0:T(8,128)(2,1)}, bf16[768,1024]{1,0:T(8,128)(2,1)}, u32[]{:S(2)}, u32[]{:S(2)}) collective-permute-start(bf16[768,1024]{1,0:T(8,128)(2,1)} %shard_map.128.refs_3_), channel_id=1, source_target_pairs={{0,4},{4,0},{1,5},{5,1},{2,6},{6,2},{3,7},{7,3},{8,12},{12,8},{9,1... | collective-permute-start | bytes 4718600 | tf_op jit(solution)/shard_map/ppermute | solution.py:163
  83.7 1.2 %copy-start.1 = (bf16[768,1024]{1,0:T(8,128)(2,1)}, bf16[768,1024]{1,0:T(8,128)(2,1)S(1)}, u32[]{:S(2)}) copy-start(bf16[768,1024]{1,0:T(8,128)(2,1)S(1)} %shard_map.127.refs_2_) | copy-start | bytes 4718596
  83.7 17.6 %collective-permute-start.8 = (bf16[768,1024]{1,0:T(8,128)(2,1)S(1)}, bf16[768,1024]{1,0:T(8,128)(2,1)}, u32[]{:S(2)}, u32[]{:S(2)}) collective-permute-start(bf16[768,1024]{1,0:T(8,128)(2,1)S(1)} %shard_map.127.refs_2_), channel_id=1, source_target_pairs={{0,4},{4,0},{1,5},{5,1},{2,6},{6,2},{3,7},{7,3},{8,12},{12,8},{9,1... | collective-permute-start | bytes 4718600 | tf_op jit(solution)/shard_map/ppermute | solution.py:163
  84.9 3.7 %copy-start = (bf16[768,1024]{1,0:T(8,128)(2,1)}, bf16[768,1024]{1,0:T(8,128)(2,1)S(1)}, u32[]{:S(2)}) copy-start(bf16[768,1024]{1,0:T(8,128)(2,1)S(1)} %shard_map.126.refs_1_) | copy-start | bytes 4718596
  84.9 16.5 %collective-permute-start.7 = (bf16[768,1024]{1,0:T(8,128)(2,1)S(1)}, bf16[768,1024]{1,0:T(8,128)(2,1)}, u32[]{:S(2)}, u32[]{:S(2)}) collective-permute-start(bf16[768,1024]{1,0:T(8,128)(2,1)S(1)} %shard_map.126.refs_1_), channel_id=1, source_target_pairs={{0,4},{4,0},{1,5},{5,1},{2,6},{6,2},{3,7},{7,3},{8,12},{12,8},{9,1... | collective-permute-start | bytes 4718600 | tf_op jit(solution)/shard_map/ppermute | solution.py:163
  85.4 0.7 copy-start.5

commit v5 on v4

--- a/solution.py
+++ b/solution.py
@@ -19,7 +19,7 @@
 PIECES = 4
 HALF = 4096
 QUARTER = 1024
-AHEAD = 3
+LAST = 48
 WORK = 10**11
 PACK_WORK = 10**10
 JOIN_WORK = 10**10
@@ -168,10 +168,10 @@
     return jnp.where(core == 0, x + 2 * y, 2 * x + y) % 4
 
 
-def join_kernel(below_ref, above_ref, far_ref, after_ref, out_ref, sem):
+def join_kernel(below_ref, above_ref, after_ref, out_ref, sem):
     copies = [
         pltpu.make_async_copy(ref, out_ref.at[pl.ds(index * ROWS, ROWS)], sem.at[index])
-        for index, ref in enumerate((below_ref, above_ref, far_ref))
+        for index, ref in enumerate((below_ref, above_ref))
     ]
     for copy in copies:
         copy.start()
@@ -209,77 +209,78 @@
     return mine, (below, above, far)
 
 
-def other_quarters(parts, after):
-    block = call(
+def joined(below, above, after):
+    return call(
         join_kernel,
-        jax.ShapeDtypeStruct((3 * ROWS, QUARTER), jnp.bfloat16),
-        [pltpu.SemaphoreType.DMA((3,))],
+        jax.ShapeDtypeStruct((2 * ROWS, QUARTER), jnp.bfloat16),
+        [pltpu.SemaphoreType.DMA((2,))],
         limit=2,
         work=JOIN_WORK,
-        in_specs=[ANYWHERE] * 4,
+        in_specs=[ANYWHERE] * 3,
         out_specs=ANYWHERE,
-    )(*parts, after)
+    )(below, above, after)
+
+
+def other_quarters(block, way):
     return [
         block,
         moved(block, lambda y, x, z, c: (y - c, x - 1 + c, z, c)),
-        moved(block, lambda y, x, z, c: (y + 1 - c, x + c, z, c)),
+        moved(block, lambda y, x, z, c: (y + way * (1 - c), x + way * c, z, c)),
         moved(block, lambda y, x, z, c: (y + c, x + 1 - c, z, c)),
     ]
 
 
-def both_halves(blocks, after):
-    blocks = blocks[:1] + [ordered(block, after) for block in blocks[1:]]
-    return blocks + [moved(block, lambda y, x, z, c: (y, x, z, 1 - c)) for block in blocks]
-
-
-def project_kernel(columns_ref, own_ref, *refs):
-    block_refs, (out_ref, weights, results, own_sem, block_sem, out_sem) = refs[:8], refs[8:]
+def project_kernel(mine_ref, theirs_ref, own_ref, *refs):
+    near_refs, far_refs = refs[:4], refs[4:8]
+    out_ref, for_them_ref, own, results, own_sem, out_sem = refs[8:]
     core, chan = lax.axis_index("core"), lax.axis_index("chan")
-    starts, loads = [], []
-    for index, block_ref in enumerate(block_refs):
-        owner = core if index < 4 else 1 - core
-        start = pl.multiple_of(owner * HALF + (colour(owner) + index) % 4 * QUARTER, QUARTER)
-        slot = index % (AHEAD + 1)
-        starts.append(start)
-        loads.append(
-            (
-                pltpu.make_async_copy(
-                    own_ref.at[:, pl.ds(start, QUARTER)],
-                    weights.at[slot, pl.ds(0, ROWS)],
-                    own_sem.at[index],
-                ),
-                pltpu.make_async_copy(
-                    block_ref, weights.at[slot, pl.ds(ROWS, 3 * ROWS)], block_sem.at[index]
-                ),
-            )
+    first = core * HALF
+    load = pltpu.make_async_copy(own_ref.at[:, pl.ds(pl.multiple_of(first, HALF), HALF)], own, own_sem)
+    load.start()
+    rows = [
+        jnp.concatenate(
+            [
+                ref[pl.ds(pl.multiple_of((chan + shift) % 4 * ROWS, ROWS), ROWS), :].T
+                for ref in (mine_ref, theirs_ref)
+            ],
+            axis=0,
         )
-    for index in range(AHEAD):
-        for load in loads[index]:
-            load.start()
-    rows = [
-        columns_ref[pl.ds(pl.multiple_of((chan + shift) % 4 * ROWS, ROWS), ROWS), :].T
         for shift in (0, 3, 1, 2)
     ]
-    left = jnp.concatenate(rows, axis=1)
+    own_columns, near_columns, far_columns = rows[0], jnp.concatenate(rows[1:3], axis=1), rows[3]
+    load.wait()
     stores = []
-    for index in range(8):
-        for load in loads[index]:
-            load.wait()
-        if index + AHEAD < 8:
-            for load in loads[index + AHEAD]:
-                load.start()
-        results[index] = matmul(left, weights[index % (AHEAD + 1)]).astype(jnp.bfloat16)
-        store = pltpu.make_async_copy(
-            results.at[index], out_ref.at[:, pl.ds(starts[index], QUARTER)], out_sem.at[index]
-        )
-        store.start()
-        stores.append(store)
+    for index in range(4):
+        start = pl.multiple_of((colour(core) + index) % 4 * QUARTER, QUARTER)
+        total = matmul(own_columns, own[:, pl.ds(start, QUARTER)])
+        total += matmul(near_columns, near_refs[index][...])
+        total += matmul(far_columns, far_refs[index][...])
+        results[index] = total.astype(jnp.bfloat16)
+        for rank, (target, offset) in enumerate(((out_ref, first + start), (for_them_ref, start))):
+            store = pltpu.make_async_copy(
+                results.at[index, pl.ds(rank * LANES, LANES)],
+                target.at[:, pl.ds(pl.multiple_of(offset, QUARTER), QUARTER)],
+                out_sem.at[index, rank],
+            )
+            store.start()
+            stores.append(store)
     for store in stores:
         store.wait()
 
 
+def fill_kernel(half_ref, from_them_ref, out_ref, sem):
+    start = pl.multiple_of((1 - lax.axis_index("core")) * HALF, HALF)
+    copy = pltpu.make_async_copy(from_them_ref, out_ref.at[:, pl.ds(start, HALF)], sem)
+    copy.start()
+    copy.wait()
+
+
+def swapped(array):
+    return moved(array, lambda y, x, z, c: (y, x, z, 1 - c))
+
+
 def body(signal, gate, filter_taps, skip_weight, out_weight):
-    mine, parts = first_quarter(out_weight)
+    mine, (below, above, far) = first_quarter(out_weight)
     tables = transform_tables()
     packed, packed_token = call(
         pack_kernel,
@@ -288,7 +289,8 @@
         work=PACK_WORK,
         in_specs=[pl.BlockSpec(memory_space=pltpu.VMEM)] * 2 + [ANYWHERE],
     )(signal, filter_taps, mine)
-    blocks = other_quarters(parts, packed_token)
+    near = other_quarters(joined(below, above, packed_token), 1)
+    far = other_quarters(far, -1)
     arrived = lax.all_to_all(
         packed.reshape(SEQ_DEVICES, 32, LANES), AXES, split_axis=0, concat_axis=0, tiled=True
     )
@@ -301,7 +303,6 @@
         ],
         work=WORK,
     )(arrived.reshape(SEQ_DEVICES * 32, LANES), *tables)
-    weights = both_halves(blocks, convolved_token)
     returned = lax.all_to_all(
         convolved.reshape(SEQ_DEVICES, 16, LANES), AXES, split_axis=0, concat_axis=0, tiled=True
     )
@@ -316,20 +317,34 @@
         work=WORK,
     )(returned.reshape(SEQ_DEVICES * 16, LANES), signal, gate, skip_weight[:, None])
     mine = lax.all_to_all(rounded, "chan", split_axis=0, concat_axis=0, tiled=True)
-    width = out_weight.shape[1]
+    mine = mine.reshape(4 * channels, LANES)
+    half_filled, for_them = call(
+        project_kernel,
+        (
+            jax.ShapeDtypeStruct((LANES, 2 * HALF), jnp.bfloat16),
+            jax.ShapeDtypeStruct((LANES, HALF), jnp.bfloat16),
+        ),
+        [
+            pltpu.VMEM((ROWS, HALF), jnp.bfloat16),
+            pltpu.VMEM((4, 2 * LANES, QUARTER), jnp.bfloat16),
+            pltpu.SemaphoreType.DMA(()),
+            pltpu.SemaphoreType.DMA((4, 2)),
+        ],
+        limit=LAST,
+        in_specs=[pl.BlockSpec(memory_space=pltpu.VMEM)] * 2
+        + [ANYWHERE]
+        + [pl.BlockSpec(memory_space=pltpu.VMEM)] * 8,
+        out_specs=(ANYWHERE, ANYWHERE),
+    )(mine, swapped(mine), out_weight, *near, *far)
     projected = call(
-        project_kernel,
-        jax.ShapeDtypeStruct((LANES, width), jnp.bfloat16),
-        [
-            pltpu.VMEM((AHEAD + 1, 4 * ROWS, QUARTER), jnp.bfloat16),
-            pltpu.VMEM((8, LANES, QUARTER), jnp.bfloat16),
-            pltpu.SemaphoreType.DMA((8,)),
-            pltpu.SemaphoreType.DMA((8,)),
-            pltpu.SemaphoreType.DMA((8,)),
-        ],
-        in_specs=[pl.BlockSpec(memory_space=pltpu.VMEM)] + [ANYWHERE] * 9,
+        fill_kernel,
+        jax.ShapeDtypeStruct(half_filled.shape, half_filled.dtype),
+        [pltpu.SemaphoreType.DMA(())],
+        limit=2,
+        in_specs=[ANYWHERE] * 2,
         out_specs=ANYWHERE,
-    )(mine.reshape(4 * channels, LANES), out_weight, *weights)
+        input_output_aliases={0: 0},
+    )(half_filled, swapped(for_them))
     return mixed, projected
 
 

time: 111 us -> 113 us (1.018)
  blocking collectives: 12.8 us -> 0 us
  waiting for transfers between devices: 37.1 us -> 46.3 us
  starting transfers between devices: 33.5 us -> 41.4 us
  Pallas kernels: 21.5 us -> 19.7 us
    all_to_all x1, waiting for transfers between devices: 0.01 us -> 12.9 us  [body(): lax.all_to_all(packed.reshape(SEQ_DEVICES, 32, LANES), AXES, split_axis=0...]
    all_to_all x1 -> x0, blocking collectives: 12.8 us -> none  [body(): lax.all_to_all(rounded, 'chan', split_axis=0, concat_axis=0, tiled=True)]
    ppermute x10 -> x11, waiting for transfers between devices: 37.1 us -> 27.7 us  [moved(): return lax.ppermute(array, (*AXES, 'chan'), device_pairs(move))]
    all_to_all x1, waiting for transfers between devices: 0.01 us -> 5.61 us  [body(): lax.all_to_all(convolved.reshape(SEQ_DEVICES, 16, LANES), AXES, split_axi...]
    all_to_all x0 -> x1, starting transfers between devices: none -> 5.05 us  [body(): lax.all_to_all(rounded, 'chan', split_axis=0, concat_axis=0, tiled=True)]
    all_to_all x1, starting transfers between devices: 11.2 us -> 15.6 us  [body(): lax.all_to_all(packed.reshape(SEQ_DEVICES, 32, LANES), AXES, split_axis=0...]
    all_to_all x1, starting transfers between devices: 8.34 us -> 4.19 us  [body(): lax.all_to_all(convolved.reshape(SEQ_DEVICES, 16, LANES), AXES, split_axi...]
    ppermute x10 -> x11, starting transfers between devices: 14 us -> 16.6 us  [moved(): return lax.ppermute(array, (*AXES, 'chan'), device_pairs(move))]
  transfers between devices with their start and end apart: 12 -> 14, of which waited for: 3 -> 6; matrix products, arithmetic and copies ran while one was open for 1% -> 1% of each run, Pallas kernels for 11% -> 7%
where the time goes in v5:
time: 113 us
  waiting for transfers between devices  46.3 us (41%)
  starting transfers between devices  41.4 us (37%)
  Pallas kernels  19.7 us (17%)
  local copies, waits for them, and re-layouts  4.17 us (4%)
    ppermute x11, waiting for transfers between devices, moved(): return lax.ppermute(array, (*AXES, 'chan'), device_pairs(move))  27.7 us
    ppermute x11, starting transfers between devices, moved(): return lax.ppermute(array, (*AXES, 'chan'), device_pairs(move))  16.6 us
    all_to_all x1, starting transfers between devices, body(): lax.all_to_all(packed.reshape(SEQ_DEVICES, 32, LANES), AXES, split_axis=0...  15.6 us
    all_to_all x1, waiting for transfers between devices, body(): lax.all_to_all(packed.reshape(SEQ_DEVICES, 32, LANES), AXES, split_axis=0...  12.9 us
    pallas_call x1, Pallas kernels, body(): call(project_kernel, (jax.ShapeDtypeStruct((LANES, 2 * HALF), jnp.bfloat1...  7.22 us
    pallas_call x1, Pallas kernels, body(): call(convolve_kernel, (jax.ShapeDtypeStruct((SEQ_DEVICES * 16, LANES), jn...  5.91 us
    all_to_all x1, waiting for transfers between devices, body(): lax.all_to_all(convolved.reshape(SEQ_DEVICES, 16, LANES), AXES, split_axi...  5.61 us
    all_to_all x1, starting transfers between devices, body(): lax.all_to_all(rounded, 'chan', split_axis=0, concat_axis=0, tiled=True)  5.05 us
  transfers between devices with their start and end apart: 14, of which 6 were waited for; matrix products, arithmetic and copies ran while one was open for 1% of the time, Pallas kernels for 7%

profile of v5, /device:TPU:1, one launch (start us, length us, event | category | flops | bytes accessed | tf_op | source)
XLA Modules:
  0.0 112.5 jit_solution(10228640198152126780)
XLA Ops:
  0.7 1.9 %constant_dynamic-slice_fusion.after_ref = bf16[256,1024]{1,0:T(8,128)(2,1)} fusion(bf16[256,8192]{1,0:T(8,128)(2,1)} %own_ref.1, s32[]{:T(128)S(6)} %select_n.15), kind=kLoop, calls=%fused_computation | loop fusion | bytes 1048580 | tf_op jit(solution)/shard_map/dynamic_slice | solution.py:205
  2.5 0.0 copy-start.2
  2.5 0.0 copy-start.4
  2.5 3.1 %shard_map.122 = (bf16[2048,128]{1,0:T(8,128)(2,1)}, f32[8,128]{1,0:T(8,128)}) custom-call(f32[256,512]{1,0:T(8,128)} %signal_ref.3, f32[256,512]{1,0:T(8,128)} %filter_ref.1, bf16[256,1024]{1,0:T(8,128)(2,1)} %constant_dynamic-slice_fusion.after_ref), custom_call_target="tpu_custom_call" | custom-call | flops 10000000000 | tf_op jit(solution)/shard_map/pallas_call | solution.py:285
  5.7 15.6 %all-to-all-start = ((bf16[64,32,128]{2,1,0:T(8,128)(2,1)}), bf16[64,32,128]{2,1,0:T(8,128)(2,1)S(1)}, u32[]{:S(2)}, u32[]{:S(2)}) async-start(bf16[64,32,128]{2,1,0:T(8,128)(2,1)} %bitcast.9), calls=%async_computation | async-start | bytes 1048576 | tf_op jit(solution)/shard_map/all_to_all | solution.py:294
  21.3 0.0 copy-done.2
  21.3 4.5 %collective-permute-start.6 = (bf16[256,1024]{1,0:T(8,128)(2,1)S(1)}, bf16[256,1024]{1,0:T(8,128)(2,1)S(1)}, u32[]{:S(2)}, u32[]{:S(2)}) collective-permute-start(bf16[256,1024]{1,0:T(8,128)(2,1)S(1)} %copy-done.2), channel_id=1, source_target_pairs={{0,2},{4,14},{1,3},{5,15},{2,8},{6,4},{3,9},{7,5},{8,10},{12,6},{9... | collective-permute-start | bytes 1572872 | tf_op jit(solution)/shard_map/ppermute | solution.py:163
  25.8 0.7 collective-permute-start.2
  26.5 0.7 collective-permute-start.1
  27.3 0.0 copy-done.4
  27.3 0.8 copy.14.skip_ref
  28.1 12.9 %all-to-all-done = bf16[64,32,128]{2,1,0:T(8,128)(2,1)S(1)} async-done(((bf16[64,32,128]{2,1,0:T(8,128)(2,1)}), bf16[64,32,128]{2,1,0:T(8,128)(2,1)S(1)}, u32[]{:S(2)}, u32[]{:S(2)}) %all-to-all-start) | async-done | bytes 524320 | tf_op jit(solution)/shard_map/all_to_all | solution.py:294
  41.0 0.0 copy-start.1
  41.0 0.8 copy-done.1
  41.8 0.0 copy-start
  41.8 5.9 %shard_map.123 = (bf16[1024,128]{1,0:T(8,128)(2,1)}, f32[8,128]{1,0:T(8,128)}) custom-call(bf16[2048,128]{1,0:T(8,128)(2,1)} %bitcast.8, bf16[512,256]{1,0:T(8,128)(2,1)} %constant.49.clone.one_ref, bf16[256,256]{1,0:T(8,128)(2,1)} %constant.50.clone.two_ref, bf16[256,256]{1,0:T(8,128)(2,1)} %constant.51.clone.back_two_ref, ...), custom_call_target="tpu_custom_call" | custom-call | flops 99999997952 | tf_op jit(solution)/shard_map/pallas_call | solution.py:297
  47.7 4.2 %all-to-all-start.1 = ((bf16[64,16,128]{2,1,0:T(8,128)(2,1)}), bf16[64,16,128]{2,1,0:T(8,128)(2,1)S(1)}, u32[]{:S(2)}, u32[]{:S(2)}) async-start(bf16[64,16,128]{2,1,0:T(8,128)(2,1)} %bitcast.10), calls=%async_computation.1 | async-start | bytes 524288 | tf_op jit(solution)/shard_map/all_to_all | solution.py:306
  51.9 5.9 %collective-permute-done.2.above_ref = bf16[256,1024]{1,0:T(8,128)(2,1)S(1)} collective-permute-done((bf16[256,1024]{1,0:T(8,128)(2,1)S(1)}, bf16[256,1024]{1,0:T(8,128)(2,1)S(1)}, u32[]{:S(2)}, u32[]{:S(2)}) %collective-permute-start.2) | collective-permute-done | bytes 524320 | tf_op jit(solution)/shard_map/ppermute | solution.py:163
  57.8 0.0 collective-permute-done.1.below_ref
  57.8 0.0 copy-done
  57.8 0.1 shard_map.125.refs_0_
  57.9 1.4 %collective-permute-start.5 = (bf16[512,1024]{1,0:T(8,128)(2,1)S(1)}, bf16[512,1024]{1,0:T(8,128)(2,1)}, u32[]{:S(2)}, u32[]{:S(2)}) collective-permute-start(bf16[512,1024]{1,0:T(8,128)(2,1)S(1)} %shard_map.125.refs_0_), channel_id=1, source_target_pairs={{0,16},{4,68},{1,17},{5,69},{2,18},{6,70},{3,19},{7,71},{8,24},{12... | collective-permute-start | bytes 3145736 | tf_op jit(solution)/shard_map/ppermute | solution.py:163
  59.4 1.2 %collective-permute-start.4 = (bf16[512,1024]{1,0:T(8,128)(2,1)S(1)}, bf16[512,1024]{1,0:T(8,128)(2,1)}, u32[]{:S(2)}, u32[]{:S(2)}) collective-permute-start(bf16[512,1024]{1,0:T(8,128)(2,1)S(1)} %shard_map.125.refs_0_), channel_id=1, source_target_pairs={{0,64},{4,20},{1,65},{5,21},{2,66},{6,22},{3,67},{7,23},{8,72},{12... | collective-permute-start | bytes 3145736 | tf_op jit(solution)/shard_map/ppermute | solution.py:163
  60.6 1.5 %collective-permute-start.3 = (bf16[512,1024]{1,0:T(8,128)(2,1)S(1)}, bf16[512,1024]{1,0:T(8,128)(2,1)S(1)}, u32[]{:S(2)}, u32[]{:S(2)}) collective-permute-start(bf16[512,1024]{1,0:T(8,128)(2,1)S(1)} %shard_map.125.refs_0_), channel_id=1, source_target_pairs={{0,48},{4,196},{1,49},{5,197},{2,50},{6,198},{3,51},{7,199},{8,56}... | collective-permute-start | bytes 3145736 | tf_op jit(solution)/shard_map/ppermute | solution.py:163
  62.1 0.0 collective-permute-done.6.refs_4_
  62.1 0.0 collective-permute-start.9
  62.1 1.5 %collective-permute-start.8 = (bf16[256,1024]{1,0:T(8,128)(2,1)S(1)}, bf16[256,1024]{1,0:T(8,128)(2,1)}, u32[]{:S(2)}, u32[]{:S(2)}) collective-permute-start(bf16[256,1024]{1,0:T(8,128)(2,1)S(1)} %collective-permute-done.6.refs_4_), channel_id=1, source_target_pairs={{0,192},{4,52},{1,193},{5,53},{2,194},{6,54},{3,195},{7,55},{8,200... | collective-permute-start | bytes 1572872 | tf_op jit(solution)/shard_map/ppermute | solution.py:163
  63.6 5.6 %all-to-all-done.1 = bf16[64,16,128]{2,1,0:T(8,128)(2,1)S(1)} async-done(((bf16[64,16,128]{2,1,0:T(8,128)(2,1)}), bf16[64,16,128]{2,1,0:T(8,128)(2,1)S(1)}, u32[]{:S(2)}, u32[]{:S(2)}) %all-to-all-start.1) | async-done | bytes 262176 | tf_op jit(solution)/shard_map/all_to_all | solution.py:306
  69.2 0.0 copy-start.3
  69.2 0.7 copy-done.3
  69.9 2.4 %shard_map.124 = (f32[256,512]{1,0:T(8,128)}, bf16[4,256,128]{2,1,0:T(8,128)(2,1)}) custom-call(bf16[1024,128]{1,0:T(8,128)(2,1)} %bitcast.11, f32[256,512]{1,0:T(8,128)} %signal_ref.3, f32[256,512]{1,0:T(8,128)} %gate_ref.1, f32[256,1]{1,0:T(8,128)} %copy.14.skip_ref), custom_call_target="tpu_custom_call" | custom-call | flops 99999997952 | tf_op jit(solution)/shard_map/pallas_call | solution.py:310
  72.3 5.1 %all-to-all-start.2 = ((bf16[4,256,128]{2,1,0:T(8,128)(2,1)}), bf16[4,256,128]{2,1,0:T(8,128)(2,1)S(1)}, u32[]{:S(2)}, u32[]{:S(2)}) async-start(bf16[4,256,128]{2,1,0:T(8,128)(2,1)} %get-tuple-element.12), calls=%async_computation.2 | async-start | bytes 524288 | tf_op jit(solution)/shard_map/all_to_all | solution.py:319
  77.3 13.9 %collective-permute-done.9.refs_7_ = bf16[256,1024]{1,0:T(8,128)(2,1)S(1)} collective-permute-done((bf16[256,1024]{1,0:T(8,128)(2,1)S(1)}, bf16[256,1024]{1,0:T(8,128)(2,1)S(1)}, u32[]{:S(2)}, u32[]{:S(2)}) %collective-permute-start.9) | collective-permute-done | bytes 524320 | tf_op jit(solution)/shard_map/ppermute | solution.py:163
  91.2 1.2 %collective-permute-start.7 = (bf16[256,1024]{1,0:T(8,128)(2,1)S(1)}, bf16[256,1024]{1,0:T(8,128)(2,1)}, u32[]{:S(2)}, u32[]{:S(2)}) collective-permute-start(bf16[256,1024]{1,0:T(8,128)(2,1)S(1)} %collective-permute-done.6.refs_4_), channel_id=1, source_target_pairs={{0,48},{4,196},{1,49},{5,197},{2,50},{6,198},{3,51},{7,199},{8,56}... | collective-permute-start | bytes 1572872 | tf_op jit(solution)/shard_map/ppermute | solution.py:163
  92.4 0.0 collective-permute-done.8.refs_6_
  92.4 0.0 all-to-all-done.2
  92.4 1.6 %collective-permute-start = (bf16[1024,128]{1,0:T(8,128)(2,1)S(1)}, bf16[1024,128]{1,0:T(8,128)(2,1)S(1)}, u32[]{:S(2)}, u32[]{:S(2)}) collective-permute-start(bf16[1024,128]{1,0:T(8,128)(2,1)S(1)} %bitcast.6), channel_id=1, source_target_pairs={{0,4},{4,0},{1,5},{5,1},{2,6},{6,2},{3,7},{7,3},{8,12},{12,8},{9,1... | collective-permute-start | bytes 786440 | tf_op jit(solution)/shard_map/ppermute | solution.py:163
  94.0 5.6 %collective-permute-done.7.refs_5_ = bf16[256,1024]{1,0:T(8,128)(2,1)} collective-permute-done((bf16[256,1024]{1,0:T(8,128)(2,1)S(1)}, bf16[256,1024]{1,0:T(8,128)(2,1)}, u32[]{:S(2)}, u32[]{:S(2)}) %collective-permute-start.7) | collective-permute-done | bytes 524320 | tf_op jit(solution)/shard_map/ppermute | solution.py:163
  99.6 0.0 collective-permute-done.5.refs_3_
  99.6 0.0 collective-permute-done.4.refs_2_
  99.6 0.0 collective-permute-done.3.refs_1_
  99.6 0.0 collective-permute-done.theirs_ref
  99.7 7.2 %shard_map.126 = (bf16[128,8192]{1,0:T(8,128)(2,1)}, bf16[128,4096]{1,0:T(8,128)(2,1)S(1)}) custom-call(bf16[1024,128]{1,0:T(8,128)(2,1)S(1)} %bitcast.7, bf16[1024,128]{1,0:T(8,128)(2,1)S(1)} %collective-permute-done.theirs_ref, bf16[256,8192]{1,0:T(8,128)(2,1)} %own_ref.1, bf16[512,1024]{1,0:T(8,128)(2,1)S(1)} %shard_map.125.refs_0_, ...), custom_call_target="tpu_custom_call" | custom-call | tf_op jit(solution)/shard_map/pallas_call | solution.py:321
  106.9 2.2 %collective-permute-start.10 = (bf16[128,4096]{1,0:T(8,128)(2,1)S(1)}, bf16[128,4096]{1,0:T(8,128)(2,1)S(1)}, u32[]{:S(2)}, u32[]{:S(2)}) collective-permute-start(bf16[128,4096]{1,0:T(8,128)(2,1)S(1)} %get-tuple-element.15), channel_id=1, source_target_pairs={{0,4},{4,0},{1,5},{5,1},{2,6},{6,2},{3,7},{7,3},{8,12},{12,8},{9,1... | collective-permute-start | bytes 3145736 | tf_op jit(solution)/shard_map/ppermute | solution.py:163
  109.1 2.3 %collective-permute-done.10.from_them_ref = bf16[128,4096]{1,0:T(8,128)(2,1)S(1)} collective-permute-done((bf16[128,4096]{1,0:T(8,128)(2,1)S(1)}, bf16[128,4096]{1,0:T(8,128)(2,1)S(1)}, u32[]{:S(2)}, u32[]{:S(2)}) %collective-permute-start.10) | collective-permute-done | bytes 1048608 | tf_op jit(solution)/shard_map/ppermute | solution.py:163
  111.4 1.0 shard_map.127
Async XLA Ops:
  2.5 18.8 %copy-start.2 = (bf16[256,1024]{1,0:T(8,128)(2,1)S(1)}, bf16[256,1024]{1,0:T(8,128)(2,1)}, u32[]{:S(2)}) copy-start(bf16[256,1024]{1,0:T(8,128)(2,1)} %constant_dynamic-slice_fusion.after_ref) | copy-start | bytes 1572868
  2.5 24.7 %copy-start.4 = (f32[256]{0:T(256)S(1)}, f32[256]{0:T(256)}, u32[]{:S(2)}) copy-start(f32[256]{0:T(256)} %param.14) | copy-start | bytes 3076
  5.7 35.3 %all-to-all-start = ((bf16[64,32,128]{2,1,0:T(8,128)(2,1)}), bf16[64,32,128]{2,1,0:T(8,128)(2,1)S(1)}, u32[]{:S(2)}, u32[]{:S(2)}) async-start(bf16[64,32,128]{2,1,0:T(8,128)(2,1)} %bitcast.9), calls=%async_computation | async-start | bytes 1048576 | tf_op jit(solution)/shard_map/all_to_all | solution.py:294
  21.3 40.8 %collective-permute-start.6 = (bf16[256,1024]{1,0:T(8,128)(2,1)S(1)}, bf16[256,1024]{1,0:T(8,128)(2,1)S(1)}, u32[]{:S(2)}, u32[]{:S(2)}) collective-permute-start(bf16[256,1024]{1,0:T(8,128)(2,1)S(1)} %copy-done.2), channel_id=1, source_target_pairs={{0,2},{4,14},{1,3},{5,15},{2,8},{6,4},{3,9},{7,5},{8,10},{12,6},{9... | collective-permute-start | bytes 1572872 | tf_op jit(solution)/shard_map/ppermute | solution.py:163
  25.8 32.0 %collective-permute-start.2 = (bf16[256,1024]{1,0:T(8,128)(2,1)S(1)}, bf16[256,1024]{1,0:T(8,128)(2,1)S(1)}, u32[]{:S(2)}, u32[]{:S(2)}) collective-permute-start(bf16[256,1024]{1,0:T(8,128)(2,1)S(1)} %copy-done.2), channel_id=1, source_target_pairs={{0,11},{4,15},{1,0},{5,4},{2,1},{6,5},{3,2},{7,6},{8,3},{12,7},{9,... | collective-permute-start | bytes 1572872 | tf_op jit(solution)/shard_map/ppermute | solution.py:163
  26.5 31.3 %collective-permute-start.1 = (bf16[256,1024]{1,0:T(8,128)(2,1)S(1)}, bf16[256,1024]{1,0:T(8,128)(2,1)S(1)}, u32[]{:S(2)}, u32[]{:S(2)}) collective-permute-start(bf16[256,1024]{1,0:T(8,128)(2,1)S(1)} %copy-done.2), channel_id=1, source_target_pairs={{0,1},{4,5},{1,2},{5,6},{2,3},{6,7},{3,8},{7,12},{8,9},{12,13},{9,... | collective-permute-start | bytes 1572872 | tf_op jit(solution)/shard_map/ppermute | solution.py:163
  41.0 0.8 copy-start.1
  41.8 16.1 %copy-start = (f32[8,128]{1,0:T(8,128)S(1)}, f32[8,128]{1,0:T(8,128)}, u32[]{:S(2)}) copy-start(f32[8,128]{1,0:T(8,128)} %get-tuple-element.13.after_ref) | copy-start | bytes 12292
  47.7 21.5 %all-to-all-start.1 = ((bf16[64,16,128]{2,1,0:T(8,128)(2,1)}), bf16[64,16,128]{2,1,0:T(8,128)(2,1)S(1)}, u32[]{:S(2)}, u32[]{:S(2)}) async-start(bf16[64,16,128]{2,1,0:T(8,128)(2,1)} %bitcast.10), calls=%async_computation.1 | async-start | bytes 524288 | tf_op jit(solution)/shard_map/all_to_all | solution.py:306
  57.9 41.7 %collective-permute-start.5 = (bf16[512,1024]{1,0:T(8,128)(2,1)S(1)}, bf16[512,1024]{1,0:T(8,128)(2,1)}, u32[]{:S(2)}, u32[]{:S(2)}) collective-permute-start(bf16[512,1024]{1,0:T(8,128)(2,1)S(1)} %shard_map.125.refs_0_), channel_id=1, source_target_pairs={{0,16},{4,68},{1,17},{5,69},{2,18},{6,70},{3,19},{7,71},{8,24},{12... | collective-permute-start | bytes 3145736 | tf_op jit(solution)/shard_map/ppermute | solution.py:163
  59.4 40.3 %collective-permute-start.4 = (bf16[512,1024]{1,0:T(8,128)(2,1)S(1)}, bf16[512,1024]{1,0:T(8,128)(2,1)}, u32[]{:S(2)}, u32[]{:S(2)}) collective-permute-start(bf16[512,1024]{1,0:T(8,128)(2,1)S(1)} %shard_map.125.refs_0_), channel_id=1, source_target_pairs={{0,64},{4,20},{1,65},{5,21},{2,66},{6,22},{3,67},{7,23},{8,72},{12... | collective-permute-start | bytes 3145736 | tf_op jit(solution)/shard_map/ppermute | solution.py:163
  60.6 39.1 %collective-permute-start.3 = (bf16[512,1024]{1,0:T(8,128)(2,1)S(1)}, bf16[512,1024]{1,0:T(8,128)(2,1)S(1)}, u32[]{:S(2)}, u32[]{:S(2)}) collective-permute-start(bf16[512,1024]{1,0:T(8,128)(2,1)S(1)} %shard_map.125.refs_0_), channel_id=1, source_target_pairs={{0,48},{4,196},{1,49},{5,197},{2,50},{6,198},{3,51},{7,199},{8,56}... | collective-permute-start | bytes 3145736 | tf_op jit(solution)/shard_map/ppermute | solution.py:163
  62.1 29.1 %collective-permute-start.9 = (bf16[256,1024]{1,0:T(8,128)(2,1)S(1)}, bf16[256,1024]{1,0:T(8,128)(2,1)S(1)}, u32[]{:S(2)}, u32[]{:S(2)}) collective-permute-start(bf16[256,1024]{1,0:T(8,128)(2,1)S(1)} %collective-permute-done.6.refs_4_), channel_id=1, source_target_pairs={{0,16},{4,68},{1,17},{5,69},{2,18},{6,70},{3,19},{7,71},{8,24},{12... | collective-permute-start | bytes 1572872 | tf_op jit(solution)/shard_map/ppermute | solution.py:163
  62.1 30.3 %collective-permute-start.8 = (bf16[256,1024]{1,0:T(8,128)(2,1)S(1)}, bf16[256,1024]{1,0:T(8,128)(2,1)}, u32[]{:S(2)}, u32[]{:S(2)}) collective-permute-start(bf16[256,1024]{1,0:T(8,128)(2,1)S(1)} %collective-permute-done.6.refs_4_), channel_id=1, source_target_pairs={{0,192},{4,52},{1,193},{5,53},{2,194},{6,54},{3,195},{7,55},{8,200... | collective-permute-start | bytes 1572872 | tf_op jit(solution)/shard_map/ppermute | solution.py:163
  69.2 0.7 copy-start.3
  72.3 20.2 %all-to-all-start.2 = ((bf16[4,256,128]{2,1,0:T(8,128)(2,1)}), bf16[4,256,128]{2,1,0:T(8,128)(2,1)S(1)}, u32[]{:S(2)}, u32[]{:S(2)}) async-start(bf16[4,256,128]{2,1,0:T(8,128)(2,1)} %get-tuple-element.12), calls=%async_computation.2 | async-start | bytes 524288 | tf_op jit(solution)/shard_map/all_to_all | solution.py:319
  91.2 8.4 %collective-permute-start.7 = (bf16[256,1024]{1,0:T(8,128)(2,1)S(1)}, bf16[256,1024]{1,0:T(8,128)(2,1)}, u32[]{:S(2)}, u32[]{:S(2)}) collective-permute-start(bf16[256,1024]{1,0:T(8,128)(2,1)S(1)} %collective-permute-done.6.refs_4_), channel_id=1, source_target_pairs={{0,48},{4,196},{1,49},{5,197},{2,50},{6,198},{3,51},{7,199},{8,56}... | collective-permute-start | bytes 1572872 | tf_op jit(solution)/shard_map/ppermute | solution.py:163
  92.4 7.2 %collective-permute-start = (bf16[1024,128]{1,0:T(8,128)(2,1)S(1)}, bf16[1024,128]{1,0:T(8,128)(2,1)S(1)}, u32[]{:S(2)}, u32[]{:S(2)}) collective-permute-start(bf16[1024,128]{1,0:T(8,128)(2,1)S(1)} %bitcast.6), channel_id=1, source_target_pairs={{0,4},{4,0},{1,5},{5,1},{2,6},{6,2},{3,7},{7,3},{8,12},{12,8},{9,1... | collective-permute-start | bytes 786440 | tf_op jit(solution)/shard_map/ppermute | solution.py:163
  106.9 4.5 %collective-permute-start.10 = (bf16[128,4096]{1,0:T(8,128)(2,1)S(1)}, bf16[128,4096]{1,0:T(8,128)(2,1)S(1)}, u32[]{:S(2)}, u32[]{:S(2)}) collective-permute-start(bf16[128,4096]{1,0:T(8,128)(2,1)S(1)} %get-tuple-element.15), channel_id=1, source_target_pairs={{0,4},{4,0},{1,5},{5,1},{2,6},{6,2},{3,7},{7,3},{8,12},{12,8},{9,1... | collective-permute-start | bytes 3145736 | tf_op jit(solution)/shard_map/ppermute | solution.py:163

commit v6 on v5

--- a/solution.py
+++ b/solution.py
@@ -22,7 +22,6 @@
 LAST = 48
 WORK = 10**11
 PACK_WORK = 10**10
-JOIN_WORK = 10**10
 
 
 def transform_tables():
@@ -60,7 +59,6 @@
                     piece * LANES : (piece + 1) * LANES,
                 ]
     out_ref[...] = wide[...].astype(jnp.bfloat16)
-    token_ref[...] = jnp.zeros_like(token_ref)
 
 
 def matmul(left, right):
@@ -76,7 +74,6 @@
     cos_ref,
     sin_ref,
     out_ref,
-    token_ref,
     wide,
     result,
 ):
@@ -121,7 +118,6 @@
                 piece * SEQ_DEVICES : (piece + 1) * SEQ_DEVICES
             ]
     out_ref[...] = result[...].astype(jnp.bfloat16)
-    token_ref[...] = jnp.zeros_like(token_ref)
 
 
 def mix_kernel(conv_ref, signal_ref, gate_ref, skip_ref, mixed_ref, rounded_ref, wide):
@@ -168,7 +164,7 @@
     return jnp.where(core == 0, x + 2 * y, 2 * x + y) % 4
 
 
-def join_kernel(below_ref, above_ref, after_ref, out_ref, sem):
+def join_kernel(below_ref, above_ref, after_ref, out_ref, token_ref, sem):
     copies = [
         pltpu.make_async_copy(ref, out_ref.at[pl.ds(index * ROWS, ROWS)], sem.at[index])
         for index, ref in enumerate((below_ref, above_ref))
@@ -179,7 +175,7 @@
         copy.wait()
 
 
-def keep_kernel(block_ref, after_ref, out_ref):
+def keep_kernel(block_ref, *refs):
     pass
 
 
@@ -187,16 +183,25 @@
 TOKEN = jax.ShapeDtypeStruct((8, LANES), jnp.float32)
 
 
-def ordered(block, after):
+def ordered(block, *after):
     return call(
         keep_kernel,
         jax.ShapeDtypeStruct(block.shape, block.dtype),
         [],
-        limit=2,
-        in_specs=[ANYWHERE] * 2,
+        in_specs=[ANYWHERE] * (1 + len(after)),
         out_specs=ANYWHERE,
         input_output_aliases={0: 0},
-    )(block, after)
+    )(block, *after)
+
+
+def nothing_kernel(*refs):
+    pass
+
+
+def token_of(*blocks):
+    return call(
+        nothing_kernel, TOKEN, [], limit=2, in_specs=[ANYWHERE] * len(blocks), out_specs=ANYWHERE
+    )(*blocks)
 
 
 def first_quarter(out_weight):
@@ -205,19 +210,17 @@
     mine = lax.dynamic_slice_in_dim(out_weight, start, QUARTER, 1)
     below = moved(mine, lambda y, x, z, c: (y, x, z + 1, c))
     above = moved(mine, lambda y, x, z, c: (y, x, z - 1, c))
-    far = moved(mine, lambda y, x, z, c: (y, x, z + 2 - 4 * c, c))
-    return mine, (below, above, far)
+    return mine, below, above
 
 
 def joined(below, above, after):
     return call(
         join_kernel,
-        jax.ShapeDtypeStruct((2 * ROWS, QUARTER), jnp.bfloat16),
+        (jax.ShapeDtypeStruct((2 * ROWS, QUARTER), jnp.bfloat16), TOKEN),
         [pltpu.SemaphoreType.DMA((2,))],
         limit=2,
-        work=JOIN_WORK,
         in_specs=[ANYWHERE] * 3,
-        out_specs=ANYWHERE,
+        out_specs=(ANYWHERE, ANYWHERE),
     )(below, above, after)
 
 
@@ -252,10 +255,12 @@
     stores = []
     for index in range(4):
         start = pl.multiple_of((colour(core) + index) % 4 * QUARTER, QUARTER)
-        total = matmul(own_columns, own[:, pl.ds(start, QUARTER)])
-        total += matmul(near_columns, near_refs[index][...])
-        total += matmul(far_columns, far_refs[index][...])
-        results[index] = total.astype(jnp.bfloat16)
+        for tile in range(0, QUARTER, ROWS):
+            lanes = slice(tile, tile + ROWS)
+            total = matmul(own_columns, own[:, pl.ds(pl.multiple_of(start + tile, ROWS), ROWS)])
+            total += matmul(near_columns, near_refs[index][:, lanes])
+            total += matmul(far_columns, far_refs[index][:, lanes])
+            results[index, :, lanes] = total.astype(jnp.bfloat16)
         for rank, (target, offset) in enumerate(((out_ref, first + start), (for_them_ref, start))):
             store = pltpu.make_async_copy(
                 results.at[index, pl.ds(rank * LANES, LANES)],
@@ -280,7 +285,7 @@
 
 
 def body(signal, gate, filter_taps, skip_weight, out_weight):
-    mine, (below, above, far) = first_quarter(out_weight)
+    mine, below, above = first_quarter(out_weight)
     tables = transform_tables()
     packed, packed_token = call(
         pack_kernel,
@@ -288,24 +293,30 @@
         [pltpu.VMEM((SEQ_DEVICES * 32, LANES), jnp.float32)],
         work=PACK_WORK,
         in_specs=[pl.BlockSpec(memory_space=pltpu.VMEM)] * 2 + [ANYWHERE],
+        out_specs=(pl.BlockSpec(memory_space=pltpu.VMEM), ANYWHERE),
     )(signal, filter_taps, mine)
-    near = other_quarters(joined(below, above, packed_token), 1)
-    far = other_quarters(far, -1)
+    near, near_token = joined(below, above, packed_token)
+    packed = ordered(packed, near_token)
+    near = other_quarters(near, 1)
+    far = moved(ordered(mine, near_token), lambda y, x, z, c: (y, x, z + 2 - 4 * c, c))
     arrived = lax.all_to_all(
         packed.reshape(SEQ_DEVICES, 32, LANES), AXES, split_axis=0, concat_axis=0, tiled=True
     )
-    convolved, convolved_token = call(
+    convolved = call(
         convolve_kernel,
-        (jax.ShapeDtypeStruct((SEQ_DEVICES * 16, LANES), jnp.bfloat16), TOKEN),
+        jax.ShapeDtypeStruct((SEQ_DEVICES * 16, LANES), jnp.bfloat16),
         [
             pltpu.VMEM((SEQ_DEVICES * 32, LANES), jnp.float32),
             pltpu.VMEM((SEQ_DEVICES * 16, LANES), jnp.float32),
         ],
         work=WORK,
     )(arrived.reshape(SEQ_DEVICES * 32, LANES), *tables)
+    convolved = ordered(convolved, token_of(far, *near[1:]))
+    far = other_quarters(far, -1)
     returned = lax.all_to_all(
         convolved.reshape(SEQ_DEVICES, 16, LANES), AXES, split_axis=0, concat_axis=0, tiled=True
     )
+    returned = returned.reshape(SEQ_DEVICES * 16, LANES)
     channels, shard_len = signal.shape
     mixed, rounded = call(
         mix_kernel,
@@ -315,7 +326,8 @@
         ),
         [pltpu.VMEM((SEQ_DEVICES * 16, LANES), jnp.float32)],
         work=WORK,
-    )(returned.reshape(SEQ_DEVICES * 16, LANES), signal, gate, skip_weight[:, None])
+    )(returned, signal, gate, skip_weight[:, None])
+    rounded = ordered(rounded, token_of(*far[1:]))
     mine = lax.all_to_all(rounded, "chan", split_axis=0, concat_axis=0, tiled=True)
     mine = mine.reshape(4 * channels, LANES)
     half_filled, for_them = call(

time: 113 us -> 126 us (1.12)
  blocking collectives: 0 us -> 12.5 us
  waiting for transfers between devices: 46.3 us -> 43.7 us
  Pallas kernels: 19.7 us -> 21.2 us
    all_to_all x1, waiting for transfers between devices: 12.9 us -> 0.01 us  [body(): lax.all_to_all(packed.reshape(SEQ_DEVICES, 32, LANES), AXES, split_axis=0...]
    all_to_all x0 -> x1, blocking collectives: none -> 12.5 us  [body(): lax.all_to_all(rounded, 'chan', split_axis=0, concat_axis=0, tiled=True)]
    ppermute x11, starting transfers between devices: 16.6 us -> 24.1 us  [moved(): return lax.ppermute(array, (*AXES, 'chan'), device_pairs(move))]
    all_to_all x1, waiting for transfers between devices: 5.61 us -> 12.6 us  [body(): lax.all_to_all(convolved.reshape(SEQ_DEVICES, 16, LANES), AXES, split_axi...]
    all_to_all x1 -> x0, starting transfers between devices: 5.05 us -> none  [body(): lax.all_to_all(rounded, 'chan', split_axis=0, concat_axis=0, tiled=True)]
    all_to_all x1, starting transfers between devices: 15.6 us -> 10.6 us  [body(): lax.all_to_all(packed.reshape(SEQ_DEVICES, 32, LANES), AXES, split_axis=0...]
    all_to_all x1, starting transfers between devices: 4.19 us -> 7.75 us  [body(): lax.all_to_all(convolved.reshape(SEQ_DEVICES, 16, LANES), AXES, split_axi...]
    ppermute x11, waiting for transfers between devices: 27.7 us -> 31.1 us  [moved(): return lax.ppermute(array, (*AXES, 'chan'), device_pairs(move))]
  transfers between devices with their start and end apart: 14 -> 13, of which waited for: 6 -> 6; matrix products, arithmetic and copies ran while one was open for 1% -> 1% of each run, Pallas kernels for 7% -> 7%
where the time goes in v6:
time: 126 us
  waiting for transfers between devices  43.7 us (35%)
  starting transfers between devices  42.4 us (34%)
  Pallas kernels  21.2 us (17%)
  blocking collectives  12.5 us (10%)
  local copies, waits for them, and re-layouts  5.03 us (4%)
    ppermute x11, waiting for transfers between devices, moved(): return lax.ppermute(array, (*AXES, 'chan'), device_pairs(move))  31.1 us
    ppermute x11, starting transfers between devices, moved(): return lax.ppermute(array, (*AXES, 'chan'), device_pairs(move))  24.1 us
    all_to_all x1, waiting for transfers between devices, body(): lax.all_to_all(convolved.reshape(SEQ_DEVICES, 16, LANES), AXES, split_axi...  12.6 us
    all_to_all x1, blocking collectives, body(): lax.all_to_all(rounded, 'chan', split_axis=0, concat_axis=0, tiled=True)  12.5 us
    all_to_all x1, starting transfers between devices, body(): lax.all_to_all(packed.reshape(SEQ_DEVICES, 32, LANES), AXES, split_axis=0...  10.6 us
    pallas_call x1, Pallas kernels, body(): call(project_kernel, (jax.ShapeDtypeStruct((LANES, 2 * HALF), jnp.bfloat1...  7.79 us
    all_to_all x1, starting transfers between devices, body(): lax.all_to_all(convolved.reshape(SEQ_DEVICES, 16, LANES), AXES, split_axi...  7.75 us
    pallas_call x1, Pallas kernels, body(): call(convolve_kernel, jax.ShapeDtypeStruct((SEQ_DEVICES * 16, LANES), jnp...  5.9 us
  transfers between devices with their start and end apart: 13, of which 6 were waited for; matrix products, arithmetic and copies ran while one was open for 1% of the time, Pallas kernels for 7%

profile of v6, /device:TPU:1, one launch (start us, length us, event | category | flops | bytes accessed | tf_op | source)
XLA Modules:
  0.0 125.8 jit_solution(5877359520545099929)
XLA Ops:
  0.7 1.1 constant_dynamic-slice_fusion.after_ref.block_ref
  1.7 0.0 copy-start.6
  1.8 6.5 %collective-permute-start.1 = (bf16[256,1024]{1,0:T(8,128)(2,1)S(1)}, bf16[256,1024]{1,0:T(8,128)(2,1)S(1)}, u32[]{:S(2)}, u32[]{:S(2)}) collective-permute-start(bf16[256,1024]{1,0:T(8,128)(2,1)S(1)} %constant_dynamic-slice_fusion.after_ref.block_ref), channel_id=1, source_target_pairs={{0,11},{4,15},{1,0},{5,4},{2,1},{6,5},{3,2},{7,6},{8,3},{12,7},{9,... | collective-permute-start | bytes 1572872 | tf_op jit(solution)/shard_map/ppermute | solution.py:159
  8.2 0.0 collective-permute-start
  8.2 0.0 copy-done.6
  8.2 3.1 %shard_map.122 = (bf16[2048,128]{1,0:T(8,128)(2,1)}, f32[8,128]{1,0:T(8,128)}) custom-call(f32[256,512]{1,0:T(8,128)} %signal_ref.3, f32[256,512]{1,0:T(8,128)} %filter_ref.1, bf16[256,1024]{1,0:T(8,128)(2,1)} %copy-done.6), custom_call_target="tpu_custom_call" | custom-call | flops 10000000000 | tf_op jit(solution)/shard_map/pallas_call | solution.py:290
  11.3 7.5 %collective-permute-done.1.above_ref = bf16[256,1024]{1,0:T(8,128)(2,1)S(1)} collective-permute-done((bf16[256,1024]{1,0:T(8,128)(2,1)S(1)}, bf16[256,1024]{1,0:T(8,128)(2,1)S(1)}, u32[]{:S(2)}, u32[]{:S(2)}) %collective-permute-start.1) | collective-permute-done | bytes 524320 | tf_op jit(solution)/shard_map/ppermute | solution.py:159
  18.8 3.1 %collective-permute-done.below_ref = bf16[256,1024]{1,0:T(8,128)(2,1)S(1)} collective-permute-done((bf16[256,1024]{1,0:T(8,128)(2,1)S(1)}, bf16[256,1024]{1,0:T(8,128)(2,1)S(1)}, u32[]{:S(2)}, u32[]{:S(2)}) %collective-permute-start) | collective-permute-done | bytes 524320 | tf_op jit(solution)/shard_map/ppermute | solution.py:159
  21.9 0.7 copy-done.5
  22.6 1.0 shard_map.123
  23.6 0.0 copy-start.2
  23.6 0.6 copy-done.2
  24.2 1.3 %collective-permute-start.5 = (bf16[512,1024]{1,0:T(8,128)(2,1)}, bf16[512,1024]{1,0:T(8,128)(2,1)S(1)}, u32[]{:S(2)}, u32[]{:S(2)}) collective-permute-start(bf16[512,1024]{1,0:T(8,128)(2,1)} %get-tuple-element.13.refs_0_), channel_id=1, source_target_pairs={{0,16},{4,68},{1,17},{5,69},{2,18},{6,70},{3,19},{7,71},{8,24},{12... | collective-permute-start | bytes 3145736 | tf_op jit(solution)/shard_map/ppermute | solution.py:159
  25.5 10.6 %all-to-all-start = ((bf16[64,32,128]{2,1,0:T(8,128)(2,1)}), bf16[64,32,128]{2,1,0:T(8,128)(2,1)}, u32[]{:S(2)}, u32[]{:S(2)}) async-start(bf16[64,32,128]{2,1,0:T(8,128)(2,1)} %bitcast.8), calls=%async_computation | async-start | bytes 1048576 | tf_op jit(solution)/shard_map/all_to_all | solution.py:302
  36.1 3.9 %collective-permute-start.2 = (bf16[256,1024]{1,0:T(8,128)(2,1)}, bf16[256,1024]{1,0:T(8,128)(2,1)}, u32[]{:S(2)}, u32[]{:S(2)}) collective-permute-start(bf16[256,1024]{1,0:T(8,128)(2,1)} %shard_map.126), channel_id=1, source_target_pairs={{0,2},{4,14},{1,3},{5,15},{2,8},{6,4},{3,9},{7,5},{8,10},{12,6},{9... | collective-permute-start | bytes 1572872 | tf_op jit(solution)/shard_map/ppermute | solution.py:159
  40.0 1.2 collective-permute-start.4
  41.2 2.6 %collective-permute-start.3 = (bf16[512,1024]{1,0:T(8,128)(2,1)}, bf16[512,1024]{1,0:T(8,128)(2,1)S(1)}, u32[]{:S(2)}, u32[]{:S(2)}) collective-permute-start(bf16[512,1024]{1,0:T(8,128)(2,1)} %get-tuple-element.13.refs_0_), channel_id=1, source_target_pairs={{0,48},{4,196},{1,49},{5,197},{2,50},{6,198},{3,51},{7,199},{8,56}... | collective-permute-start | bytes 3145736 | tf_op jit(solution)/shard_map/ppermute | solution.py:159
  43.9 17.1 %collective-permute-done.2.refs_0_.refs_4_ = bf16[256,1024]{1,0:T(8,128)(2,1)} collective-permute-done((bf16[256,1024]{1,0:T(8,128)(2,1)}, bf16[256,1024]{1,0:T(8,128)(2,1)}, u32[]{:S(2)}, u32[]{:S(2)}) %collective-permute-start.2) | collective-permute-done | bytes 524320 | tf_op jit(solution)/shard_map/ppermute | solution.py:159
  60.9 1.4 %collective-permute-start.8 = (bf16[256,1024]{1,0:T(8,128)(2,1)}, bf16[256,1024]{1,0:T(8,128)(2,1)}, u32[]{:S(2)}, u32[]{:S(2)}) collective-permute-start(bf16[256,1024]{1,0:T(8,128)(2,1)} %collective-permute-done.2.refs_0_.refs_4_), channel_id=1, source_target_pairs={{0,16},{4,68},{1,17},{5,69},{2,18},{6,70},{3,19},{7,71},{8,24},{12... | collective-permute-start | bytes 1572872 | tf_op jit(solution)/shard_map/ppermute | solution.py:159
  62.3 2.5 %collective-permute-start.7 = (bf16[256,1024]{1,0:T(8,128)(2,1)}, bf16[256,1024]{1,0:T(8,128)(2,1)}, u32[]{:S(2)}, u32[]{:S(2)}) collective-permute-start(bf16[256,1024]{1,0:T(8,128)(2,1)} %collective-permute-done.2.refs_0_.refs_4_), channel_id=1, source_target_pairs={{0,192},{4,52},{1,193},{5,53},{2,194},{6,54},{3,195},{7,55},{8,200... | collective-permute-start | bytes 1572872 | tf_op jit(solution)/shard_map/ppermute | solution.py:159
  64.8 0.0 collective-permute-done.5.refs_3_
  64.8 1.4 %collective-permute-start.6 = (bf16[256,1024]{1,0:T(8,128)(2,1)}, bf16[256,1024]{1,0:T(8,128)(2,1)}, u32[]{:S(2)}, u32[]{:S(2)}) collective-permute-start(bf16[256,1024]{1,0:T(8,128)(2,1)} %collective-permute-done.2.refs_0_.refs_4_), channel_id=1, source_target_pairs={{0,48},{4,196},{1,49},{5,197},{2,50},{6,198},{3,51},{7,199},{8,56}... | collective-permute-start | bytes 1572872 | tf_op jit(solution)/shard_map/ppermute | solution.py:159
  66.2 0.0 all-to-all-done
  66.2 5.9 %shard_map.125.block_ref = bf16[1024,128]{1,0:T(8,128)(2,1)} custom-call(bf16[2048,128]{1,0:T(8,128)(2,1)} %bitcast.1.data_ref, bf16[512,256]{1,0:T(8,128)(2,1)} %constant.49.clone.one_ref, bf16[256,256]{1,0:T(8,128)(2,1)} %constant.50.clone.two_ref, bf16[256,256]{1,0:T(8,128)(2,1)} %constant.51.clone.back_two_ref, ...), custom_call_target="tpu_custom_call" | custom-call | flops 99999997952 | tf_op jit(solution)/shard_map/pallas_call | solution.py:305
  72.1 0.0 collective-permute-done.4.refs_2_
  72.1 0.0 collective-permute-done.3.refs_1_
  72.1 0.0 copy-done
  72.1 0.0 copy-start.4
  72.2 0.6 copy-done.4
  72.7 7.8 %all-to-all-start.1 = ((bf16[64,16,128]{2,1,0:T(8,128)(2,1)}), bf16[64,16,128]{2,1,0:T(8,128)(2,1)S(1)}, u32[]{:S(2)}, u32[]{:S(2)}) async-start(bf16[64,16,128]{2,1,0:T(8,128)(2,1)} %bitcast.9), calls=%async_computation.1 | async-start | bytes 524288 | tf_op jit(solution)/shard_map/all_to_all | solution.py:316
  80.5 0.0 copy-done.8
  80.5 0.8 copy.18.skip_ref
  81.3 0.0 collective-permute-done.8.refs_2_.refs_7_
  81.3 0.0 collective-permute-done.7.refs_1_.refs_6_
  81.3 0.0 collective-permute-done.6.refs_0_.refs_5_
  81.3 0.0 copy-start.3
  81.3 0.6 copy-done.3
  81.9 12.6 %all-to-all-done.1 = bf16[64,16,128]{2,1,0:T(8,128)(2,1)S(1)} async-done(((bf16[64,16,128]{2,1,0:T(8,128)(2,1)}), bf16[64,16,128]{2,1,0:T(8,128)(2,1)S(1)}, u32[]{:S(2)}, u32[]{:S(2)}) %all-to-all-start.1) | async-done | bytes 262176 | tf_op jit(solution)/shard_map/all_to_all | solution.py:316
  94.5 0.7 copy-done.7
  95.2 2.4 %shard_map.129 = (f32[256,512]{1,0:T(8,128)}, bf16[4,256,128]{2,1,0:T(8,128)(2,1)}) custom-call(bf16[1024,128]{1,0:T(8,128)(2,1)} %bitcast.10, f32[256,512]{1,0:T(8,128)} %signal_ref.3, f32[256,512]{1,0:T(8,128)} %gate_ref.1, f32[256,1]{1,0:T(8,128)} %copy.18.skip_ref), custom_call_target="tpu_custom_call" | custom-call | flops 99999997952 | tf_op jit(solution)/shard_map/pallas_call | solution.py:321
  97.6 0.0 copy-done.1
  97.6 12.5 %all_to_all.15 = bf16[4,256,128]{2,1,0:T(8,128)(2,1)S(1)} all-to-all(bf16[4,256,128]{2,1,0:T(8,128)(2,1)} %shard_map.131), channel_id=1, replica_groups=mesh['y'=4,'x'=4,'zh'=2,'core'=2,'chan'=4] {'chan'}, dimensions={0} | all-to-all | bytes 524288 | tf_op jit(solution)/shard_map/all_to_all | solution.py:331
  110.2 2.8 %collective-permute-start.9 = (bf16[1024,128]{1,0:T(8,128)(2,1)S(1)}, bf16[1024,128]{1,0:T(8,128)(2,1)S(1)}, u32[]{:S(2)}, u32[]{:S(2)}) collective-permute-start(bf16[1024,128]{1,0:T(8,128)(2,1)S(1)} %bitcast.6), channel_id=1, source_target_pairs={{0,4},{4,0},{1,5},{5,1},{2,6},{6,2},{3,7},{7,3},{8,12},{12,8},{9,1... | collective-permute-start | bytes 786440 | tf_op jit(solution)/shard_map/ppermute | solution.py:159
  113.0 1.2 collective-permute-done.9.theirs_ref
  114.2 7.8 %shard_map.132 = (bf16[128,8192]{1,0:T(8,128)(2,1)}, bf16[128,4096]{1,0:T(8,128)(2,1)S(1)}) custom-call(bf16[1024,128]{1,0:T(8,128)(2,1)S(1)} %bitcast.7, bf16[1024,128]{1,0:T(8,128)(2,1)S(1)} %collective-permute-done.9.theirs_ref, bf16[256,8192]{1,0:T(8,128)(2,1)} %own_ref.1, bf16[512,1024]{1,0:T(8,128)(2,1)} %get-tuple-element.13.refs_0_, ...), custom_call_target="tpu_custom_call" | custom-call | tf_op jit(solution)/shard_map/pallas_call | solution.py:333
  122.0 0.5 collective-permute-start.10
  122.4 2.3 %collective-permute-done.10.from_them_ref = bf16[128,4096]{1,0:T(8,128)(2,1)S(1)} collective-permute-done((bf16[128,4096]{1,0:T(8,128)(2,1)S(1)}, bf16[128,4096]{1,0:T(8,128)(2,1)S(1)}, u32[]{:S(2)}, u32[]{:S(2)}) %collective-permute-start.10) | collective-permute-done | bytes 1048608 | tf_op jit(solution)/shard_map/ppermute | solution.py:159
  124.7 1.0 shard_map.133
  (11 shorter events, 0.0 us)
Async XLA Ops:
  1.7 6.5 %copy-start.6 = (bf16[256,1024]{1,0:T(8,128)(2,1)}, bf16[256,1024]{1,0:T(8,128)(2,1)S(1)}, u32[]{:S(2)}) copy-start(bf16[256,1024]{1,0:T(8,128)(2,1)S(1)} %constant_dynamic-slice_fusion.after_ref.block_ref) | copy-start | bytes 1572868
  1.8 17.1 %collective-permute-start.1 = (bf16[256,1024]{1,0:T(8,128)(2,1)S(1)}, bf16[256,1024]{1,0:T(8,128)(2,1)S(1)}, u32[]{:S(2)}, u32[]{:S(2)}) collective-permute-start(bf16[256,1024]{1,0:T(8,128)(2,1)S(1)} %constant_dynamic-slice_fusion.after_ref.block_ref), channel_id=1, source_target_pairs={{0,11},{4,15},{1,0},{5,4},{2,1},{6,5},{3,2},{7,6},{8,3},{12,7},{9,... | collective-permute-start | bytes 1572872 | tf_op jit(solution)/shard_map/ppermute | solution.py:159
  8.2 13.7 %collective-permute-start = (bf16[256,1024]{1,0:T(8,128)(2,1)S(1)}, bf16[256,1024]{1,0:T(8,128)(2,1)S(1)}, u32[]{:S(2)}, u32[]{:S(2)}) collective-permute-start(bf16[256,1024]{1,0:T(8,128)(2,1)S(1)} %constant_dynamic-slice_fusion.after_ref.block_ref), channel_id=1, source_target_pairs={{0,1},{4,5},{1,2},{5,6},{2,3},{6,7},{3,8},{7,12},{8,9},{12,13},{9,... | collective-permute-start | bytes 1572872 | tf_op jit(solution)/shard_map/ppermute | solution.py:159
  21.9 0.7 copy-start.5
  23.6 0.6 copy-start.2
  24.2 40.5 %collective-permute-start.5 = (bf16[512,1024]{1,0:T(8,128)(2,1)}, bf16[512,1024]{1,0:T(8,128)(2,1)S(1)}, u32[]{:S(2)}, u32[]{:S(2)}) collective-permute-start(bf16[512,1024]{1,0:T(8,128)(2,1)} %get-tuple-element.13.refs_0_), channel_id=1, source_target_pairs={{0,16},{4,68},{1,17},{5,69},{2,18},{6,70},{3,19},{7,71},{8,24},{12... | collective-permute-start | bytes 3145736 | tf_op jit(solution)/shard_map/ppermute | solution.py:159
  25.5 40.7 %all-to-all-start = ((bf16[64,32,128]{2,1,0:T(8,128)(2,1)}), bf16[64,32,128]{2,1,0:T(8,128)(2,1)}, u32[]{:S(2)}, u32[]{:S(2)}) async-start(bf16[64,32,128]{2,1,0:T(8,128)(2,1)} %bitcast.8), calls=%async_computation | async-start | bytes 1048576 | tf_op jit(solution)/shard_map/all_to_all | solution.py:302
  36.1 24.8 %collective-permute-start.2 = (bf16[256,1024]{1,0:T(8,128)(2,1)}, bf16[256,1024]{1,0:T(8,128)(2,1)}, u32[]{:S(2)}, u32[]{:S(2)}) collective-permute-start(bf16[256,1024]{1,0:T(8,128)(2,1)} %shard_map.126), channel_id=1, source_target_pairs={{0,2},{4,14},{1,3},{5,15},{2,8},{6,4},{3,9},{7,5},{8,10},{12,6},{9... | collective-permute-start | bytes 1572872 | tf_op jit(solution)/shard_map/ppermute | solution.py:159
  40.0 32.1 %collective-permute-start.4 = (bf16[512,1024]{1,0:T(8,128)(2,1)}, bf16[512,1024]{1,0:T(8,128)(2,1)S(1)}, u32[]{:S(2)}, u32[]{:S(2)}) collective-permute-start(bf16[512,1024]{1,0:T(8,128)(2,1)} %get-tuple-element.13.refs_0_), channel_id=1, source_target_pairs={{0,64},{4,20},{1,65},{5,21},{2,66},{6,22},{3,67},{7,23},{8,72},{12... | collective-permute-start | bytes 3145736 | tf_op jit(solution)/shard_map/ppermute | solution.py:159
  41.2 30.9 %collective-permute-start.3 = (bf16[512,1024]{1,0:T(8,128)(2,1)}, bf16[512,1024]{1,0:T(8,128)(2,1)S(1)}, u32[]{:S(2)}, u32[]{:S(2)}) collective-permute-start(bf16[512,1024]{1,0:T(8,128)(2,1)} %get-tuple-element.13.refs_0_), channel_id=1, source_target_pairs={{0,48},{4,196},{1,49},{5,197},{2,50},{6,198},{3,51},{7,199},{8,56}... | collective-permute-start | bytes 3145736 | tf_op jit(solution)/shard_map/ppermute | solution.py:159
  60.9 20.4 %collective-permute-start.8 = (bf16[256,1024]{1,0:T(8,128)(2,1)}, bf16[256,1024]{1,0:T(8,128)(2,1)}, u32[]{:S(2)}, u32[]{:S(2)}) collective-permute-start(bf16[256,1024]{1,0:T(8,128)(2,1)} %collective-permute-done.2.refs_0_.refs_4_), channel_id=1, source_target_pairs={{0,16},{4,68},{1,17},{5,69},{2,18},{6,70},{3,19},{7,71},{8,24},{12... | collective-permute-start | bytes 1572872 | tf_op jit(solution)/shard_map/ppermute | solution.py:159
  62.3 19.0 %collective-permute-start.7 = (bf16[256,1024]{1,0:T(8,128)(2,1)}, bf16[256,1024]{1,0:T(8,128)(2,1)}, u32[]{:S(2)}, u32[]{:S(2)}) collective-permute-start(bf16[256,1024]{1,0:T(8,128)(2,1)} %collective-permute-done.2.refs_0_.refs_4_), channel_id=1, source_target_pairs={{0,192},{4,52},{1,193},{5,53},{2,194},{6,54},{3,195},{7,55},{8,200... | collective-permute-start | bytes 1572872 | tf_op jit(solution)/shard_map/ppermute | solution.py:159
  64.8 7.4 %copy-start = (bf16[512,1024]{1,0:T(8,128)(2,1)}, bf16[512,1024]{1,0:T(8,128)(2,1)S(1)}, u32[]{:S(2)}) copy-start(bf16[512,1024]{1,0:T(8,128)(2,1)S(1)} %collective-permute-done.5.refs_3_) | copy-start | bytes 3145732
  64.8 16.6 %collective-permute-start.6 = (bf16[256,1024]{1,0:T(8,128)(2,1)}, bf16[256,1024]{1,0:T(8,128)(2,1)}, u32[]{:S(2)}, u32[]{:S(2)}) collective-permute-start(bf16[256,1024]{1,0:T(8,128)(2,1)} %collective-permute-done.2.refs_0_.refs_4_), channel_id=1, source_target_pairs={{0,48},{4,196},{1,49},{5,197},{2,50},{6,198},{3,51},{7,199},{8,56}... | collective-permute-start | bytes 1572872 | tf_op jit(solution)/shard_map/ppermute | solution.py:159
  72.1 8.4 %copy-start.8 = (f32[256]{0:T(256)S(1)}, f32[256]{0:T(256)}, u32[]{:S(2)}) copy-start(f32[256]{0:T(256)} %param.14) | copy-start | bytes 3076
  72.1 25.5 %copy-start.1 = (bf16[512,1024]{1,0:T(8,128)(2,1)}, bf16[512,1024]{1,0:T(8,128)(2,1)S(1)}, u32[]{:S(2)}) copy-start(bf16[512,1024]{1,0:T(8,128)(2,1)S(1)} %collective-permute-done.4.refs_2_) | copy-start | bytes 3145732
  72.1 0.6 copy-start.4
  72.7 21.8 %all-to-all-start.1 = ((bf16[64,16,128]{2,1,0:T(8,128)(2,1)}), bf16[64,16,128]{2,1,0:T(8,128)(2,1)S(1)}, u32[]{:S(2)}, u32[]{:S(2)}) async-start(bf16[64,16,128]{2,1,0:T(8,128)(2,1)} %bitcast.9), calls=%async_computation.1 | async-start | bytes 524288 | tf_op jit(solution)/shard_map/all_to_all | solution.py:316
  81.3 0.6 copy-start.3
  94.5 0.7 copy-start.7
  110.2 4.0 %collective-permute-start.9 = (bf16[1024,128]{1,0:T(8,128)(2,1)S(1)}, bf16[1024,128]{1,0:T(8,128)(2,1)S(1)}, u32[]{:S(2)}, u32[]{:S(2)}) collective-permute-start(bf16[1024,128]{1,0:T(8,128)(2,1)S(1)} %bitcast.6), channel_id=1, source_target_pairs={{0,4},{4,0},{1,5},{5,1},{2,6},{6,2},{3,7},{7,3},{8,12},{12,8},{9,1... | collective-permute-start | bytes 786440 | tf_op jit(solution)/shard_map/ppermute | solution.py:159
  122.0 2.8 %collective-permute-start.10 = (bf16[128,4096]{1,0:T(8,128)(2,1)S(1)}, bf16[128,4096]{1,0:T(8,128)(2,1)S(1)}, u32[]{:S(2)}, u32[]{:S(2)}) collective-permute-start(bf16[128,4096]{1,0:T(8,128)(2,1)S(1)} %get-tuple-element.17), channel_id=1, source_target_pairs={{0,4},{4,0},{1,5},{5,1},{2,6},{6,2},{3,7},{7,3},{8,12},{12,8},{9,1... | collective-permute-start | bytes 3145736 | tf_op jit(solution)/shard_map/ppermute | solution.py:159

commit v7 on v3

--- a/solution.py
+++ b/solution.py
@@ -20,6 +20,9 @@
 HALF = 4096
 QUARTER = 1024
 SPLIT = 384
+CONVOLVE = 60
+MIX = 24
+LAST = 30
 WORK = 10**11
 PACK_WORK = 10**10
 JOIN_WORK = 10**10
@@ -40,17 +43,12 @@
     def narrow(table):
         return table.astype(np.float32).astype(ml_dtypes.bfloat16)
 
-    return (
-        narrow(forward_one),
-        narrow(forward_two),
-        narrow(back_two),
-        narrow(back_one),
-        turn.real.astype(np.float32),
-        turn.imag.astype(np.float32),
-    )
-
-
-def pack_kernel(signal_ref, filter_ref, after_ref, out_ref, wide):
+    left, right = np.split(back_one, 2, axis=1)
+    factors = np.concatenate([forward_one, forward_two, back_two, left, right], 0)
+    return narrow(factors), np.concatenate([turn.real, turn.imag], 0).astype(np.float32)
+
+
+def pack_kernel(signal_ref, filter_ref, after_ref, out_ref, token_ref, wide):
     for which, source in enumerate((signal_ref, filter_ref)):
         for own in range(OWN_CHANNELS):
             for piece in range(PIECES):
@@ -66,9 +64,11 @@
     return jnp.dot(left, right, preferred_element_type=jnp.float32)
 
 
-def convolve_kernel(
-    data_ref, one_ref, two_ref, back_two_ref, back_one_ref, cos_ref, sin_ref, out_ref, wide, result
-):
+def convolve_kernel(data_ref, factors_ref, turn_ref, out_ref, token_ref, wide, result):
+    forward_one = factors_ref[: 2 * ROWS]
+    forward_two, back_two, back_left, back_right = (
+        factors_ref[row * ROWS : (row + 1) * ROWS] for row in range(2, 6)
+    )
     wide[...] = data_ref[...].astype(jnp.float32)
     columns = []
     for which in range(2):
@@ -78,15 +78,15 @@
                 for piece in range(PIECES)
             ]
             columns.append(jnp.concatenate(pieces, axis=0).astype(jnp.bfloat16))
-    turn_cos, turn_sin = cos_ref[...], sin_ref[...]
+    turn_cos, turn_sin = turn_ref[:ROWS], turn_ref[ROWS:]
 
     def spectrum(column):
-        part = matmul(one_ref[...], column)
+        part = matmul(forward_one, column)
         real, imag = part[:ROWS], part[ROWS:]
         turned = jnp.concatenate(
             [real * turn_cos - imag * turn_sin, real * turn_sin + imag * turn_cos], axis=1
         )
-        both = matmul(turned.astype(jnp.bfloat16), two_ref[...])
+        both = matmul(turned.astype(jnp.bfloat16), forward_two)
         return both[:, :LANES], both[:, LANES:]
 
     for own in range(OWN_CHANNELS):
@@ -99,12 +99,12 @@
             ],
             axis=1,
         )
-        back = matmul(product.astype(jnp.bfloat16), back_two_ref[...])
+        back = matmul(product.astype(jnp.bfloat16), back_two)
         real, imag = back[:, :LANES], back[:, LANES:]
-        turned = jnp.concatenate(
-            [real * turn_cos + imag * turn_sin, imag * turn_cos - real * turn_sin], axis=0
-        )
-        values = matmul(back_one_ref[...], turned.astype(jnp.bfloat16)) * (1.0 / POSITIONS)
+        turned_real = (real * turn_cos + imag * turn_sin).astype(jnp.bfloat16)
+        turned_imag = (imag * turn_cos - real * turn_sin).astype(jnp.bfloat16)
+        values = matmul(back_left, turned_real) + matmul(back_right, turned_imag)
+        values = values * (1.0 / POSITIONS)
         for piece in range(PIECES):
             result[pl.ds(own * PIECES + piece, SEQ_DEVICES, stride=16), :] = values[
                 piece * SEQ_DEVICES : (piece + 1) * SEQ_DEVICES
@@ -172,6 +172,8 @@
 
 
 ANYWHERE = pl.BlockSpec(memory_space=pl.ANY)
+INSIDE = pl.BlockSpec(memory_space=pltpu.VMEM)
+TOKEN = jax.ShapeDtypeStruct((8, LANES), jnp.float32)
 
 
 def ordered(block, after):
@@ -254,27 +256,31 @@
 def body(signal, gate, filter_taps, skip_weight, out_weight):
     mine, parts = first_quarter(out_weight)
     tables = transform_tables()
-    packed = call(
+    packed, packed_token = call(
         pack_kernel,
-        jax.ShapeDtypeStruct((SEQ_DEVICES * 32, LANES), jnp.bfloat16),
+        (jax.ShapeDtypeStruct((SEQ_DEVICES * 32, LANES), jnp.bfloat16), TOKEN),
         [pltpu.VMEM((SEQ_DEVICES * 32, LANES), jnp.float32)],
         work=PACK_WORK,
-        in_specs=[pl.BlockSpec(memory_space=pltpu.VMEM)] * 2 + [ANYWHERE],
+        in_specs=[INSIDE] * 2 + [ANYWHERE],
+        out_specs=(INSIDE, ANYWHERE),
     )(signal, filter_taps, mine)
-    blocks = other_quarters(parts, packed)
+    blocks = other_quarters(parts, packed_token)
     arrived = lax.all_to_all(
         packed.reshape(SEQ_DEVICES, 32, LANES), AXES, split_axis=0, concat_axis=0, tiled=True
     )
-    convolved = call(
+    convolved, convolved_token = call(
         convolve_kernel,
-        jax.ShapeDtypeStruct((SEQ_DEVICES * 16, LANES), jnp.bfloat16),
+        (jax.ShapeDtypeStruct((SEQ_DEVICES * 16, LANES), jnp.bfloat16), TOKEN),
         [
             pltpu.VMEM((SEQ_DEVICES * 32, LANES), jnp.float32),
             pltpu.VMEM((SEQ_DEVICES * 16, LANES), jnp.float32),
         ],
+        limit=CONVOLVE,
+        in_specs=[INSIDE] * 3,
+        out_specs=(INSIDE, ANYWHERE),
         work=WORK,
     )(arrived.reshape(SEQ_DEVICES * 32, LANES), *tables)
-    weights = both_halves(blocks, convolved)
+    weights = both_halves(blocks, convolved_token)
     returned = lax.all_to_all(
         convolved.reshape(SEQ_DEVICES, 16, LANES), AXES, split_axis=0, concat_axis=0, tiled=True
     )
@@ -286,6 +292,7 @@
             jax.ShapeDtypeStruct((PIECES, channels, LANES), jnp.bfloat16),
         ),
         [pltpu.VMEM((SEQ_DEVICES * 16, LANES), jnp.float32)],
+        limit=MIX,
         work=WORK,
     )(returned.reshape(SEQ_DEVICES * 16, LANES), signal, gate, skip_weight[:, None])
     mine = lax.all_to_all(rounded, "chan", split_axis=0, concat_axis=0, tiled=True)
@@ -297,8 +304,8 @@
             pltpu.VMEM((8, LANES, QUARTER), jnp.bfloat16),
             pltpu.SemaphoreType.DMA((8,)),
         ],
-        limit=30,
-        in_specs=[pl.BlockSpec(memory_space=pltpu.VMEM)] * 12,
+        limit=LAST,
+        in_specs=[INSIDE] * 12,
         out_specs=ANYWHERE,
     )(mine.reshape(4 * channels, LANES), out_weight, *weights)
     return mixed, projected

time: 105 us -> 102 us (0.971)
  local copies, waits for them, and re-layouts: 8.03 us -> 5.95 us
  Pallas kernels: 18.6 us -> 17.3 us
    unnamed x14 -> x16, local copies, waits for them, and re-layouts: 4.89 us -> 3.46 us
    pallas_call x1, Pallas kernels: 2.41 us -> 1.03 us  [body(): call(mix_kernel, (jax.ShapeDtypeStruct((channels, shard_len), jnp.float32...]
  transfers between devices with their start and end apart: 14 -> 14, of which waited for: 7 -> 7; matrix products, arithmetic and copies ran while one was open for 2% -> 1% of each run, Pallas kernels for 11% -> 10%
where the time goes in v7:
time: 102 us; the launch traced here: 101 us
  starting transfers between devices  34.7 us (34%)
  waiting for transfers between devices  30.8 us (30%)
  Pallas kernels  17.3 us (17%)
  blocking collectives  11.5 us (11%)
  local copies, waits for them, and re-layouts  5.95 us (6%)
    ppermute x12, waiting for transfers between devices, moved(): return lax.ppermute(array, (*AXES, 'chan'), device_pairs(move))  26.7 us
    ppermute x12, starting transfers between devices, moved(): return lax.ppermute(array, (*AXES, 'chan'), device_pairs(move))  14.6 us
    all_to_all x1, blocking collectives, body(): lax.all_to_all(rounded, 'chan', split_axis=0, concat_axis=0, tiled=True)  11.5 us
    all_to_all x1, starting transfers between devices, body(): lax.all_to_all(packed.reshape(SEQ_DEVICES, 32, LANES), AXES, split_axis=0...  11.2 us
    all_to_all x1, starting transfers between devices, body(): lax.all_to_all(convolved.reshape(SEQ_DEVICES, 16, LANES), AXES, split_axi...  8.84 us
    pallas_call x1, Pallas kernels, body(): call(project_kernel, jax.ShapeDtypeStruct((LANES, width), jnp.bfloat16),...  7.08 us
    pallas_call x1, Pallas kernels, body(): call(convolve_kernel, (jax.ShapeDtypeStruct((SEQ_DEVICES * 16, LANES), jn...  5.92 us
    all_to_all x1, waiting for transfers between devices, body(): lax.all_to_all(convolved.reshape(SEQ_DEVICES, 16, LANES), AXES, split_axi...  4.1 us
  transfers between devices with their start and end apart: 14, of which 7 were waited for; matrix products, arithmetic and copies ran while one was open for 1% of the time, Pallas kernels for 10%

profile of v7, /device:TPU:1, one launch (start us, length us, event | category | flops | bytes accessed | tf_op | source)
XLA Modules:
  0.0 101.1 jit_solution(6774708126144744337)
XLA Ops:
  0.7 1.1 %constant_dynamic-slice_fusion.after_ref = bf16[256,1024]{1,0:T(8,128)(2,1)S(1)} fusion(bf16[256,8192]{1,0:T(8,128)(2,1)} %own_ref.1, s32[]{:T(128)S(6)} %select_n.15), kind=kLoop, calls=%fused_computation | loop fusion | bytes 1048580 | tf_op jit(solution)/shard_map/dynamic_slice | solution.py:194
  1.7 0.0 copy-start.6
  1.8 6.9 %collective-permute-start.2 = (bf16[256,1024]{1,0:T(8,128)(2,1)S(1)}, bf16[256,1024]{1,0:T(8,128)(2,1)S(1)}, u32[]{:S(2)}, u32[]{:S(2)}) collective-permute-start(bf16[256,1024]{1,0:T(8,128)(2,1)S(1)} %constant_dynamic-slice_fusion.after_ref), channel_id=1, source_target_pairs={{0,2},{4,14},{1,3},{5,15},{2,8},{6,4},{3,9},{7,5},{8,10},{12,6},{9... | collective-permute-start | bytes 1572872 | tf_op jit(solution)/shard_map/ppermute | solution.py:151
  8.7 0.7 collective-permute-start.1
  9.4 0.7 collective-permute-start
  10.1 0.0 copy-done.6
  10.1 3.1 %shard_map.86 = (bf16[2048,128]{1,0:T(8,128)(2,1)}, f32[8,128]{1,0:T(8,128)}) custom-call(f32[256,512]{1,0:T(8,128)} %signal_ref.3, f32[256,512]{1,0:T(8,128)} %filter_ref.1, bf16[256,1024]{1,0:T(8,128)(2,1)} %copy-done.6), custom_call_target="tpu_custom_call" | custom-call | flops 10000000000 | tf_op jit(solution)/shard_map/pallas_call | solution.py:259
  13.2 11.2 %all-to-all-start = ((bf16[64,32,128]{2,1,0:T(8,128)(2,1)}), bf16[64,32,128]{2,1,0:T(8,128)(2,1)}, u32[]{:S(2)}, u32[]{:S(2)}) async-start(bf16[64,32,128]{2,1,0:T(8,128)(2,1)} %bitcast.8), calls=%async_computation | async-start | bytes 1048576 | tf_op jit(solution)/shard_map/all_to_all | solution.py:268
  24.4 0.9 collective-permute-done.2.far_ref
  25.3 17.6 %collective-permute-done.1.above_ref = bf16[256,1024]{1,0:T(8,128)(2,1)S(1)} collective-permute-done((bf16[256,1024]{1,0:T(8,128)(2,1)S(1)}, bf16[256,1024]{1,0:T(8,128)(2,1)S(1)}, u32[]{:S(2)}, u32[]{:S(2)}) %collective-permute-start.1) | collective-permute-done | bytes 524320 | tf_op jit(solution)/shard_map/ppermute | solution.py:151
  42.9 0.0 collective-permute-done.below_ref
  42.9 0.0 copy-start.5
  42.9 0.7 copy-done.5
  43.6 0.1 shard_map.89.refs_0_
  43.7 1.4 %collective-permute-start.6 = (bf16[768,1024]{1,0:T(8,128)(2,1)S(1)}, bf16[768,1024]{1,0:T(8,128)(2,1)}, u32[]{:S(2)}, u32[]{:S(2)}) collective-permute-start(bf16[768,1024]{1,0:T(8,128)(2,1)S(1)} %shard_map.89.refs_0_), channel_id=1, source_target_pairs={{0,16},{4,68},{1,17},{5,69},{2,18},{6,70},{3,19},{7,71},{8,24},{12... | collective-permute-start | bytes 4718600 | tf_op jit(solution)/shard_map/ppermute | solution.py:151
  45.1 1.6 %collective-permute-start.3 = (bf16[768,1024]{1,0:T(8,128)(2,1)S(1)}, bf16[768,1024]{1,0:T(8,128)(2,1)S(1)}, u32[]{:S(2)}, u32[]{:S(2)}) collective-permute-start(bf16[768,1024]{1,0:T(8,128)(2,1)S(1)} %shard_map.89.refs_0_), channel_id=1, source_target_pairs={{0,48},{4,196},{1,49},{5,197},{2,50},{6,198},{3,51},{7,199},{8,56}... | collective-permute-start | bytes 4718600 | tf_op jit(solution)/shard_map/ppermute | solution.py:151
  46.7 1.3 %fusion = (bf16[384,1024]{1,0:T(8,128)(2,1)}, bf16[384,1024]{1,0:T(8,128)(2,1)}) fusion(bf16[768,1024]{1,0:T(8,128)(2,1)S(1)} %shard_map.89.refs_0_), kind=kLoop, calls=%fused_computation.1 | loop fusion | bytes 3145728 | tf_op jit(solution)/shard_map/slice | solution.py:211
  47.9 2.4 %collective-permute-start.5 = (bf16[384,1024]{1,0:T(8,128)(2,1)}, bf16[384,1024]{1,0:T(8,128)(2,1)}, u32[]{:S(2)}, u32[]{:S(2)}) collective-permute-start(bf16[384,1024]{1,0:T(8,128)(2,1)} %get-tuple-element.14), channel_id=1, source_target_pairs={{0,192},{4,52},{1,193},{5,53},{2,194},{6,54},{3,195},{7,55},{8,200... | collective-permute-start | bytes 2359304 | tf_op jit(solution)/shard_map/ppermute | solution.py:151
  50.4 0.0 collective-permute-start.4
  50.4 0.0 all-to-all-done
  50.4 0.0 copy-start.7
  50.4 5.9 %shard_map.87 = (bf16[1024,128]{1,0:T(8,128)(2,1)}, f32[8,128]{1,0:T(8,128)}) custom-call(bf16[2048,128]{1,0:T(8,128)(2,1)} %bitcast.1.data_ref, bf16[1536,256]{1,0:T(8,128)(2,1)} %constant.41.clone.factors_ref, f32[512,128]{1,0:T(8,128)} %constant.42.clone.turn_ref), custom_call_target="tpu_custom_call" | custom-call | flops 99999997952 | tf_op jit(solution)/shard_map/pallas_call | solution.py:271
  56.3 8.8 %all-to-all-start.1 = ((bf16[64,16,128]{2,1,0:T(8,128)(2,1)}), bf16[64,16,128]{2,1,0:T(8,128)(2,1)S(1)}, u32[]{:S(2)}, u32[]{:S(2)}) async-start(bf16[64,16,128]{2,1,0:T(8,128)(2,1)} %bitcast.9), calls=%async_computation.1 | async-start | bytes 524288 | tf_op jit(solution)/shard_map/all_to_all | solution.py:284
  65.2 0.0 copy-done.7
  65.2 0.1 copy.13.skip_ref
  65.3 0.5 collective-permute-start.7
  65.9 2.4 %collective-permute-done.5.block_ref = bf16[384,1024]{1,0:T(8,128)(2,1)} collective-permute-done((bf16[384,1024]{1,0:T(8,128)(2,1)}, bf16[384,1024]{1,0:T(8,128)(2,1)}, u32[]{:S(2)}, u32[]{:S(2)}) %collective-permute-start.5) | collective-permute-done | bytes 786464 | tf_op jit(solution)/shard_map/ppermute | solution.py:151
  68.3 0.7 copy-done.1
  69.0 0.0 collective-permute-start.10
  69.0 1.5 %collective-permute-done.4.block_ref = bf16[384,1024]{1,0:T(8,128)(2,1)} collective-permute-done((bf16[384,1024]{1,0:T(8,128)(2,1)}, bf16[384,1024]{1,0:T(8,128)(2,1)}, u32[]{:S(2)}, u32[]{:S(2)}) %collective-permute-start.4) | collective-permute-done | bytes 786464 | tf_op jit(solution)/shard_map/ppermute | solution.py:151
  70.5 0.0 collective-permute-start.9
  70.5 4.1 %collective-permute-done.6.block_ref = bf16[768,1024]{1,0:T(8,128)(2,1)} collective-permute-done((bf16[768,1024]{1,0:T(8,128)(2,1)S(1)}, bf16[768,1024]{1,0:T(8,128)(2,1)}, u32[]{:S(2)}, u32[]{:S(2)}) %collective-permute-start.6) | collective-permute-done | bytes 1572896 | tf_op jit(solution)/shard_map/ppermute | solution.py:151
  74.6 0.0 copy-done.2
  74.6 0.0 collective-permute-start.11
  74.6 0.2 collective-permute-done.3.block_ref
  74.8 0.3 collective-permute-start.8
  75.1 4.1 %all-to-all-done.1 = bf16[64,16,128]{2,1,0:T(8,128)(2,1)S(1)} async-done(((bf16[64,16,128]{2,1,0:T(8,128)(2,1)}), bf16[64,16,128]{2,1,0:T(8,128)(2,1)S(1)}, u32[]{:S(2)}, u32[]{:S(2)}) %all-to-all-start.1) | async-done | bytes 262176 | tf_op jit(solution)/shard_map/all_to_all | solution.py:284
  79.2 1.0 %copy-done.3 = f32[256,512]{1,0:T(8,128)S(1)} copy-done((f32[256,512]{1,0:T(8,128)S(1)}, f32[256,512]{1,0:T(8,128)}, u32[]{:S(2)}) %copy-start.3) | copy-done | bytes 524312
  80.2 1.0 %copy-done.4 = f32[256,512]{1,0:T(8,128)S(1)} copy-done((f32[256,512]{1,0:T(8,128)S(1)}, f32[256,512]{1,0:T(8,128)}, u32[]{:S(2)}) %copy-start.4) | copy-done | bytes 524312
  81.3 1.0 %shard_map.88 = (f32[256,512]{1,0:T(8,128)}, bf16[4,256,128]{2,1,0:T(8,128)(2,1)S(1)}) custom-call(bf16[1024,128]{1,0:T(8,128)(2,1)S(1)} %bitcast.7, f32[256,512]{1,0:T(8,128)S(1)} %copy-done.3, f32[256,512]{1,0:T(8,128)S(1)} %copy-done.4, f32[256,1]{1,0:T(8,128)S(1)} %copy.13.skip_ref), custom_call_target="tpu_custom_call" | custom-call | flops 99999997952 | tf_op jit(solution)/shard_map/pallas_call | solution.py:288
  82.3 11.5 %all_to_all.15 = bf16[4,256,128]{2,1,0:T(8,128)(2,1)S(1)} all-to-all(bf16[4,256,128]{2,1,0:T(8,128)(2,1)S(1)} %get-tuple-element.11), channel_id=1, replica_groups=mesh['y'=4,'x'=4,'zh'=2,'core'=2,'chan'=4] {'chan'}, dimensions={0} | all-to-all | bytes 524288 | tf_op jit(solution)/shard_map/all_to_all | solution.py:298
  93.8 0.0 collective-permute-done.10.refs_8_
  93.8 0.0 collective-permute-done.9.refs_7_
  93.8 0.0 collective-permute-done.7.refs_5_
  93.8 0.0 collective-permute-done.11.refs_9_
  93.8 0.0 collective-permute-done.8.refs_6_
  93.9 0.0 copy-done
  93.9 7.1 %shard_map.94 = bf16[128,8192]{1,0:T(8,128)(2,1)} custom-call(bf16[1024,128]{1,0:T(8,128)(2,1)S(1)} %bitcast.6, bf16[256,8192]{1,0:T(8,128)(2,1)S(1)} %copy-done, bf16[768,1024]{1,0:T(8,128)(2,1)S(1)} %shard_map.89.refs_0_, bf16[768,1024]{1,0:T(8,128)(2,1)S(1)} %shard_map.90.refs_1_, bf16[384,1024]{1,0:T(8,128)(2,1)} %shard_map.91.refs_2_, ...), custom_call_target="tpu_custom_call" | custom-call | tf_op jit(solution)/shard_map/pallas_call | solution.py:300
  (9 shorter events, 0.0 us)
Async XLA Ops:
  1.7 8.4 %copy-start.6 = (bf16[256,1024]{1,0:T(8,128)(2,1)}, bf16[256,1024]{1,0:T(8,128)(2,1)S(1)}, u32[]{:S(2)}) copy-start(bf16[256,1024]{1,0:T(8,128)(2,1)S(1)} %constant_dynamic-slice_fusion.after_ref) | copy-start | bytes 1572868
  1.8 23.6 %collective-permute-start.2 = (bf16[256,1024]{1,0:T(8,128)(2,1)S(1)}, bf16[256,1024]{1,0:T(8,128)(2,1)S(1)}, u32[]{:S(2)}, u32[]{:S(2)}) collective-permute-start(bf16[256,1024]{1,0:T(8,128)(2,1)S(1)} %constant_dynamic-slice_fusion.after_ref), channel_id=1, source_target_pairs={{0,2},{4,14},{1,3},{5,15},{2,8},{6,4},{3,9},{7,5},{8,10},{12,6},{9... | collective-permute-start | bytes 1572872 | tf_op jit(solution)/shard_map/ppermute | solution.py:151
  8.7 34.2 %collective-permute-start.1 = (bf16[256,1024]{1,0:T(8,128)(2,1)S(1)}, bf16[256,1024]{1,0:T(8,128)(2,1)S(1)}, u32[]{:S(2)}, u32[]{:S(2)}) collective-permute-start(bf16[256,1024]{1,0:T(8,128)(2,1)S(1)} %constant_dynamic-slice_fusion.after_ref), channel_id=1, source_target_pairs={{0,11},{4,15},{1,0},{5,4},{2,1},{6,5},{3,2},{7,6},{8,3},{12,7},{9,... | collective-permute-start | bytes 1572872 | tf_op jit(solution)/shard_map/ppermute | solution.py:151
  9.4 33.5 %collective-permute-start = (bf16[256,1024]{1,0:T(8,128)(2,1)S(1)}, bf16[256,1024]{1,0:T(8,128)(2,1)S(1)}, u32[]{:S(2)}, u32[]{:S(2)}) collective-permute-start(bf16[256,1024]{1,0:T(8,128)(2,1)S(1)} %constant_dynamic-slice_fusion.after_ref), channel_id=1, source_target_pairs={{0,1},{4,5},{1,2},{5,6},{2,3},{6,7},{3,8},{7,12},{8,9},{12,13},{9,... | collective-permute-start | bytes 1572872 | tf_op jit(solution)/shard_map/ppermute | solution.py:151
  13.2 37.2 %all-to-all-start = ((bf16[64,32,128]{2,1,0:T(8,128)(2,1)}), bf16[64,32,128]{2,1,0:T(8,128)(2,1)}, u32[]{:S(2)}, u32[]{:S(2)}) async-start(bf16[64,32,128]{2,1,0:T(8,128)(2,1)} %bitcast.8), calls=%async_computation | async-start | bytes 1048576 | tf_op jit(solution)/shard_map/all_to_all | solution.py:268
  42.9 0.7 copy-start.5
  43.7 30.8 %collective-permute-start.6 = (bf16[768,1024]{1,0:T(8,128)(2,1)S(1)}, bf16[768,1024]{1,0:T(8,128)(2,1)}, u32[]{:S(2)}, u32[]{:S(2)}) collective-permute-start(bf16[768,1024]{1,0:T(8,128)(2,1)S(1)} %shard_map.89.refs_0_), channel_id=1, source_target_pairs={{0,16},{4,68},{1,17},{5,69},{2,18},{6,70},{3,19},{7,71},{8,24},{12... | collective-permute-start | bytes 4718600 | tf_op jit(solution)/shard_map/ppermute | solution.py:151
  45.1 29.7 %collective-permute-start.3 = (bf16[768,1024]{1,0:T(8,128)(2,1)S(1)}, bf16[768,1024]{1,0:T(8,128)(2,1)S(1)}, u32[]{:S(2)}, u32[]{:S(2)}) collective-permute-start(bf16[768,1024]{1,0:T(8,128)(2,1)S(1)} %shard_map.89.refs_0_), channel_id=1, source_target_pairs={{0,48},{4,196},{1,49},{5,197},{2,50},{6,198},{3,51},{7,199},{8,56}... | collective-permute-start | bytes 4718600 | tf_op jit(solution)/shard_map/ppermute | solution.py:151
  47.9 20.4 %collective-permute-start.5 = (bf16[384,1024]{1,0:T(8,128)(2,1)}, bf16[384,1024]{1,0:T(8,128)(2,1)}, u32[]{:S(2)}, u32[]{:S(2)}) collective-permute-start(bf16[384,1024]{1,0:T(8,128)(2,1)} %get-tuple-element.14), channel_id=1, source_target_pairs={{0,192},{4,52},{1,193},{5,53},{2,194},{6,54},{3,195},{7,55},{8,200... | collective-permute-start | bytes 2359304 | tf_op jit(solution)/shard_map/ppermute | solution.py:151
  50.4 20.1 %collective-permute-start.4 = (bf16[384,1024]{1,0:T(8,128)(2,1)}, bf16[384,1024]{1,0:T(8,128)(2,1)}, u32[]{:S(2)}, u32[]{:S(2)}) collective-permute-start(bf16[384,1024]{1,0:T(8,128)(2,1)} %get-tuple-element.15), channel_id=1, source_target_pairs={{0,64},{4,20},{1,65},{5,21},{2,66},{6,22},{3,67},{7,23},{8,72},{12... | collective-permute-start | bytes 2359304 | tf_op jit(solution)/shard_map/ppermute | solution.py:151
  50.4 14.8 %copy-start.7 = (f32[256]{0:T(256)S(1)}, f32[256]{0:T(256)}, u32[]{:S(2)}) copy-start(f32[256]{0:T(256)} %param.10) | copy-start | bytes 3076
  56.3 22.9 %all-to-all-start.1 = ((bf16[64,16,128]{2,1,0:T(8,128)(2,1)}), bf16[64,16,128]{2,1,0:T(8,128)(2,1)S(1)}, u32[]{:S(2)}, u32[]{:S(2)}) async-start(bf16[64,16,128]{2,1,0:T(8,128)(2,1)} %bitcast.9), calls=%async_computation.1 | async-start | bytes 524288 | tf_op jit(solution)/shard_map/all_to_all | solution.py:284
  65.3 28.5 %collective-permute-start.7 = (bf16[768,1024]{1,0:T(8,128)(2,1)S(1)}, bf16[768,1024]{1,0:T(8,128)(2,1)}, u32[]{:S(2)}, u32[]{:S(2)}) collective-permute-start(bf16[768,1024]{1,0:T(8,128)(2,1)S(1)} %shard_map.89.refs_0_), channel_id=1, source_target_pairs={{0,4},{4,0},{1,5},{5,1},{2,6},{6,2},{3,7},{7,3},{8,12},{12,8},{9,1... | collective-permute-start | bytes 4718600 | tf_op jit(solution)/shard_map/ppermute | solution.py:151
  68.3 0.7 copy-start.1
  69.0 5.6 %copy-start.2 = (f32[8,128]{1,0:T(8,128)S(1)}, f32[8,128]{1,0:T(8,128)}, u32[]{:S(2)}) copy-start(f32[8,128]{1,0:T(8,128)} %get-tuple-element.13.after_ref) | copy-start | bytes 12292
  69.0 24.9 %collective-permute-start.10 = (bf16[384,1024]{1,0:T(8,128)(2,1)}, bf16[384,1024]{1,0:T(8,128)(2,1)}, u32[]{:S(2)}, u32[]{:S(2)}) collective-permute-start(bf16[384,1024]{1,0:T(8,128)(2,1)} %shard_map.92.refs_3_), channel_id=1, source_target_pairs={{0,4},{4,0},{1,5},{5,1},{2,6},{6,2},{3,7},{7,3},{8,12},{12,8},{9,1... | collective-permute-start | bytes 2359304 | tf_op jit(solution)/shard_map/ppermute | solution.py:151
  70.5 23.4 %collective-permute-start.9 = (bf16[384,1024]{1,0:T(8,128)(2,1)}, bf16[384,1024]{1,0:T(8,128)(2,1)}, u32[]{:S(2)}, u32[]{:S(2)}) collective-permute-start(bf16[384,1024]{1,0:T(8,128)(2,1)} %shard_map.91.refs_2_), channel_id=1, source_target_pairs={{0,4},{4,0},{1,5},{5,1},{2,6},{6,2},{3,7},{7,3},{8,12},{12,8},{9,1... | collective-permute-start | bytes 2359304 | tf_op jit(solution)/shard_map/ppermute | solution.py:151
  74.6 19.3 %collective-permute-start.11 = (bf16[768,1024]{1,0:T(8,128)(2,1)}, bf16[768,1024]{1,0:T(8,128)(2,1)}, u32[]{:S(2)}, u32[]{:S(2)}) collective-permute-start(bf16[768,1024]{1,0:T(8,128)(2,1)} %shard_map.93.refs_4_), channel_id=1, source_target_pairs={{0,4},{4,0},{1,5},{5,1},{2,6},{6,2},{3,7},{7,3},{8,12},{12,8},{9,1... | collective-permute-start | bytes 4718600 | tf_op jit(solution)/shard_map/ppermute | solution.py:151
  74.8 19.1 %collective-permute-start.8 = (bf16[768,1024]{1,0:T(8,128)(2,1)S(1)}, bf16[768,1024]{1,0:T(8,128)(2,1)}, u32[]{:S(2)}, u32[]{:S(2)}) collective-permute-start(bf16[768,1024]{1,0:T(8,128)(2,1)S(1)} %shard_map.90.refs_1_), channel_id=1, source_target_pairs={{0,4},{4,0},{1,5},{5,1},{2,6},{6,2},{3,7},{7,3},{8,12},{12,8},{9,1... | collective-permute-start | bytes 4718600 | tf_op jit(solution)/shard_map/ppermute | solution.py:151
  79.2 1.0 %copy-start.3 = (f32[256,512]{1,0:T(8,128)S(1)}, f32[256,512]{1,0:T(8,128)}, u32[]{:S(2)}) copy-start(f32[256,512]{1,0:T(8,128)} %signal_ref.3) | copy-start | bytes 1572868
  80.2 1.0 %copy-start.4 = (f32[256,512]{1,0:T(8,128)S(1)}, f32[256,512]{1,0:T(8,128)}, u32[]{:S(2)}) copy-start(f32[256,512]{1,0:T(8,128)} %gate_ref.1) | copy-start | bytes 1572868
  81.3 12.6 %copy-start = (bf16[256,8192]{1,0:T(8,128)(2,1)S(1)}, bf16[256,8192]{1,0:T(8,128)(2,1)}, u32[]{:S(2)}) copy-start(bf16[256,8192]{1,0:T(8,128)(2,1)} %own_ref.1) | copy-start | bytes 12582916

commit v8 on v7

--- a/solution.py
+++ b/solution.py
@@ -48,7 +48,7 @@
     return narrow(factors), np.concatenate([turn.real, turn.imag], 0).astype(np.float32)
 
 
-def pack_kernel(signal_ref, filter_ref, after_ref, out_ref, token_ref, wide):
+def pack_kernel(signal_ref, filter_ref, out_ref, token_ref, wide):
     for which, source in enumerate((signal_ref, filter_ref)):
         for own in range(OWN_CHANNELS):
             for piece in range(PIECES):
@@ -64,7 +64,7 @@
     return jnp.dot(left, right, preferred_element_type=jnp.float32)
 
 
-def convolve_kernel(data_ref, factors_ref, turn_ref, out_ref, token_ref, wide, result):
+def convolve_kernel(data_ref, factors_ref, turn_ref, out_ref, wide, result):
     forward_one = factors_ref[: 2 * ROWS]
     forward_two, back_two, back_left, back_right = (
         factors_ref[row * ROWS : (row + 1) * ROWS] for row in range(2, 6)
@@ -167,25 +167,9 @@
         copy.wait()
 
 
-def keep_kernel(block_ref, after_ref, out_ref):
-    pass
-
-
 ANYWHERE = pl.BlockSpec(memory_space=pl.ANY)
 INSIDE = pl.BlockSpec(memory_space=pltpu.VMEM)
 TOKEN = jax.ShapeDtypeStruct((8, LANES), jnp.float32)
-
-
-def ordered(block, after):
-    return call(
-        keep_kernel,
-        jax.ShapeDtypeStruct(block.shape, block.dtype),
-        [],
-        limit=2,
-        in_specs=[ANYWHERE] * 2,
-        out_specs=ANYWHERE,
-        input_output_aliases={0: 0},
-    )(block, after)
 
 
 def first_quarter(out_weight):
@@ -195,7 +179,7 @@
     below = moved(mine, lambda y, x, z, c: (y, x, z + 1, c))
     above = moved(mine, lambda y, x, z, c: (y, x, z - 1, c))
     far = moved(mine, lambda y, x, z, c: (y, x, z + 2 - 4 * c, c))
-    return mine, (below, above, far)
+    return below, above, far
 
 
 def other_quarters(parts, after):
@@ -218,34 +202,37 @@
     ]
 
 
-def both_halves(blocks, after):
-    blocks = blocks[:1] + [ordered(block, after) for block in blocks[1:]]
-    return blocks + [moved(block, lambda y, x, z, c: (y, x, z, 1 - c)) for block in blocks]
-
-
-def project_kernel(columns_ref, own_ref, *refs):
-    block_refs, (out_ref, results, out_sem) = refs[:10], refs[10:]
+def project_kernel(mine_ref, theirs_ref, own_ref, *refs):
+    block_refs, (out_ref, for_them_ref, results, out_sem) = refs[:5], refs[5:]
     core, chan = lax.axis_index("core"), lax.axis_index("chan")
+    first = core * HALF
     rows = [
-        columns_ref[pl.ds(pl.multiple_of((chan + shift) % 4 * ROWS, ROWS), ROWS), :].T
+        jnp.concatenate(
+            [
+                ref[pl.ds(pl.multiple_of((chan + shift) % 4 * ROWS, ROWS), ROWS), :].T
+                for ref in (mine_ref, theirs_ref)
+            ],
+            axis=0,
+        )
         for shift in (0, 3, 1, 2)
     ]
     own_columns, columns = rows[0], jnp.concatenate(rows[1:], axis=1)
     stores = []
-    for half in range(2):
-        owner = core if half == 0 else 1 - core
-        for step, parts in enumerate(((0,), (1,), (2, 3), (4,))):
-            index = 4 * half + step
-            start = pl.multiple_of(owner * HALF + (colour(owner) + step) % 4 * QUARTER, QUARTER)
-            total = matmul(own_columns, own_ref[:, pl.ds(start, QUARTER)])
-            row = 0
-            for part in parts:
-                block = block_refs[5 * half + part][...]
-                total += matmul(columns[:, row : row + block.shape[0]], block)
-                row += block.shape[0]
-            results[index] = total.astype(jnp.bfloat16)
+    for index, parts in enumerate(((0,), (1,), (2, 3), (4,))):
+        start = pl.multiple_of((colour(core) + index) % 4 * QUARTER, QUARTER)
+        place = pl.multiple_of(first + start, QUARTER)
+        total = matmul(own_columns, own_ref[:, pl.ds(place, QUARTER)])
+        row = 0
+        for part in parts:
+            block = block_refs[part][...]
+            total += matmul(columns[:, row : row + block.shape[0]], block)
+            row += block.shape[0]
+        results[index] = total.astype(jnp.bfloat16)
+        for rank, (target, offset) in enumerate(((out_ref, place), (for_them_ref, start))):
             store = pltpu.make_async_copy(
-                results.at[index], out_ref.at[:, pl.ds(start, QUARTER)], out_sem.at[index]
+                results.at[index, pl.ds(rank * LANES, LANES)],
+                target.at[:, pl.ds(offset, QUARTER)],
+                out_sem.at[index, rank],
             )
             store.start()
             stores.append(store)
@@ -253,34 +240,42 @@
         store.wait()
 
 
+def fill_kernel(half_ref, from_them_ref, out_ref, sem):
+    start = pl.multiple_of((1 - lax.axis_index("core")) * HALF, HALF)
+    copy = pltpu.make_async_copy(from_them_ref, out_ref.at[:, pl.ds(start, HALF)], sem)
+    copy.start()
+    copy.wait()
+
+
+def swapped(array):
+    return moved(array, lambda y, x, z, c: (y, x, z, 1 - c))
+
+
 def body(signal, gate, filter_taps, skip_weight, out_weight):
-    mine, parts = first_quarter(out_weight)
+    parts = first_quarter(out_weight)
     tables = transform_tables()
     packed, packed_token = call(
         pack_kernel,
         (jax.ShapeDtypeStruct((SEQ_DEVICES * 32, LANES), jnp.bfloat16), TOKEN),
         [pltpu.VMEM((SEQ_DEVICES * 32, LANES), jnp.float32)],
         work=PACK_WORK,
-        in_specs=[INSIDE] * 2 + [ANYWHERE],
+        in_specs=[INSIDE] * 2,
         out_specs=(INSIDE, ANYWHERE),
-    )(signal, filter_taps, mine)
+    )(signal, filter_taps)
     blocks = other_quarters(parts, packed_token)
     arrived = lax.all_to_all(
         packed.reshape(SEQ_DEVICES, 32, LANES), AXES, split_axis=0, concat_axis=0, tiled=True
     )
-    convolved, convolved_token = call(
+    convolved = call(
         convolve_kernel,
-        (jax.ShapeDtypeStruct((SEQ_DEVICES * 16, LANES), jnp.bfloat16), TOKEN),
+        jax.ShapeDtypeStruct((SEQ_DEVICES * 16, LANES), jnp.bfloat16),
         [
             pltpu.VMEM((SEQ_DEVICES * 32, LANES), jnp.float32),
             pltpu.VMEM((SEQ_DEVICES * 16, LANES), jnp.float32),
         ],
         limit=CONVOLVE,
-        in_specs=[INSIDE] * 3,
-        out_specs=(INSIDE, ANYWHERE),
         work=WORK,
     )(arrived.reshape(SEQ_DEVICES * 32, LANES), *tables)
-    weights = both_halves(blocks, convolved_token)
     returned = lax.all_to_all(
         convolved.reshape(SEQ_DEVICES, 16, LANES), AXES, split_axis=0, concat_axis=0, tiled=True
     )
@@ -296,18 +291,30 @@
         work=WORK,
     )(returned.reshape(SEQ_DEVICES * 16, LANES), signal, gate, skip_weight[:, None])
     mine = lax.all_to_all(rounded, "chan", split_axis=0, concat_axis=0, tiled=True)
-    width = out_weight.shape[1]
-    projected = call(
+    mine = mine.reshape(4 * channels, LANES)
+    half_filled, for_them = call(
         project_kernel,
-        jax.ShapeDtypeStruct((LANES, width), jnp.bfloat16),
+        (
+            jax.ShapeDtypeStruct((LANES, 2 * HALF), jnp.bfloat16),
+            jax.ShapeDtypeStruct((LANES, HALF), jnp.bfloat16),
+        ),
         [
-            pltpu.VMEM((8, LANES, QUARTER), jnp.bfloat16),
-            pltpu.SemaphoreType.DMA((8,)),
+            pltpu.VMEM((4, 2 * LANES, QUARTER), jnp.bfloat16),
+            pltpu.SemaphoreType.DMA((4, 2)),
         ],
         limit=LAST,
-        in_specs=[INSIDE] * 12,
+        in_specs=[INSIDE] * 8,
+        out_specs=(ANYWHERE, ANYWHERE),
+    )(mine, swapped(mine), out_weight, *blocks)
+    projected = call(
+        fill_kernel,
+        jax.ShapeDtypeStruct(half_filled.shape, half_filled.dtype),
+        [pltpu.SemaphoreType.DMA(())],
+        limit=2,
+        in_specs=[ANYWHERE] * 2,
         out_specs=ANYWHERE,
-    )(mine.reshape(4 * channels, LANES), out_weight, *weights)
+        input_output_aliases={0: 0},
+    )(half_filled, swapped(for_them))
     return mixed, projected
 
 

time: 102 us -> 101 us (level)
  waiting for transfers between devices: 30.8 us -> 26.3 us
  starting transfers between devices: 34.7 us -> 38.5 us
    ppermute x12 -> x9, waiting for transfers between devices: 26.7 us -> 6.51 us  [moved(): return lax.ppermute(array, (*AXES, 'chan'), device_pairs(move))]
    all_to_all x1, waiting for transfers between devices: 0.01 us -> 14.4 us  [body(): lax.all_to_all(packed.reshape(SEQ_DEVICES, 32, LANES), AXES, split_axis=0...]
    all_to_all x1, starting transfers between devices: 8.84 us -> 4.18 us  [body(): lax.all_to_all(convolved.reshape(SEQ_DEVICES, 16, LANES), AXES, split_axi...]
    all_to_all x1, starting transfers between devices: 11.2 us -> 15.7 us  [body(): lax.all_to_all(packed.reshape(SEQ_DEVICES, 32, LANES), AXES, split_axis=0...]
    ppermute x12 -> x9, starting transfers between devices: 14.6 us -> 18.6 us  [moved(): return lax.ppermute(array, (*AXES, 'chan'), device_pairs(move))]
    all_to_all x1, waiting for transfers between devices: 4.1 us -> 5.44 us  [body(): lax.all_to_all(convolved.reshape(SEQ_DEVICES, 16, LANES), AXES, split_axi...]
    unnamed x16 -> x12, local copies, waits for them, and re-layouts: 3.46 us -> 2.89 us
    pallas_call x6 -> x3, Pallas kernels: 13 us -> 12.6 us  [the longest x1 5.92 us: body(): call(convolve_kernel, jax.ShapeDtypeStruct((SEQ_DEVICES * 16, LANES), jnp...]
  transfers between devices with their start and end apart: 14 -> 11, of which waited for: 7 -> 6; matrix products, arithmetic and copies ran while one was open for 1% -> 2% of each run, Pallas kernels for 10% -> 7%
where the time goes in v8:
time: 101 us; the launch traced here: 100 us
  starting transfers between devices  38.5 us (38%)
  waiting for transfers between devices  26.3 us (26%)
  Pallas kernels  16.8 us (17%)
  blocking collectives  12.1 us (12%)
  local copies, waits for them, and re-layouts  5.38 us (5%)
    ppermute x9, starting transfers between devices, moved(): return lax.ppermute(array, (*AXES, 'chan'), device_pairs(move))  18.6 us
    all_to_all x1, starting transfers between devices, body(): lax.all_to_all(packed.reshape(SEQ_DEVICES, 32, LANES), AXES, split_axis=0...  15.7 us
    all_to_all x1, waiting for transfers between devices, body(): lax.all_to_all(packed.reshape(SEQ_DEVICES, 32, LANES), AXES, split_axis=0...  14.4 us
    all_to_all x1, blocking collectives, body(): lax.all_to_all(rounded, 'chan', split_axis=0, concat_axis=0, tiled=True)  12.1 us
    ppermute x9, waiting for transfers between devices, moved(): return lax.ppermute(array, (*AXES, 'chan'), device_pairs(move))  6.51 us
    pallas_call x1, Pallas kernels, body(): call(convolve_kernel, jax.ShapeDtypeStruct((SEQ_DEVICES * 16, LANES), jnp...  5.92 us
    pallas_call x1, Pallas kernels, body(): call(project_kernel, (jax.ShapeDtypeStruct((LANES, 2 * HALF), jnp.bfloat1...  5.68 us
    all_to_all x1, waiting for transfers between devices, body(): lax.all_to_all(convolved.reshape(SEQ_DEVICES, 16, LANES), AXES, split_axi...  5.44 us
  transfers between devices with their start and end apart: 11, of which 6 were waited for; matrix products, arithmetic and copies ran while one was open for 2% of the time, Pallas kernels for 7%

profile of v8, /device:TPU:1, one launch (start us, length us, event | category | flops | bytes accessed | tf_op | source)
XLA Modules:
  0.0 100.0 jit_solution(7145828755710055905)
XLA Ops:
  0.6 3.1 %shard_map.86 = (bf16[2048,128]{1,0:T(8,128)(2,1)}, f32[8,128]{1,0:T(8,128)}) custom-call(f32[256,512]{1,0:T(8,128)} %signal_ref.3, f32[256,512]{1,0:T(8,128)} %filter_ref.1), custom_call_target="tpu_custom_call" | custom-call | flops 10000000000 | tf_op jit(solution)/shard_map/pallas_call | solution.py:257
  3.7 0.0 copy-start.5
  3.7 15.7 %all-to-all-start = ((bf16[64,32,128]{2,1,0:T(8,128)(2,1)}), bf16[64,32,128]{2,1,0:T(8,128)(2,1)S(1)}, u32[]{:S(2)}, u32[]{:S(2)}) async-start(bf16[64,32,128]{2,1,0:T(8,128)(2,1)} %bitcast.10), calls=%async_computation | async-start | bytes 1048576 | tf_op jit(solution)/shard_map/all_to_all | solution.py:266
  19.5 1.1 %constant_dynamic-slice_fusion = bf16[256,1024]{1,0:T(8,128)(2,1)S(1)} fusion(bf16[256,8192]{1,0:T(8,128)(2,1)} %own_ref.1, s32[]{:T(128)S(6)} %select_n.15), kind=kLoop, calls=%fused_computation | loop fusion | bytes 1048580 | tf_op jit(solution)/shard_map/dynamic_slice | solution.py:178
  20.6 4.5 %collective-permute-start.3 = (bf16[256,1024]{1,0:T(8,128)(2,1)S(1)}, bf16[256,1024]{1,0:T(8,128)(2,1)S(1)}, u32[]{:S(2)}, u32[]{:S(2)}) collective-permute-start(bf16[256,1024]{1,0:T(8,128)(2,1)S(1)} %constant_dynamic-slice_fusion), channel_id=1, source_target_pairs={{0,2},{4,14},{1,3},{5,15},{2,8},{6,4},{3,9},{7,5},{8,10},{12,6},{9... | collective-permute-start | bytes 1572872 | tf_op jit(solution)/shard_map/ppermute | solution.py:151
  25.1 0.7 collective-permute-start.2
  25.8 0.7 collective-permute-start.1
  26.5 0.0 copy-done.5
  26.5 0.1 copy.10.skip_ref
  26.7 14.4 %all-to-all-done = bf16[64,32,128]{2,1,0:T(8,128)(2,1)S(1)} async-done(((bf16[64,32,128]{2,1,0:T(8,128)(2,1)}), bf16[64,32,128]{2,1,0:T(8,128)(2,1)S(1)}, u32[]{:S(2)}, u32[]{:S(2)}) %all-to-all-start) | async-done | bytes 524320 | tf_op jit(solution)/shard_map/all_to_all | solution.py:266
  41.0 0.0 copy-start.4
  41.0 0.8 copy-done.4
  41.8 0.0 copy-start.3
  41.8 5.9 %shard_map.87 = bf16[1024,128]{1,0:T(8,128)(2,1)} custom-call(bf16[2048,128]{1,0:T(8,128)(2,1)} %bitcast.9, bf16[1536,256]{1,0:T(8,128)(2,1)} %constant.41.clone.factors_ref, f32[512,128]{1,0:T(8,128)} %constant.42.clone.turn_ref), custom_call_target="tpu_custom_call" | custom-call | flops 99999997952 | tf_op jit(solution)/shard_map/pallas_call | solution.py:269
  47.8 4.2 %all-to-all-start.1 = ((bf16[64,16,128]{2,1,0:T(8,128)(2,1)}), bf16[64,16,128]{2,1,0:T(8,128)(2,1)S(1)}, u32[]{:S(2)}, u32[]{:S(2)}) async-start(bf16[64,16,128]{2,1,0:T(8,128)(2,1)} %bitcast.11), calls=%async_computation.1 | async-start | bytes 524288 | tf_op jit(solution)/shard_map/all_to_all | solution.py:279
  51.9 0.0 collective-permute-done.3.far_ref
  52.0 3.1 %collective-permute-done.2.above_ref = bf16[256,1024]{1,0:T(8,128)(2,1)S(1)} collective-permute-done((bf16[256,1024]{1,0:T(8,128)(2,1)S(1)}, bf16[256,1024]{1,0:T(8,128)(2,1)S(1)}, u32[]{:S(2)}, u32[]{:S(2)}) %collective-permute-start.2) | collective-permute-done | bytes 524320 | tf_op jit(solution)/shard_map/ppermute | solution.py:151
  55.0 0.0 collective-permute-done.1.below_ref
  55.0 0.0 copy-done.3
  55.0 0.1 shard_map.89.refs_0_
  55.2 1.5 %collective-permute-start.7 = (bf16[768,1024]{1,0:T(8,128)(2,1)S(1)}, bf16[768,1024]{1,0:T(8,128)(2,1)S(1)}, u32[]{:S(2)}, u32[]{:S(2)}) collective-permute-start(bf16[768,1024]{1,0:T(8,128)(2,1)S(1)} %shard_map.89.refs_0_), channel_id=1, source_target_pairs={{0,16},{4,68},{1,17},{5,69},{2,18},{6,70},{3,19},{7,71},{8,24},{12... | collective-permute-start | bytes 4718600 | tf_op jit(solution)/shard_map/ppermute | solution.py:151
  56.6 1.5 %collective-permute-start.4 = (bf16[768,1024]{1,0:T(8,128)(2,1)S(1)}, bf16[768,1024]{1,0:T(8,128)(2,1)}, u32[]{:S(2)}, u32[]{:S(2)}) collective-permute-start(bf16[768,1024]{1,0:T(8,128)(2,1)S(1)} %shard_map.89.refs_0_), channel_id=1, source_target_pairs={{0,48},{4,196},{1,49},{5,197},{2,50},{6,198},{3,51},{7,199},{8,56}... | collective-permute-start | bytes 4718600 | tf_op jit(solution)/shard_map/ppermute | solution.py:151
  58.1 1.3 %fusion = (bf16[384,1024]{1,0:T(8,128)(2,1)}, bf16[384,1024]{1,0:T(8,128)(2,1)}) fusion(bf16[768,1024]{1,0:T(8,128)(2,1)S(1)} %shard_map.89.refs_0_), kind=kLoop, calls=%fused_computation.1 | loop fusion | bytes 3145728 | tf_op jit(solution)/shard_map/slice | solution.py:195
  59.4 2.5 %collective-permute-start.6 = (bf16[384,1024]{1,0:T(8,128)(2,1)}, bf16[384,1024]{1,0:T(8,128)(2,1)}, u32[]{:S(2)}, u32[]{:S(2)}) collective-permute-start(bf16[384,1024]{1,0:T(8,128)(2,1)} %get-tuple-element.14), channel_id=1, source_target_pairs={{0,192},{4,52},{1,193},{5,53},{2,194},{6,54},{3,195},{7,55},{8,200... | collective-permute-start | bytes 2359304 | tf_op jit(solution)/shard_map/ppermute | solution.py:151
  61.9 0.0 collective-permute-start.5
  61.9 5.4 %all-to-all-done.1 = bf16[64,16,128]{2,1,0:T(8,128)(2,1)S(1)} async-done(((bf16[64,16,128]{2,1,0:T(8,128)(2,1)}), bf16[64,16,128]{2,1,0:T(8,128)(2,1)S(1)}, u32[]{:S(2)}, u32[]{:S(2)}) %all-to-all-start.1) | async-done | bytes 262176 | tf_op jit(solution)/shard_map/all_to_all | solution.py:279
  67.3 0.0 copy-start.1
  67.3 1.0 %copy-done.1 = f32[256,512]{1,0:T(8,128)S(1)} copy-done((f32[256,512]{1,0:T(8,128)S(1)}, f32[256,512]{1,0:T(8,128)}, u32[]{:S(2)}) %copy-start.1) | copy-done | bytes 524312
  68.4 0.0 copy-start.2
  68.4 1.0 %copy-done.2 = f32[256,512]{1,0:T(8,128)S(1)} copy-done((f32[256,512]{1,0:T(8,128)S(1)}, f32[256,512]{1,0:T(8,128)}, u32[]{:S(2)}) %copy-start.2) | copy-done | bytes 524312
  69.4 0.0 copy-start
  69.4 1.0 %shard_map.88 = (f32[256,512]{1,0:T(8,128)}, bf16[4,256,128]{2,1,0:T(8,128)(2,1)S(1)}) custom-call(bf16[1024,128]{1,0:T(8,128)(2,1)S(1)} %bitcast.8, f32[256,512]{1,0:T(8,128)S(1)} %copy-done.1, f32[256,512]{1,0:T(8,128)S(1)} %copy-done.2, f32[256,1]{1,0:T(8,128)S(1)} %copy.10.skip_ref), custom_call_target="tpu_custom_call" | custom-call | flops 99999997952 | tf_op jit(solution)/shard_map/pallas_call | solution.py:283
  70.5 12.1 %all_to_all.15 = bf16[4,256,128]{2,1,0:T(8,128)(2,1)S(1)} all-to-all(bf16[4,256,128]{2,1,0:T(8,128)(2,1)S(1)} %get-tuple-element.10), channel_id=1, replica_groups=mesh['y'=4,'x'=4,'zh'=2,'core'=2,'chan'=4] {'chan'}, dimensions={0} | all-to-all | bytes 524288 | tf_op jit(solution)/shard_map/all_to_all | solution.py:293
  82.5 2.7 %collective-permute-start = (bf16[1024,128]{1,0:T(8,128)(2,1)S(1)}, bf16[1024,128]{1,0:T(8,128)(2,1)S(1)}, u32[]{:S(2)}, u32[]{:S(2)}) collective-permute-start(bf16[1024,128]{1,0:T(8,128)(2,1)S(1)} %bitcast.6), channel_id=1, source_target_pairs={{0,4},{4,0},{1,5},{5,1},{2,6},{6,2},{3,7},{7,3},{8,12},{12,8},{9,1... | collective-permute-start | bytes 786440 | tf_op jit(solution)/shard_map/ppermute | solution.py:151
  85.3 0.0 collective-permute-done.6.refs_3_
  85.3 0.0 collective-permute-done.5.refs_2_
  85.3 0.0 collective-permute-done.7.refs_4_
  85.3 0.8 collective-permute-done.4.refs_1_
  86.1 0.4 collective-permute-done.theirs_ref
  86.4 0.0 copy-done
  86.4 5.7 %shard_map.90 = (bf16[128,8192]{1,0:T(8,128)(2,1)}, bf16[128,4096]{1,0:T(8,128)(2,1)S(1)}) custom-call(bf16[1024,128]{1,0:T(8,128)(2,1)S(1)} %bitcast.7, bf16[1024,128]{1,0:T(8,128)(2,1)S(1)} %collective-permute-done.theirs_ref, bf16[256,8192]{1,0:T(8,128)(2,1)S(1)} %copy-done, bf16[768,1024]{1,0:T(8,128)(2,1)S(1)} %shard_map.89.refs_0_, ...), custom_call_target="tpu_custom_call" | custom-call | tf_op jit(solution)/shard_map/pallas_call | solution.py:295
  92.1 4.5 %collective-permute-start.8 = (bf16[128,4096]{1,0:T(8,128)(2,1)S(1)}, bf16[128,4096]{1,0:T(8,128)(2,1)S(1)}, u32[]{:S(2)}, u32[]{:S(2)}) collective-permute-start(bf16[128,4096]{1,0:T(8,128)(2,1)S(1)} %get-tuple-element.13), channel_id=1, source_target_pairs={{0,4},{4,0},{1,5},{5,1},{2,6},{6,2},{3,7},{7,3},{8,12},{12,8},{9,1... | collective-permute-start | bytes 3145736 | tf_op jit(solution)/shard_map/ppermute | solution.py:151
  96.6 2.3 %collective-permute-done.8.from_them_ref = bf16[128,4096]{1,0:T(8,128)(2,1)S(1)} collective-permute-done((bf16[128,4096]{1,0:T(8,128)(2,1)S(1)}, bf16[128,4096]{1,0:T(8,128)(2,1)S(1)}, u32[]{:S(2)}, u32[]{:S(2)}) %collective-permute-start.8) | collective-permute-done | bytes 1048608 | tf_op jit(solution)/shard_map/ppermute | solution.py:151
  98.9 1.0 shard_map.91
Async XLA Ops:
  3.7 22.8 %copy-start.5 = (f32[256]{0:T(256)S(1)}, f32[256]{0:T(256)}, u32[]{:S(2)}) copy-start(f32[256]{0:T(256)} %param.10) | copy-start | bytes 3076
  3.7 37.3 %all-to-all-start = ((bf16[64,32,128]{2,1,0:T(8,128)(2,1)}), bf16[64,32,128]{2,1,0:T(8,128)(2,1)S(1)}, u32[]{:S(2)}, u32[]{:S(2)}) async-start(bf16[64,32,128]{2,1,0:T(8,128)(2,1)} %bitcast.10), calls=%async_computation | async-start | bytes 1048576 | tf_op jit(solution)/shard_map/all_to_all | solution.py:266
  20.6 31.4 %collective-permute-start.3 = (bf16[256,1024]{1,0:T(8,128)(2,1)S(1)}, bf16[256,1024]{1,0:T(8,128)(2,1)S(1)}, u32[]{:S(2)}, u32[]{:S(2)}) collective-permute-start(bf16[256,1024]{1,0:T(8,128)(2,1)S(1)} %constant_dynamic-slice_fusion), channel_id=1, source_target_pairs={{0,2},{4,14},{1,3},{5,15},{2,8},{6,4},{3,9},{7,5},{8,10},{12,6},{9... | collective-permute-start | bytes 1572872 | tf_op jit(solution)/shard_map/ppermute | solution.py:151
  25.1 29.9 %collective-permute-start.2 = (bf16[256,1024]{1,0:T(8,128)(2,1)S(1)}, bf16[256,1024]{1,0:T(8,128)(2,1)S(1)}, u32[]{:S(2)}, u32[]{:S(2)}) collective-permute-start(bf16[256,1024]{1,0:T(8,128)(2,1)S(1)} %constant_dynamic-slice_fusion), channel_id=1, source_target_pairs={{0,11},{4,15},{1,0},{5,4},{2,1},{6,5},{3,2},{7,6},{8,3},{12,7},{9,... | collective-permute-start | bytes 1572872 | tf_op jit(solution)/shard_map/ppermute | solution.py:151
  25.8 29.2 %collective-permute-start.1 = (bf16[256,1024]{1,0:T(8,128)(2,1)S(1)}, bf16[256,1024]{1,0:T(8,128)(2,1)S(1)}, u32[]{:S(2)}, u32[]{:S(2)}) collective-permute-start(bf16[256,1024]{1,0:T(8,128)(2,1)S(1)} %constant_dynamic-slice_fusion), channel_id=1, source_target_pairs={{0,1},{4,5},{1,2},{5,6},{2,3},{6,7},{3,8},{7,12},{8,9},{12,13},{9,... | collective-permute-start | bytes 1572872 | tf_op jit(solution)/shard_map/ppermute | solution.py:151
  41.0 0.8 copy-start.4
  41.8 13.2 %copy-start.3 = (f32[8,128]{1,0:T(8,128)S(1)}, f32[8,128]{1,0:T(8,128)}, u32[]{:S(2)}) copy-start(f32[8,128]{1,0:T(8,128)} %get-tuple-element.11.after_ref) | copy-start | bytes 12292
  47.8 19.6 %all-to-all-start.1 = ((bf16[64,16,128]{2,1,0:T(8,128)(2,1)}), bf16[64,16,128]{2,1,0:T(8,128)(2,1)S(1)}, u32[]{:S(2)}, u32[]{:S(2)}) async-start(bf16[64,16,128]{2,1,0:T(8,128)(2,1)} %bitcast.11), calls=%async_computation.1 | async-start | bytes 524288 | tf_op jit(solution)/shard_map/all_to_all | solution.py:279
  55.2 30.1 %collective-permute-start.7 = (bf16[768,1024]{1,0:T(8,128)(2,1)S(1)}, bf16[768,1024]{1,0:T(8,128)(2,1)S(1)}, u32[]{:S(2)}, u32[]{:S(2)}) collective-permute-start(bf16[768,1024]{1,0:T(8,128)(2,1)S(1)} %shard_map.89.refs_0_), channel_id=1, source_target_pairs={{0,16},{4,68},{1,17},{5,69},{2,18},{6,70},{3,19},{7,71},{8,24},{12... | collective-permute-start | bytes 4718600 | tf_op jit(solution)/shard_map/ppermute | solution.py:151
  56.6 29.4 %collective-permute-start.4 = (bf16[768,1024]{1,0:T(8,128)(2,1)S(1)}, bf16[768,1024]{1,0:T(8,128)(2,1)}, u32[]{:S(2)}, u32[]{:S(2)}) collective-permute-start(bf16[768,1024]{1,0:T(8,128)(2,1)S(1)} %shard_map.89.refs_0_), channel_id=1, source_target_pairs={{0,48},{4,196},{1,49},{5,197},{2,50},{6,198},{3,51},{7,199},{8,56}... | collective-permute-start | bytes 4718600 | tf_op jit(solution)/shard_map/ppermute | solution.py:151
  59.4 25.8 %collective-permute-start.6 = (bf16[384,1024]{1,0:T(8,128)(2,1)}, bf16[384,1024]{1,0:T(8,128)(2,1)}, u32[]{:S(2)}, u32[]{:S(2)}) collective-permute-start(bf16[384,1024]{1,0:T(8,128)(2,1)} %get-tuple-element.14), channel_id=1, source_target_pairs={{0,192},{4,52},{1,193},{5,53},{2,194},{6,54},{3,195},{7,55},{8,200... | collective-permute-start | bytes 2359304 | tf_op jit(solution)/shard_map/ppermute | solution.py:151
  61.9 23.4 %collective-permute-start.5 = (bf16[384,1024]{1,0:T(8,128)(2,1)}, bf16[384,1024]{1,0:T(8,128)(2,1)}, u32[]{:S(2)}, u32[]{:S(2)}) collective-permute-start(bf16[384,1024]{1,0:T(8,128)(2,1)} %get-tuple-element.15), channel_id=1, source_target_pairs={{0,64},{4,20},{1,65},{5,21},{2,66},{6,22},{3,67},{7,23},{8,72},{12... | collective-permute-start | bytes 2359304 | tf_op jit(solution)/shard_map/ppermute | solution.py:151
  67.3 1.0 %copy-start.1 = (f32[256,512]{1,0:T(8,128)S(1)}, f32[256,512]{1,0:T(8,128)}, u32[]{:S(2)}) copy-start(f32[256,512]{1,0:T(8,128)} %signal_ref.3) | copy-start | bytes 1572868
  68.4 1.0 %copy-start.2 = (f32[256,512]{1,0:T(8,128)S(1)}, f32[256,512]{1,0:T(8,128)}, u32[]{:S(2)}) copy-start(f32[256,512]{1,0:T(8,128)} %gate_ref.1) | copy-start | bytes 1572868
  69.4 17.0 %copy-start = (bf16[256,8192]{1,0:T(8,128)(2,1)S(1)}, bf16[256,8192]{1,0:T(8,128)(2,1)}, u32[]{:S(2)}) copy-start(bf16[256,8192]{1,0:T(8,128)(2,1)} %own_ref.1) | copy-start | bytes 12582916
  82.5 3.9 %collective-permute-start = (bf16[1024,128]{1,0:T(8,128)(2,1)S(1)}, bf16[1024,128]{1,0:T(8,128)(2,1)S(1)}, u32[]{:S(2)}, u32[]{:S(2)}) collective-permute-start(bf16[1024,128]{1,0:T(8,128)(2,1)S(1)} %bitcast.6), channel_id=1, source_target_pairs={{0,4},{4,0},{1,5},{5,1},{2,6},{6,2},{3,7},{7,3},{8,12},{12,8},{9,1... | collective-permute-start | bytes 786440 | tf_op jit(solution)/shard_map/ppermute | solution.py:151
  92.1 6.8 %collective-permute-start.8 = (bf16[128,4096]{1,0:T(8,128)(2,1)S(1)}, bf16[128,4096]{1,0:T(8,128)(2,1)S(1)}, u32[]{:S(2)}, u32[]{:S(2)}) collective-permute-start(bf16[128,4096]{1,0:T(8,128)(2,1)S(1)} %get-tuple-element.13), channel_id=1, source_target_pairs={{0,4},{4,0},{1,5},{5,1},{2,6},{6,2},{3,7},{7,3},{8,12},{12,8},{9,1... | collective-permute-start | bytes 3145736 | tf_op jit(solution)/shard_map/ppermute | solution.py:151

commit v9 on v8

--- a/solution.py
+++ b/solution.py
@@ -1,3 +1,4 @@
+import functools
 import itertools
 
 import jax
@@ -22,7 +23,7 @@
 SPLIT = 384
 CONVOLVE = 60
 MIX = 24
-LAST = 30
+LAST = 48
 WORK = 10**11
 PACK_WORK = 10**10
 JOIN_WORK = 10**10
@@ -202,10 +203,22 @@
     ]
 
 
-def project_kernel(mine_ref, theirs_ref, own_ref, *refs):
-    block_refs, (out_ref, for_them_ref, results, out_sem) = refs[:5], refs[5:]
+def place_of(core, index):
+    return pl.multiple_of(core * HALF + (colour(core) + index) % 4 * QUARTER, QUARTER)
+
+
+def project_kernel(quarters, mine_ref, theirs_ref, own_ref, *refs):
+    count = sum(parts for _, parts in quarters)
+    block_refs, (out_ref, for_them_ref, own, results, own_sem, out_sem) = refs[:count], refs[-6:]
     core, chan = lax.axis_index("core"), lax.axis_index("chan")
-    first = core * HALF
+    loads = [
+        pltpu.make_async_copy(
+            own_ref.at[:, pl.ds(place_of(core, index), QUARTER)], own.at[order], own_sem.at[order]
+        )
+        for order, (index, _) in enumerate(quarters)
+    ]
+    for load in loads:
+        load.start()
     rows = [
         jnp.concatenate(
             [
@@ -217,22 +230,25 @@
         for shift in (0, 3, 1, 2)
     ]
     own_columns, columns = rows[0], jnp.concatenate(rows[1:], axis=1)
-    stores = []
-    for index, parts in enumerate(((0,), (1,), (2, 3), (4,))):
-        start = pl.multiple_of((colour(core) + index) % 4 * QUARTER, QUARTER)
-        place = pl.multiple_of(first + start, QUARTER)
-        total = matmul(own_columns, own_ref[:, pl.ds(place, QUARTER)])
+    stores, part = [], 0
+    for order, (index, parts) in enumerate(quarters):
+        place = place_of(core, index)
+        loads[order].wait()
+        total = matmul(own_columns, own[order])
         row = 0
-        for part in parts:
-            block = block_refs[part][...]
+        for block_ref in block_refs[part : part + parts]:
+            block = block_ref[...]
             total += matmul(columns[:, row : row + block.shape[0]], block)
             row += block.shape[0]
-        results[index] = total.astype(jnp.bfloat16)
-        for rank, (target, offset) in enumerate(((out_ref, place), (for_them_ref, start))):
+        part += parts
+        results[order] = total.astype(jnp.bfloat16)
+        targets = (
+            out_ref.at[:, pl.ds(place, QUARTER)],
+            for_them_ref.at[:, pl.ds(order * QUARTER, QUARTER)],
+        )
+        for rank, target in enumerate(targets):
             store = pltpu.make_async_copy(
-                results.at[index, pl.ds(rank * LANES, LANES)],
-                target.at[:, pl.ds(offset, QUARTER)],
-                out_sem.at[index, rank],
+                results.at[order, pl.ds(rank * LANES, LANES)], target, out_sem.at[order, rank]
             )
             store.start()
             stores.append(store)
@@ -240,11 +256,46 @@
         store.wait()
 
 
-def fill_kernel(half_ref, from_them_ref, out_ref, sem):
-    start = pl.multiple_of((1 - lax.axis_index("core")) * HALF, HALF)
-    copy = pltpu.make_async_copy(from_them_ref, out_ref.at[:, pl.ds(start, HALF)], sem)
-    copy.start()
-    copy.wait()
+def fill_kernel(filled_ref, first_ref, second_ref, out_ref, sem):
+    core = 1 - lax.axis_index("core")
+    copies = []
+    for which, (quarters, from_them_ref) in enumerate(zip(HALVES, (first_ref, second_ref))):
+        for order, (index, _) in enumerate(quarters):
+            copies.append(
+                pltpu.make_async_copy(
+                    from_them_ref.at[:, pl.ds(order * QUARTER, QUARTER)],
+                    out_ref.at[:, pl.ds(place_of(core, index), QUARTER)],
+                    sem.at[which, order],
+                )
+            )
+    for copy in copies:
+        copy.start()
+    for copy in copies:
+        copy.wait()
+
+
+HALVES = (((0, 1), (2, 2)), ((1, 1), (3, 1)))
+
+
+def projected_quarters(quarters, columns, own, blocks, filled):
+    last = [] if filled is None else [filled]
+    return call(
+        functools.partial(project_kernel, quarters),
+        (
+            jax.ShapeDtypeStruct((LANES, 2 * HALF), jnp.bfloat16),
+            jax.ShapeDtypeStruct((LANES, HALF // 2), jnp.bfloat16),
+        ),
+        [
+            pltpu.VMEM((2, ROWS, QUARTER), jnp.bfloat16),
+            pltpu.VMEM((2, 2 * LANES, QUARTER), jnp.bfloat16),
+            pltpu.SemaphoreType.DMA((2,)),
+            pltpu.SemaphoreType.DMA((2, 2)),
+        ],
+        limit=LAST,
+        in_specs=[INSIDE] * 2 + [ANYWHERE] + [INSIDE] * len(blocks) + [ANYWHERE] * len(last),
+        out_specs=(ANYWHERE, ANYWHERE),
+        input_output_aliases={3 + len(blocks): 0} if last else {},
+    )(*columns, own, *blocks, *last)
 
 
 def swapped(array):
@@ -292,29 +343,19 @@
     )(returned.reshape(SEQ_DEVICES * 16, LANES), signal, gate, skip_weight[:, None])
     mine = lax.all_to_all(rounded, "chan", split_axis=0, concat_axis=0, tiled=True)
     mine = mine.reshape(4 * channels, LANES)
-    half_filled, for_them = call(
-        project_kernel,
-        (
-            jax.ShapeDtypeStruct((LANES, 2 * HALF), jnp.bfloat16),
-            jax.ShapeDtypeStruct((LANES, HALF), jnp.bfloat16),
-        ),
-        [
-            pltpu.VMEM((4, 2 * LANES, QUARTER), jnp.bfloat16),
-            pltpu.SemaphoreType.DMA((4, 2)),
-        ],
-        limit=LAST,
-        in_specs=[INSIDE] * 8,
-        out_specs=(ANYWHERE, ANYWHERE),
-    )(mine, swapped(mine), out_weight, *blocks)
+    columns = (mine, swapped(mine))
+    lower, across, upper = blocks[1], blocks[2:4], blocks[4]
+    filled, first = projected_quarters(HALVES[0], columns, out_weight, [blocks[0], *across], None)
+    filled, second = projected_quarters(HALVES[1], columns, out_weight, [lower, upper], filled)
     projected = call(
         fill_kernel,
-        jax.ShapeDtypeStruct(half_filled.shape, half_filled.dtype),
-        [pltpu.SemaphoreType.DMA(())],
+        jax.ShapeDtypeStruct(filled.shape, filled.dtype),
+        [pltpu.SemaphoreType.DMA((2, 2))],
         limit=2,
-        in_specs=[ANYWHERE] * 2,
+        in_specs=[ANYWHERE] * 3,
         out_specs=ANYWHERE,
         input_output_aliases={0: 0},
-    )(half_filled, swapped(for_them))
+    )(filled, swapped(first), swapped(second))
     return mixed, projected
 
 

time: 101 us -> 100 us (0.990)
  Pallas kernels: 16.8 us -> 20.8 us
  starting transfers between devices: 38.5 us -> 34.7 us
    pallas_call x2 -> x3, Pallas kernels: 6.66 us -> 10.6 us  [the longest x2 9.62 us: projected_quarters(): call(functools.partial(project_kernel, quarters), (jax.ShapeDtypeStruct((...]
    ppermute x9 -> x10, starting transfers between devices: 18.6 us -> 14.8 us  [moved(): return lax.ppermute(array, (*AXES, 'chan'), device_pairs(move))]
    ppermute x9 -> x10, waiting for transfers between devices: 6.51 us -> 6.01 us  [moved(): return lax.ppermute(array, (*AXES, 'chan'), device_pairs(move))]
    unnamed x12 -> x10, local copies, waits for them, and re-layouts: 2.89 us -> 2.88 us
  transfers between devices with their start and end apart: 11 -> 12, of which waited for: 6 -> 5; matrix products, arithmetic and copies ran while one was open for 2% -> 2% of each run, Pallas kernels for 7% -> 17%
where the time goes in v9:
time: 100 us; the launch traced here: 99.5 us
  starting transfers between devices  34.7 us (35%)
  waiting for transfers between devices  25.8 us (26%)
  Pallas kernels  20.8 us (21%)
  blocking collectives  12 us (12%)
  local copies, waits for them, and re-layouts  5.36 us (5%)
    all_to_all x1, starting transfers between devices, body(): lax.all_to_all(packed.reshape(SEQ_DEVICES, 32, LANES), AXES, split_axis=0...  15.7 us
    ppermute x10, starting transfers between devices, moved(): return lax.ppermute(array, (*AXES, 'chan'), device_pairs(move))  14.8 us
    all_to_all x1, waiting for transfers between devices, body(): lax.all_to_all(packed.reshape(SEQ_DEVICES, 32, LANES), AXES, split_axis=0...  14.4 us
    all_to_all x1, blocking collectives, body(): lax.all_to_all(rounded, 'chan', split_axis=0, concat_axis=0, tiled=True)  12 us
    pallas_call x2, Pallas kernels, projected_quarters(): call(functools.partial(project_kernel, quarters), (jax.ShapeDtypeStruct((...  9.62 us
    ppermute x10, waiting for transfers between devices, moved(): return lax.ppermute(array, (*AXES, 'chan'), device_pairs(move))  6.01 us
    pallas_call x1, Pallas kernels, body(): call(convolve_kernel, jax.ShapeDtypeStruct((SEQ_DEVICES * 16, LANES), jnp...  5.92 us
    all_to_all x1, waiting for transfers between devices, body(): lax.all_to_all(convolved.reshape(SEQ_DEVICES, 16, LANES), AXES, split_axi...  5.46 us
  transfers between devices with their start and end apart: 12, of which 5 were waited for; matrix products, arithmetic and copies ran while one was open for 2% of the time, Pallas kernels for 17%

profile of v9, /device:TPU:1, one launch (start us, length us, event | category | flops | bytes accessed | tf_op | source)
XLA Modules:
  0.0 99.5 jit_solution(1208486866833287795)
XLA Ops:
  0.6 3.1 %shard_map.86 = (bf16[2048,128]{1,0:T(8,128)(2,1)}, f32[8,128]{1,0:T(8,128)}) custom-call(f32[256,512]{1,0:T(8,128)} %signal_ref.3, f32[256,512]{1,0:T(8,128)} %filter_ref.1), custom_call_target="tpu_custom_call" | custom-call | flops 10000000000 | tf_op jit(solution)/shard_map/pallas_call | solution.py:308
  3.7 0.0 copy-start.4
  3.7 15.7 %all-to-all-start = ((bf16[64,32,128]{2,1,0:T(8,128)(2,1)}), bf16[64,32,128]{2,1,0:T(8,128)(2,1)S(1)}, u32[]{:S(2)}, u32[]{:S(2)}) async-start(bf16[64,32,128]{2,1,0:T(8,128)(2,1)} %bitcast.11), calls=%async_computation | async-start | bytes 1048576 | tf_op jit(solution)/shard_map/all_to_all | solution.py:317
  19.5 1.1 %constant_dynamic-slice_fusion = bf16[256,1024]{1,0:T(8,128)(2,1)S(1)} fusion(bf16[256,8192]{1,0:T(8,128)(2,1)} %own_ref.3, s32[]{:T(128)S(6)} %select_n.15), kind=kLoop, calls=%fused_computation | loop fusion | bytes 1048580 | tf_op jit(solution)/shard_map/dynamic_slice | solution.py:179
  20.6 4.5 %collective-permute-start.3 = (bf16[256,1024]{1,0:T(8,128)(2,1)S(1)}, bf16[256,1024]{1,0:T(8,128)(2,1)S(1)}, u32[]{:S(2)}, u32[]{:S(2)}) collective-permute-start(bf16[256,1024]{1,0:T(8,128)(2,1)S(1)} %constant_dynamic-slice_fusion), channel_id=1, source_target_pairs={{0,2},{4,14},{1,3},{5,15},{2,8},{6,4},{3,9},{7,5},{8,10},{12,6},{9... | collective-permute-start | bytes 1572872 | tf_op jit(solution)/shard_map/ppermute | solution.py:152
  25.1 0.7 collective-permute-start.2
  25.8 0.7 collective-permute-start.1
  26.5 0.0 copy-done.4
  26.5 0.1 copy.11.skip_ref
  26.7 14.4 %all-to-all-done = bf16[64,32,128]{2,1,0:T(8,128)(2,1)S(1)} async-done(((bf16[64,32,128]{2,1,0:T(8,128)(2,1)}), bf16[64,32,128]{2,1,0:T(8,128)(2,1)S(1)}, u32[]{:S(2)}, u32[]{:S(2)}) %all-to-all-start) | async-done | bytes 524320 | tf_op jit(solution)/shard_map/all_to_all | solution.py:317
  41.0 0.0 copy-start.3
  41.0 0.8 copy-done.3
  41.8 0.0 copy-start.2
  41.8 5.9 %shard_map.87 = bf16[1024,128]{1,0:T(8,128)(2,1)} custom-call(bf16[2048,128]{1,0:T(8,128)(2,1)} %bitcast.10, bf16[1536,256]{1,0:T(8,128)(2,1)} %constant.41.clone.factors_ref, f32[512,128]{1,0:T(8,128)} %constant.42.clone.turn_ref), custom_call_target="tpu_custom_call" | custom-call | flops 99999997952 | tf_op jit(solution)/shard_map/pallas_call | solution.py:320
  47.8 4.2 %all-to-all-start.1 = ((bf16[64,16,128]{2,1,0:T(8,128)(2,1)}), bf16[64,16,128]{2,1,0:T(8,128)(2,1)S(1)}, u32[]{:S(2)}, u32[]{:S(2)}) async-start(bf16[64,16,128]{2,1,0:T(8,128)(2,1)} %bitcast.12), calls=%async_computation.1 | async-start | bytes 524288 | tf_op jit(solution)/shard_map/all_to_all | solution.py:330
  51.9 0.0 collective-permute-done.3.far_ref
  51.9 3.1 %collective-permute-done.2.above_ref = bf16[256,1024]{1,0:T(8,128)(2,1)S(1)} collective-permute-done((bf16[256,1024]{1,0:T(8,128)(2,1)S(1)}, bf16[256,1024]{1,0:T(8,128)(2,1)S(1)}, u32[]{:S(2)}, u32[]{:S(2)}) %collective-permute-start.2) | collective-permute-done | bytes 524320 | tf_op jit(solution)/shard_map/ppermute | solution.py:152
  55.0 0.0 collective-permute-done.1.below_ref
  55.0 0.0 copy-done.2
  55.0 0.1 shard_map.89.refs_0_
  55.2 1.5 %collective-permute-start.5 = (bf16[768,1024]{1,0:T(8,128)(2,1)S(1)}, bf16[768,1024]{1,0:T(8,128)(2,1)S(1)}, u32[]{:S(2)}, u32[]{:S(2)}) collective-permute-start(bf16[768,1024]{1,0:T(8,128)(2,1)S(1)} %shard_map.89.refs_0_), channel_id=1, source_target_pairs={{0,16},{4,68},{1,17},{5,69},{2,18},{6,70},{3,19},{7,71},{8,24},{12... | collective-permute-start | bytes 4718600 | tf_op jit(solution)/shard_map/ppermute | solution.py:152
  56.6 1.5 %collective-permute-start.4 = (bf16[768,1024]{1,0:T(8,128)(2,1)S(1)}, bf16[768,1024]{1,0:T(8,128)(2,1)}, u32[]{:S(2)}, u32[]{:S(2)}) collective-permute-start(bf16[768,1024]{1,0:T(8,128)(2,1)S(1)} %shard_map.89.refs_0_), channel_id=1, source_target_pairs={{0,48},{4,196},{1,49},{5,197},{2,50},{6,198},{3,51},{7,199},{8,56}... | collective-permute-start | bytes 4718600 | tf_op jit(solution)/shard_map/ppermute | solution.py:152
  58.1 1.3 %fusion = (bf16[384,1024]{1,0:T(8,128)(2,1)}, bf16[384,1024]{1,0:T(8,128)(2,1)}) fusion(bf16[768,1024]{1,0:T(8,128)(2,1)S(1)} %shard_map.89.refs_0_), kind=kLoop, calls=%fused_computation.1 | loop fusion | bytes 3145728 | tf_op jit(solution)/shard_map/slice | solution.py:196
  59.4 2.5 %collective-permute-start.7 = (bf16[384,1024]{1,0:T(8,128)(2,1)}, bf16[384,1024]{1,0:T(8,128)(2,1)}, u32[]{:S(2)}, u32[]{:S(2)}) collective-permute-start(bf16[384,1024]{1,0:T(8,128)(2,1)} %get-tuple-element.18), channel_id=1, source_target_pairs={{0,192},{4,52},{1,193},{5,53},{2,194},{6,54},{3,195},{7,55},{8,200... | collective-permute-start | bytes 2359304 | tf_op jit(solution)/shard_map/ppermute | solution.py:152
  61.9 0.0 collective-permute-start.6
  61.9 5.5 %all-to-all-done.1 = bf16[64,16,128]{2,1,0:T(8,128)(2,1)S(1)} async-done(((bf16[64,16,128]{2,1,0:T(8,128)(2,1)}), bf16[64,16,128]{2,1,0:T(8,128)(2,1)S(1)}, u32[]{:S(2)}, u32[]{:S(2)}) %all-to-all-start.1) | async-done | bytes 262176 | tf_op jit(solution)/shard_map/all_to_all | solution.py:330
  67.3 0.0 copy-start
  67.3 1.0 %copy-done = f32[256,512]{1,0:T(8,128)S(1)} copy-done((f32[256,512]{1,0:T(8,128)S(1)}, f32[256,512]{1,0:T(8,128)}, u32[]{:S(2)}) %copy-start) | copy-done | bytes 524312
  68.4 0.0 copy-start.1
  68.4 1.0 %copy-done.1 = f32[256,512]{1,0:T(8,128)S(1)} copy-done((f32[256,512]{1,0:T(8,128)S(1)}, f32[256,512]{1,0:T(8,128)}, u32[]{:S(2)}) %copy-start.1) | copy-done | bytes 524312
  69.4 1.0 %shard_map.88 = (f32[256,512]{1,0:T(8,128)}, bf16[4,256,128]{2,1,0:T(8,128)(2,1)S(1)}) custom-call(bf16[1024,128]{1,0:T(8,128)(2,1)S(1)} %bitcast.9, f32[256,512]{1,0:T(8,128)S(1)} %copy-done, f32[256,512]{1,0:T(8,128)S(1)} %copy-done.1, f32[256,1]{1,0:T(8,128)S(1)} %copy.11.skip_ref), custom_call_target="tpu_custom_call" | custom-call | flops 99999997952 | tf_op jit(solution)/shard_map/pallas_call | solution.py:334
  70.5 12.0 %all_to_all.15 = bf16[4,256,128]{2,1,0:T(8,128)(2,1)S(1)} all-to-all(bf16[4,256,128]{2,1,0:T(8,128)(2,1)S(1)} %get-tuple-element.12), channel_id=1, replica_groups=mesh['y'=4,'x'=4,'zh'=2,'core'=2,'chan'=4] {'chan'}, dimensions={0} | all-to-all | bytes 524288 | tf_op jit(solution)/shard_map/all_to_all | solution.py:344
  82.4 2.7 %collective-permute-start = (bf16[1024,128]{1,0:T(8,128)(2,1)S(1)}, bf16[1024,128]{1,0:T(8,128)(2,1)S(1)}, u32[]{:S(2)}, u32[]{:S(2)}) collective-permute-start(bf16[1024,128]{1,0:T(8,128)(2,1)S(1)} %bitcast.6), channel_id=1, source_target_pairs={{0,4},{4,0},{1,5},{5,1},{2,6},{6,2},{3,7},{7,3},{8,12},{12,8},{9,1... | collective-permute-start | bytes 786440 | tf_op jit(solution)/shard_map/ppermute | solution.py:152
  85.1 0.0 collective-permute-done.7.refs_2_
  85.1 0.0 collective-permute-done.6.refs_1_
  85.1 1.2 %collective-permute-done.theirs_ref = bf16[1024,128]{1,0:T(8,128)(2,1)S(1)} collective-permute-done((bf16[1024,128]{1,0:T(8,128)(2,1)S(1)}, bf16[1024,128]{1,0:T(8,128)(2,1)S(1)}, u32[]{:S(2)}, u32[]{:S(2)}) %collective-permute-start) | collective-permute-done | bytes 262176 | tf_op jit(solution)/shard_map/ppermute | solution.py:152
  86.3 4.9 %shard_map.90 = (bf16[128,8192]{1,0:T(8,128)(2,1)}, bf16[128,2048]{1,0:T(8,128)(2,1)S(1)}) custom-call(bf16[1024,128]{1,0:T(8,128)(2,1)S(1)} %bitcast.7, bf16[1024,128]{1,0:T(8,128)(2,1)S(1)} %collective-permute-done.theirs_ref, bf16[256,8192]{1,0:T(8,128)(2,1)} %own_ref.3, bf16[768,1024]{1,0:T(8,128)(2,1)S(1)} %shard_map.89.refs_0_, ...), custom_call_target="tpu_custom_call" | custom-call | tf_op jit(solution)/shard_map/pallas_call | solution.py:282
  91.2 0.5 collective-permute-start.8
  91.6 0.0 collective-permute-done.5.refs_1_
  91.6 0.0 collective-permute-done.4.refs_0_
  91.6 4.8 %shard_map.91 = (bf16[128,8192]{1,0:T(8,128)(2,1)}, bf16[128,2048]{1,0:T(8,128)(2,1)S(1)}) custom-call(bf16[1024,128]{1,0:T(8,128)(2,1)S(1)} %bitcast.8, bf16[1024,128]{1,0:T(8,128)(2,1)S(1)} %collective-permute-done.theirs_ref, bf16[256,8192]{1,0:T(8,128)(2,1)} %own_ref.3, ...), custom_call_target="tpu_custom_call", output_to_operand_aliasing={{0}: (5, {})} | custom-call | tf_op jit(solution)/shard_map/pallas_call | solution.py:282
  96.4 0.2 collective-permute-start.9
  96.6 0.0 collective-permute-done.8.first_ref
  96.6 1.8 %collective-permute-done.9.second_ref = bf16[128,2048]{1,0:T(8,128)(2,1)S(1)} collective-permute-done((bf16[128,2048]{1,0:T(8,128)(2,1)S(1)}, bf16[128,2048]{1,0:T(8,128)(2,1)S(1)}, u32[]{:S(2)}, u32[]{:S(2)}) %collective-permute-start.9) | collective-permute-done | bytes 524320 | tf_op jit(solution)/shard_map/ppermute | solution.py:152
  98.4 1.0 shard_map.92
Async XLA Ops:
  3.7 22.8 %copy-start.4 = (f32[256]{0:T(256)S(1)}, f32[256]{0:T(256)}, u32[]{:S(2)}) copy-start(f32[256]{0:T(256)} %param.10) | copy-start | bytes 3076
  3.7 37.3 %all-to-all-start = ((bf16[64,32,128]{2,1,0:T(8,128)(2,1)}), bf16[64,32,128]{2,1,0:T(8,128)(2,1)S(1)}, u32[]{:S(2)}, u32[]{:S(2)}) async-start(bf16[64,32,128]{2,1,0:T(8,128)(2,1)} %bitcast.11), calls=%async_computation | async-start | bytes 1048576 | tf_op jit(solution)/shard_map/all_to_all | solution.py:317
  20.6 31.4 %collective-permute-start.3 = (bf16[256,1024]{1,0:T(8,128)(2,1)S(1)}, bf16[256,1024]{1,0:T(8,128)(2,1)S(1)}, u32[]{:S(2)}, u32[]{:S(2)}) collective-permute-start(bf16[256,1024]{1,0:T(8,128)(2,1)S(1)} %constant_dynamic-slice_fusion), channel_id=1, source_target_pairs={{0,2},{4,14},{1,3},{5,15},{2,8},{6,4},{3,9},{7,5},{8,10},{12,6},{9... | collective-permute-start | bytes 1572872 | tf_op jit(solution)/shard_map/ppermute | solution.py:152
  25.1 29.9 %collective-permute-start.2 = (bf16[256,1024]{1,0:T(8,128)(2,1)S(1)}, bf16[256,1024]{1,0:T(8,128)(2,1)S(1)}, u32[]{:S(2)}, u32[]{:S(2)}) collective-permute-start(bf16[256,1024]{1,0:T(8,128)(2,1)S(1)} %constant_dynamic-slice_fusion), channel_id=1, source_target_pairs={{0,11},{4,15},{1,0},{5,4},{2,1},{6,5},{3,2},{7,6},{8,3},{12,7},{9,... | collective-permute-start | bytes 1572872 | tf_op jit(solution)/shard_map/ppermute | solution.py:152
  25.8 29.2 %collective-permute-start.1 = (bf16[256,1024]{1,0:T(8,128)(2,1)S(1)}, bf16[256,1024]{1,0:T(8,128)(2,1)S(1)}, u32[]{:S(2)}, u32[]{:S(2)}) collective-permute-start(bf16[256,1024]{1,0:T(8,128)(2,1)S(1)} %constant_dynamic-slice_fusion), channel_id=1, source_target_pairs={{0,1},{4,5},{1,2},{5,6},{2,3},{6,7},{3,8},{7,12},{8,9},{12,13},{9,... | collective-permute-start | bytes 1572872 | tf_op jit(solution)/shard_map/ppermute | solution.py:152
  41.0 0.8 copy-start.3
  41.8 13.2 %copy-start.2 = (f32[8,128]{1,0:T(8,128)S(1)}, f32[8,128]{1,0:T(8,128)}, u32[]{:S(2)}) copy-start(f32[8,128]{1,0:T(8,128)} %get-tuple-element.13.after_ref) | copy-start | bytes 12292
  47.8 19.6 %all-to-all-start.1 = ((bf16[64,16,128]{2,1,0:T(8,128)(2,1)}), bf16[64,16,128]{2,1,0:T(8,128)(2,1)S(1)}, u32[]{:S(2)}, u32[]{:S(2)}) async-start(bf16[64,16,128]{2,1,0:T(8,128)(2,1)} %bitcast.12), calls=%async_computation.1 | async-start | bytes 524288 | tf_op jit(solution)/shard_map/all_to_all | solution.py:330
  55.2 36.5 %collective-permute-start.5 = (bf16[768,1024]{1,0:T(8,128)(2,1)S(1)}, bf16[768,1024]{1,0:T(8,128)(2,1)S(1)}, u32[]{:S(2)}, u32[]{:S(2)}) collective-permute-start(bf16[768,1024]{1,0:T(8,128)(2,1)S(1)} %shard_map.89.refs_0_), channel_id=1, source_target_pairs={{0,16},{4,68},{1,17},{5,69},{2,18},{6,70},{3,19},{7,71},{8,24},{12... | collective-permute-start | bytes 4718600 | tf_op jit(solution)/shard_map/ppermute | solution.py:152
  56.6 35.0 %collective-permute-start.4 = (bf16[768,1024]{1,0:T(8,128)(2,1)S(1)}, bf16[768,1024]{1,0:T(8,128)(2,1)}, u32[]{:S(2)}, u32[]{:S(2)}) collective-permute-start(bf16[768,1024]{1,0:T(8,128)(2,1)S(1)} %shard_map.89.refs_0_), channel_id=1, source_target_pairs={{0,48},{4,196},{1,49},{5,197},{2,50},{6,198},{3,51},{7,199},{8,56}... | collective-permute-start | bytes 4718600 | tf_op jit(solution)/shard_map/ppermute | solution.py:152
  59.4 25.7 %collective-permute-start.7 = (bf16[384,1024]{1,0:T(8,128)(2,1)}, bf16[384,1024]{1,0:T(8,128)(2,1)}, u32[]{:S(2)}, u32[]{:S(2)}) collective-permute-start(bf16[384,1024]{1,0:T(8,128)(2,1)} %get-tuple-element.18), channel_id=1, source_target_pairs={{0,192},{4,52},{1,193},{5,53},{2,194},{6,54},{3,195},{7,55},{8,200... | collective-permute-start | bytes 2359304 | tf_op jit(solution)/shard_map/ppermute | solution.py:152
  61.9 23.3 %collective-permute-start.6 = (bf16[384,1024]{1,0:T(8,128)(2,1)}, bf16[384,1024]{1,0:T(8,128)(2,1)}, u32[]{:S(2)}, u32[]{:S(2)}) collective-permute-start(bf16[384,1024]{1,0:T(8,128)(2,1)} %get-tuple-element.19), channel_id=1, source_target_pairs={{0,64},{4,20},{1,65},{5,21},{2,66},{6,22},{3,67},{7,23},{8,72},{12... | collective-permute-start | bytes 2359304 | tf_op jit(solution)/shard_map/ppermute | solution.py:152
  67.3 1.0 %copy-start = (f32[256,512]{1,0:T(8,128)S(1)}, f32[256,512]{1,0:T(8,128)}, u32[]{:S(2)}) copy-start(f32[256,512]{1,0:T(8,128)} %signal_ref.3) | copy-start | bytes 1572868
  68.4 1.0 %copy-start.1 = (f32[256,512]{1,0:T(8,128)S(1)}, f32[256,512]{1,0:T(8,128)}, u32[]{:S(2)}) copy-start(f32[256,512]{1,0:T(8,128)} %gate_ref.1) | copy-start | bytes 1572868
  82.4 3.9 %collective-permute-start = (bf16[1024,128]{1,0:T(8,128)(2,1)S(1)}, bf16[1024,128]{1,0:T(8,128)(2,1)S(1)}, u32[]{:S(2)}, u32[]{:S(2)}) collective-permute-start(bf16[1024,128]{1,0:T(8,128)(2,1)S(1)} %bitcast.6), channel_id=1, source_target_pairs={{0,4},{4,0},{1,5},{5,1},{2,6},{6,2},{3,7},{7,3},{8,12},{12,8},{9,1... | collective-permute-start | bytes 786440 | tf_op jit(solution)/shard_map/ppermute | solution.py:152
  91.2 5.5 %collective-permute-start.8 = (bf16[128,2048]{1,0:T(8,128)(2,1)S(1)}, bf16[128,2048]{1,0:T(8,128)(2,1)S(1)}, u32[]{:S(2)}, u32[]{:S(2)}) collective-permute-start(bf16[128,2048]{1,0:T(8,128)(2,1)S(1)} %get-tuple-element.16), channel_id=1, source_target_pairs={{0,4},{4,0},{1,5},{5,1},{2,6},{6,2},{3,7},{7,3},{8,12},{12,8},{9,1... | collective-permute-start | bytes 1572872 | tf_op jit(solution)/shard_map/ppermute | solution.py:152
  96.4 2.0 %collective-permute-start.9 = (bf16[128,2048]{1,0:T(8,128)(2,1)S(1)}, bf16[128,2048]{1,0:T(8,128)(2,1)S(1)}, u32[]{:S(2)}, u32[]{:S(2)}) collective-permute-start(bf16[128,2048]{1,0:T(8,128)(2,1)S(1)} %get-tuple-element.17), channel_id=1, source_target_pairs={{0,4},{4,0},{1,5},{5,1},{2,6},{6,2},{3,7},{7,3},{8,12},{12,8},{9,1... | collective-permute-start | bytes 1572872 | tf_op jit(solution)/shard_map/ppermute | solution.py:152

commit v10 on v9

--- a/solution.py
+++ b/solution.py
@@ -207,18 +207,8 @@
     return pl.multiple_of(core * HALF + (colour(core) + index) % 4 * QUARTER, QUARTER)
 
 
-def project_kernel(quarters, mine_ref, theirs_ref, own_ref, *refs):
-    count = sum(parts for _, parts in quarters)
-    block_refs, (out_ref, for_them_ref, own, results, own_sem, out_sem) = refs[:count], refs[-6:]
-    core, chan = lax.axis_index("core"), lax.axis_index("chan")
-    loads = [
-        pltpu.make_async_copy(
-            own_ref.at[:, pl.ds(place_of(core, index), QUARTER)], own.at[order], own_sem.at[order]
-        )
-        for order, (index, _) in enumerate(quarters)
-    ]
-    for load in loads:
-        load.start()
+def transposed_columns(mine_ref, theirs_ref):
+    chan = lax.axis_index("chan")
     rows = [
         jnp.concatenate(
             [
@@ -229,21 +219,45 @@
         )
         for shift in (0, 3, 1, 2)
     ]
-    own_columns, columns = rows[0], jnp.concatenate(rows[1:], axis=1)
-    stores, part = [], 0
+    return jnp.concatenate(rows, axis=1)
+
+
+def project_kernel(quarters, given, *refs):
+    count = sum(parts for _, parts in quarters)
+    columns_refs, own_ref = refs[:given], refs[given]
+    block_refs = refs[given + 1 : given + 1 + count]
+    weights, results, load_sem, out_sem = refs[-4:]
+    out_ref, for_them_ref = refs[-6:-4] if given == 1 else refs[-7:-5]
+    core = lax.axis_index("core")
+    loads, part = [], 0
     for order, (index, parts) in enumerate(quarters):
-        place = place_of(core, index)
-        loads[order].wait()
-        total = matmul(own_columns, own[order])
-        row = 0
-        for block_ref in block_refs[part : part + parts]:
-            block = block_ref[...]
-            total += matmul(columns[:, row : row + block.shape[0]], block)
-            row += block.shape[0]
+        sources = [own_ref.at[:, pl.ds(place_of(core, index), QUARTER)]]
+        sources += block_refs[part : part + parts]
         part += parts
-        results[order] = total.astype(jnp.bfloat16)
+        group, row = [], 0
+        for which, source in enumerate(sources):
+            depth = ROWS if which == 0 else source.shape[0]
+            group.append(
+                pltpu.make_async_copy(
+                    source, weights.at[order, pl.ds(row, depth)], load_sem.at[order, which]
+                )
+            )
+            row += depth
+        for load in group:
+            load.start()
+        loads.append(group)
+    if given == 1:
+        columns = columns_refs[0][...]
+    else:
+        columns = transposed_columns(*columns_refs)
+        refs[-5][...] = columns
+    stores = []
+    for order, (index, _) in enumerate(quarters):
+        for load in loads[order]:
+            load.wait()
+        results[order] = matmul(columns, weights[order]).astype(jnp.bfloat16)
         targets = (
-            out_ref.at[:, pl.ds(place, QUARTER)],
+            out_ref.at[:, pl.ds(place_of(core, index), QUARTER)],
             for_them_ref.at[:, pl.ds(order * QUARTER, QUARTER)],
         )
         for rank, target in enumerate(targets):
@@ -279,22 +293,27 @@
 
 def projected_quarters(quarters, columns, own, blocks, filled):
     last = [] if filled is None else [filled]
+    shapes = [
+        jax.ShapeDtypeStruct((LANES, 2 * HALF), jnp.bfloat16),
+        jax.ShapeDtypeStruct((LANES, HALF // 2), jnp.bfloat16),
+    ]
+    places = [ANYWHERE, ANYWHERE]
+    if not last:
+        shapes.append(jax.ShapeDtypeStruct((2 * LANES, 4 * ROWS), jnp.bfloat16))
+        places.append(INSIDE)
     return call(
-        functools.partial(project_kernel, quarters),
-        (
-            jax.ShapeDtypeStruct((LANES, 2 * HALF), jnp.bfloat16),
-            jax.ShapeDtypeStruct((LANES, HALF // 2), jnp.bfloat16),
-        ),
+        functools.partial(project_kernel, quarters, len(columns)),
+        tuple(shapes),
         [
-            pltpu.VMEM((2, ROWS, QUARTER), jnp.bfloat16),
+            pltpu.VMEM((2, 4 * ROWS, QUARTER), jnp.bfloat16),
             pltpu.VMEM((2, 2 * LANES, QUARTER), jnp.bfloat16),
-            pltpu.SemaphoreType.DMA((2,)),
+            pltpu.SemaphoreType.DMA((2, 3)),
             pltpu.SemaphoreType.DMA((2, 2)),
         ],
         limit=LAST,
-        in_specs=[INSIDE] * 2 + [ANYWHERE] + [INSIDE] * len(blocks) + [ANYWHERE] * len(last),
-        out_specs=(ANYWHERE, ANYWHERE),
-        input_output_aliases={3 + len(blocks): 0} if last else {},
+        in_specs=[INSIDE] * len(columns) + [ANYWHERE] * (1 + len(blocks) + len(last)),
+        out_specs=tuple(places),
+        input_output_aliases={len(columns) + 1 + len(blocks): 0} if last else {},
     )(*columns, own, *blocks, *last)
 
 
@@ -345,8 +364,12 @@
     mine = mine.reshape(4 * channels, LANES)
     columns = (mine, swapped(mine))
     lower, across, upper = blocks[1], blocks[2:4], blocks[4]
-    filled, first = projected_quarters(HALVES[0], columns, out_weight, [blocks[0], *across], None)
-    filled, second = projected_quarters(HALVES[1], columns, out_weight, [lower, upper], filled)
+    filled, first, turned = projected_quarters(
+        HALVES[0], columns, out_weight, [blocks[0], *across], None
+    )
+    filled, second = projected_quarters(
+        HALVES[1], [turned], out_weight, [lower, upper], filled
+    )
     projected = call(
         fill_kernel,
         jax.ShapeDtypeStruct(filled.shape, filled.dtype),

time: 100 us -> 99.3 us (level)
  Pallas kernels: 20.8 us -> 17.7 us
  starting transfers between devices: 34.7 us -> 36.8 us
    pallas_call x2, Pallas kernels: 9.62 us -> 6.56 us  [projected_quarters(): call(functools.partial(project_kernel, quarters, len(columns)), tuple(sha...]
    ppermute x10, starting transfers between devices: 14.8 us -> 16.9 us  [moved(): return lax.ppermute(array, (*AXES, 'chan'), device_pairs(move))]
  transfers between devices with their start and end apart: 12 -> 12, of which waited for: 5 -> 5; matrix products, arithmetic and copies ran while one was open for 2% -> 3% of each run, Pallas kernels for 17% -> 14%
where the time goes in v10:
time: 99.3 us; the launch traced here: 98.7 us
  starting transfers between devices  36.8 us (37%)
  waiting for transfers between devices  26 us (26%)
  Pallas kernels  17.7 us (18%)
  blocking collectives  12 us (12%)
  local copies, waits for them, and re-layouts  5.36 us (5%)
    ppermute x10, starting transfers between devices, moved(): return lax.ppermute(array, (*AXES, 'chan'), device_pairs(move))  16.9 us
    all_to_all x1, starting transfers between devices, body(): lax.all_to_all(packed.reshape(SEQ_DEVICES, 32, LANES), AXES, split_axis=0...  15.7 us
    all_to_all x1, waiting for transfers between devices, body(): lax.all_to_all(packed.reshape(SEQ_DEVICES, 32, LANES), AXES, split_axis=0...  14.4 us
    all_to_all x1, blocking collectives, body(): lax.all_to_all(rounded, 'chan', split_axis=0, concat_axis=0, tiled=True)  12 us
    pallas_call x2, Pallas kernels, projected_quarters(): call(functools.partial(project_kernel, quarters, len(columns)), tuple(sha...  6.56 us
    ppermute x10, waiting for transfers between devices, moved(): return lax.ppermute(array, (*AXES, 'chan'), device_pairs(move))  6.09 us
    pallas_call x1, Pallas kernels, body(): call(convolve_kernel, jax.ShapeDtypeStruct((SEQ_DEVICES * 16, LANES), jnp...  5.92 us
    all_to_all x1, waiting for transfers between devices, body(): lax.all_to_all(convolved.reshape(SEQ_DEVICES, 16, LANES), AXES, split_axi...  5.55 us
  transfers between devices with their start and end apart: 12, of which 5 were waited for; matrix products, arithmetic and copies ran while one was open for 3% of the time, Pallas kernels for 14%

profile of v10, /device:TPU:1, one launch (start us, length us, event | category | flops | bytes accessed | tf_op | source)
XLA Modules:
  0.0 98.7 jit_solution(12770742839636004557)
XLA Ops:
  0.6 3.1 %shard_map.86 = (bf16[2048,128]{1,0:T(8,128)(2,1)}, f32[8,128]{1,0:T(8,128)}) custom-call(f32[256,512]{1,0:T(8,128)} %signal_ref.3, f32[256,512]{1,0:T(8,128)} %filter_ref.1), custom_call_target="tpu_custom_call" | custom-call | flops 10000000000 | tf_op jit(solution)/shard_map/pallas_call | solution.py:327
  3.7 0.0 copy-start.4
  3.7 15.7 %all-to-all-start = ((bf16[64,32,128]{2,1,0:T(8,128)(2,1)}), bf16[64,32,128]{2,1,0:T(8,128)(2,1)S(1)}, u32[]{:S(2)}, u32[]{:S(2)}) async-start(bf16[64,32,128]{2,1,0:T(8,128)(2,1)} %bitcast.10), calls=%async_computation | async-start | bytes 1048576 | tf_op jit(solution)/shard_map/all_to_all | solution.py:336
  19.5 1.1 %constant_dynamic-slice_fusion = bf16[256,1024]{1,0:T(8,128)(2,1)S(1)} fusion(bf16[256,8192]{1,0:T(8,128)(2,1)} %refs_1_.1, s32[]{:T(128)S(6)} %select_n.15), kind=kLoop, calls=%fused_computation | loop fusion | bytes 1048580 | tf_op jit(solution)/shard_map/dynamic_slice | solution.py:179
  20.6 4.5 %collective-permute-start.3 = (bf16[256,1024]{1,0:T(8,128)(2,1)S(1)}, bf16[256,1024]{1,0:T(8,128)(2,1)S(1)}, u32[]{:S(2)}, u32[]{:S(2)}) collective-permute-start(bf16[256,1024]{1,0:T(8,128)(2,1)S(1)} %constant_dynamic-slice_fusion), channel_id=1, source_target_pairs={{0,2},{4,14},{1,3},{5,15},{2,8},{6,4},{3,9},{7,5},{8,10},{12,6},{9... | collective-permute-start | bytes 1572872 | tf_op jit(solution)/shard_map/ppermute | solution.py:152
  25.1 0.7 collective-permute-start.2
  25.8 0.7 collective-permute-start.1
  26.5 0.0 copy-done.4
  26.5 0.1 copy.11.skip_ref
  26.7 14.4 %all-to-all-done = bf16[64,32,128]{2,1,0:T(8,128)(2,1)S(1)} async-done(((bf16[64,32,128]{2,1,0:T(8,128)(2,1)}), bf16[64,32,128]{2,1,0:T(8,128)(2,1)S(1)}, u32[]{:S(2)}, u32[]{:S(2)}) %all-to-all-start) | async-done | bytes 524320 | tf_op jit(solution)/shard_map/all_to_all | solution.py:336
  41.0 0.0 copy-start.3
  41.0 0.8 copy-done.3
  41.8 0.0 copy-start.2
  41.8 5.9 %shard_map.87 = bf16[1024,128]{1,0:T(8,128)(2,1)} custom-call(bf16[2048,128]{1,0:T(8,128)(2,1)} %bitcast.9, bf16[1536,256]{1,0:T(8,128)(2,1)} %constant.41.clone.factors_ref, f32[512,128]{1,0:T(8,128)} %constant.42.clone.turn_ref), custom_call_target="tpu_custom_call" | custom-call | flops 99999997952 | tf_op jit(solution)/shard_map/pallas_call | solution.py:339
  47.8 4.2 %all-to-all-start.1 = ((bf16[64,16,128]{2,1,0:T(8,128)(2,1)}), bf16[64,16,128]{2,1,0:T(8,128)(2,1)S(1)}, u32[]{:S(2)}, u32[]{:S(2)}) async-start(bf16[64,16,128]{2,1,0:T(8,128)(2,1)} %bitcast.11), calls=%async_computation.1 | async-start | bytes 524288 | tf_op jit(solution)/shard_map/all_to_all | solution.py:349
  51.9 0.0 collective-permute-done.3.far_ref
  51.9 3.1 %collective-permute-done.2.above_ref = bf16[256,1024]{1,0:T(8,128)(2,1)S(1)} collective-permute-done((bf16[256,1024]{1,0:T(8,128)(2,1)S(1)}, bf16[256,1024]{1,0:T(8,128)(2,1)S(1)}, u32[]{:S(2)}, u32[]{:S(2)}) %collective-permute-start.2) | collective-permute-done | bytes 524320 | tf_op jit(solution)/shard_map/ppermute | solution.py:152
  55.0 0.0 collective-permute-done.1.below_ref
  55.0 0.0 copy-done.2
  55.0 0.1 shard_map.89.refs_3_
  55.2 2.9 %collective-permute-start.6 = (bf16[768,1024]{1,0:T(8,128)(2,1)S(1)}, bf16[768,1024]{1,0:T(8,128)(2,1)S(1)}, u32[]{:S(2)}, u32[]{:S(2)}) collective-permute-start(bf16[768,1024]{1,0:T(8,128)(2,1)S(1)} %shard_map.89.refs_3_), channel_id=1, source_target_pairs={{0,48},{4,196},{1,49},{5,197},{2,50},{6,198},{3,51},{7,199},{8,56}... | collective-permute-start | bytes 4718600 | tf_op jit(solution)/shard_map/ppermute | solution.py:152
  58.1 0.0 collective-permute-start.7
  58.1 1.3 %fusion = (bf16[384,1024]{1,0:T(8,128)(2,1)}, bf16[384,1024]{1,0:T(8,128)(2,1)}) fusion(bf16[768,1024]{1,0:T(8,128)(2,1)S(1)} %shard_map.89.refs_3_), kind=kLoop, calls=%fused_computation.1 | loop fusion | bytes 3145728 | tf_op jit(solution)/shard_map/slice | solution.py:196
  59.3 2.5 %collective-permute-start.5 = (bf16[384,1024]{1,0:T(8,128)(2,1)}, bf16[384,1024]{1,0:T(8,128)(2,1)}, u32[]{:S(2)}, u32[]{:S(2)}) collective-permute-start(bf16[384,1024]{1,0:T(8,128)(2,1)} %get-tuple-element.20), channel_id=1, source_target_pairs={{0,192},{4,52},{1,193},{5,53},{2,194},{6,54},{3,195},{7,55},{8,200... | collective-permute-start | bytes 2359304 | tf_op jit(solution)/shard_map/ppermute | solution.py:152
  61.8 0.0 collective-permute-start.4
  61.8 5.5 %all-to-all-done.1 = bf16[64,16,128]{2,1,0:T(8,128)(2,1)S(1)} async-done(((bf16[64,16,128]{2,1,0:T(8,128)(2,1)}), bf16[64,16,128]{2,1,0:T(8,128)(2,1)S(1)}, u32[]{:S(2)}, u32[]{:S(2)}) %all-to-all-start.1) | async-done | bytes 262176 | tf_op jit(solution)/shard_map/all_to_all | solution.py:349
  67.3 0.0 copy-start
  67.3 1.0 %copy-done = f32[256,512]{1,0:T(8,128)S(1)} copy-done((f32[256,512]{1,0:T(8,128)S(1)}, f32[256,512]{1,0:T(8,128)}, u32[]{:S(2)}) %copy-start) | copy-done | bytes 524312
  68.4 0.0 copy-start.1
  68.4 1.0 %copy-done.1 = f32[256,512]{1,0:T(8,128)S(1)} copy-done((f32[256,512]{1,0:T(8,128)S(1)}, f32[256,512]{1,0:T(8,128)}, u32[]{:S(2)}) %copy-start.1) | copy-done | bytes 524312
  69.4 1.0 %shard_map.88 = (f32[256,512]{1,0:T(8,128)}, bf16[4,256,128]{2,1,0:T(8,128)(2,1)S(1)}) custom-call(bf16[1024,128]{1,0:T(8,128)(2,1)S(1)} %bitcast.8, f32[256,512]{1,0:T(8,128)S(1)} %copy-done, f32[256,512]{1,0:T(8,128)S(1)} %copy-done.1, f32[256,1]{1,0:T(8,128)S(1)} %copy.11.skip_ref), custom_call_target="tpu_custom_call" | custom-call | flops 99999997952 | tf_op jit(solution)/shard_map/pallas_call | solution.py:353
  70.5 12.0 %all_to_all.15 = bf16[4,256,128]{2,1,0:T(8,128)(2,1)S(1)} all-to-all(bf16[4,256,128]{2,1,0:T(8,128)(2,1)S(1)} %get-tuple-element.13), channel_id=1, replica_groups=mesh['y'=4,'x'=4,'zh'=2,'core'=2,'chan'=4] {'chan'}, dimensions={0} | all-to-all | bytes 524288 | tf_op jit(solution)/shard_map/all_to_all | solution.py:363
  82.4 2.7 %collective-permute-start = (bf16[1024,128]{1,0:T(8,128)(2,1)S(1)}, bf16[1024,128]{1,0:T(8,128)(2,1)S(1)}, u32[]{:S(2)}, u32[]{:S(2)}) collective-permute-start(bf16[1024,128]{1,0:T(8,128)(2,1)S(1)} %bitcast.6), channel_id=1, source_target_pairs={{0,4},{4,0},{1,5},{5,1},{2,6},{6,2},{3,7},{7,3},{8,12},{12,8},{9,1... | collective-permute-start | bytes 786440 | tf_op jit(solution)/shard_map/ppermute | solution.py:152
  85.1 0.0 collective-permute-done.5.refs_5_
  85.1 0.0 collective-permute-done.4.refs_4_
  85.1 1.2 %collective-permute-done.refs_1_ = bf16[1024,128]{1,0:T(8,128)(2,1)S(1)} collective-permute-done((bf16[1024,128]{1,0:T(8,128)(2,1)S(1)}, bf16[1024,128]{1,0:T(8,128)(2,1)S(1)}, u32[]{:S(2)}, u32[]{:S(2)}) %collective-permute-start) | collective-permute-done | bytes 262176 | tf_op jit(solution)/shard_map/ppermute | solution.py:152
  86.3 3.3 %shard_map.90 = (bf16[128,8192]{1,0:T(8,128)(2,1)}, bf16[128,2048]{1,0:T(8,128)(2,1)S(1)}, bf16[256,1024]{1,0:T(8,128)(2,1)S(1)}) custom-call(bf16[1024,128]{1,0:T(8,128)(2,1)S(1)} %bitcast.7, bf16[1024,128]{1,0:T(8,128)(2,1)S(1)} %collective-permute-done.refs_1_, bf16[256,8192]{1,0:T(8,128)(2,1)} %refs_1_.1, bf16[768,1024]{1,0:T(8,128)(2,1)S(1)} %shard_map.89.refs_3_, ...), custom_call_target="tpu_custom_call" | custom-call | tf_op jit(solution)/shard_map/pallas_call | solution.py:304
  89.6 2.7 %collective-permute-start.8 = (bf16[128,2048]{1,0:T(8,128)(2,1)S(1)}, bf16[128,2048]{1,0:T(8,128)(2,1)S(1)}, u32[]{:S(2)}, u32[]{:S(2)}) collective-permute-start(bf16[128,2048]{1,0:T(8,128)(2,1)S(1)} %get-tuple-element.18), channel_id=1, source_target_pairs={{0,4},{4,0},{1,5},{5,1},{2,6},{6,2},{3,7},{7,3},{8,12},{12,8},{9,1... | collective-permute-start | bytes 1572872 | tf_op jit(solution)/shard_map/ppermute | solution.py:152
  92.3 0.0 collective-permute-done.6.refs_2_
  92.3 0.0 collective-permute-done.7.refs_3_
  92.3 3.3 %shard_map.91 = (bf16[128,8192]{1,0:T(8,128)(2,1)}, bf16[128,2048]{1,0:T(8,128)(2,1)S(1)}) custom-call(bf16[256,1024]{1,0:T(8,128)(2,1)S(1)} %get-tuple-element.15.refs_0_, bf16[256,8192]{1,0:T(8,128)(2,1)} %refs_1_.1, bf16[768,1024]{1,0:T(8,128)(2,1)S(1)} %collective-permute-done.6.refs_2_, ...), custom_call_target="tpu_custom_call", output_to_operand_aliasing={{0}: (4, {})} | custom-call | tf_op jit(solution)/shard_map/pallas_call | solution.py:304
  95.6 0.1 collective-permute-start.9
  95.7 0.0 collective-permute-done.8.first_ref
  95.7 1.8 %collective-permute-done.9.second_ref = bf16[128,2048]{1,0:T(8,128)(2,1)S(1)} collective-permute-done((bf16[128,2048]{1,0:T(8,128)(2,1)S(1)}, bf16[128,2048]{1,0:T(8,128)(2,1)S(1)}, u32[]{:S(2)}, u32[]{:S(2)}) %collective-permute-start.9) | collective-permute-done | bytes 524320 | tf_op jit(solution)/shard_map/ppermute | solution.py:152
  97.6 1.0 %shard_map.92 = bf16[128,8192]{1,0:T(8,128)(2,1)} custom-call(bf16[128,8192]{1,0:T(8,128)(2,1)} %get-tuple-element.17.filled_ref, bf16[128,2048]{1,0:T(8,128)(2,1)S(1)} %collective-permute-done.8.first_ref, bf16[128,2048]{1,0:T(8,128)(2,1)S(1)} %collective-permute-done.9.second_ref), custom_call_target="tpu_custom_call", output_to_operand_aliasing={{}: (0, {})} | custom-call | tf_op jit(solution)/shard_map/pallas_call | solution.py:373
Async XLA Ops:
  3.7 22.8 %copy-start.4 = (f32[256]{0:T(256)S(1)}, f32[256]{0:T(256)}, u32[]{:S(2)}) copy-start(f32[256]{0:T(256)} %param.10) | copy-start | bytes 3076
  3.7 37.3 %all-to-all-start = ((bf16[64,32,128]{2,1,0:T(8,128)(2,1)}), bf16[64,32,128]{2,1,0:T(8,128)(2,1)S(1)}, u32[]{:S(2)}, u32[]{:S(2)}) async-start(bf16[64,32,128]{2,1,0:T(8,128)(2,1)} %bitcast.10), calls=%async_computation | async-start | bytes 1048576 | tf_op jit(solution)/shard_map/all_to_all | solution.py:336
  20.6 31.4 %collective-permute-start.3 = (bf16[256,1024]{1,0:T(8,128)(2,1)S(1)}, bf16[256,1024]{1,0:T(8,128)(2,1)S(1)}, u32[]{:S(2)}, u32[]{:S(2)}) collective-permute-start(bf16[256,1024]{1,0:T(8,128)(2,1)S(1)} %constant_dynamic-slice_fusion), channel_id=1, source_target_pairs={{0,2},{4,14},{1,3},{5,15},{2,8},{6,4},{3,9},{7,5},{8,10},{12,6},{9... | collective-permute-start | bytes 1572872 | tf_op jit(solution)/shard_map/ppermute | solution.py:152
  25.1 29.9 %collective-permute-start.2 = (bf16[256,1024]{1,0:T(8,128)(2,1)S(1)}, bf16[256,1024]{1,0:T(8,128)(2,1)S(1)}, u32[]{:S(2)}, u32[]{:S(2)}) collective-permute-start(bf16[256,1024]{1,0:T(8,128)(2,1)S(1)} %constant_dynamic-slice_fusion), channel_id=1, source_target_pairs={{0,11},{4,15},{1,0},{5,4},{2,1},{6,5},{3,2},{7,6},{8,3},{12,7},{9,... | collective-permute-start | bytes 1572872 | tf_op jit(solution)/shard_map/ppermute | solution.py:152
  25.8 29.2 %collective-permute-start.1 = (bf16[256,1024]{1,0:T(8,128)(2,1)S(1)}, bf16[256,1024]{1,0:T(8,128)(2,1)S(1)}, u32[]{:S(2)}, u32[]{:S(2)}) collective-permute-start(bf16[256,1024]{1,0:T(8,128)(2,1)S(1)} %constant_dynamic-slice_fusion), channel_id=1, source_target_pairs={{0,1},{4,5},{1,2},{5,6},{2,3},{6,7},{3,8},{7,12},{8,9},{12,13},{9,... | collective-permute-start | bytes 1572872 | tf_op jit(solution)/shard_map/ppermute | solution.py:152
  41.0 0.8 copy-start.3
  41.8 13.2 %copy-start.2 = (f32[8,128]{1,0:T(8,128)S(1)}, f32[8,128]{1,0:T(8,128)}, u32[]{:S(2)}) copy-start(f32[8,128]{1,0:T(8,128)} %get-tuple-element.14.after_ref) | copy-start | bytes 12292
  47.8 19.6 %all-to-all-start.1 = ((bf16[64,16,128]{2,1,0:T(8,128)(2,1)}), bf16[64,16,128]{2,1,0:T(8,128)(2,1)S(1)}, u32[]{:S(2)}, u32[]{:S(2)}) async-start(bf16[64,16,128]{2,1,0:T(8,128)(2,1)} %bitcast.11), calls=%async_computation.1 | async-start | bytes 524288 | tf_op jit(solution)/shard_map/all_to_all | solution.py:349
  55.2 37.1 %collective-permute-start.6 = (bf16[768,1024]{1,0:T(8,128)(2,1)S(1)}, bf16[768,1024]{1,0:T(8,128)(2,1)S(1)}, u32[]{:S(2)}, u32[]{:S(2)}) collective-permute-start(bf16[768,1024]{1,0:T(8,128)(2,1)S(1)} %shard_map.89.refs_3_), channel_id=1, source_target_pairs={{0,48},{4,196},{1,49},{5,197},{2,50},{6,198},{3,51},{7,199},{8,56}... | collective-permute-start | bytes 4718600 | tf_op jit(solution)/shard_map/ppermute | solution.py:152
  58.1 34.2 %collective-permute-start.7 = (bf16[768,1024]{1,0:T(8,128)(2,1)S(1)}, bf16[768,1024]{1,0:T(8,128)(2,1)}, u32[]{:S(2)}, u32[]{:S(2)}) collective-permute-start(bf16[768,1024]{1,0:T(8,128)(2,1)S(1)} %shard_map.89.refs_3_), channel_id=1, source_target_pairs={{0,16},{4,68},{1,17},{5,69},{2,18},{6,70},{3,19},{7,71},{8,24},{12... | collective-permute-start | bytes 4718600 | tf_op jit(solution)/shard_map/ppermute | solution.py:152
  59.3 25.8 %collective-permute-start.5 = (bf16[384,1024]{1,0:T(8,128)(2,1)}, bf16[384,1024]{1,0:T(8,128)(2,1)}, u32[]{:S(2)}, u32[]{:S(2)}) collective-permute-start(bf16[384,1024]{1,0:T(8,128)(2,1)} %get-tuple-element.20), channel_id=1, source_target_pairs={{0,192},{4,52},{1,193},{5,53},{2,194},{6,54},{3,195},{7,55},{8,200... | collective-permute-start | bytes 2359304 | tf_op jit(solution)/shard_map/ppermute | solution.py:152
  61.8 23.3 %collective-permute-start.4 = (bf16[384,1024]{1,0:T(8,128)(2,1)}, bf16[384,1024]{1,0:T(8,128)(2,1)}, u32[]{:S(2)}, u32[]{:S(2)}) collective-permute-start(bf16[384,1024]{1,0:T(8,128)(2,1)} %get-tuple-element.21), channel_id=1, source_target_pairs={{0,64},{4,20},{1,65},{5,21},{2,66},{6,22},{3,67},{7,23},{8,72},{12... | collective-permute-start | bytes 2359304 | tf_op jit(solution)/shard_map/ppermute | solution.py:152
  67.3 1.0 %copy-start = (f32[256,512]{1,0:T(8,128)S(1)}, f32[256,512]{1,0:T(8,128)}, u32[]{:S(2)}) copy-start(f32[256,512]{1,0:T(8,128)} %signal_ref.3) | copy-start | bytes 1572868
  68.4 1.0 %copy-start.1 = (f32[256,512]{1,0:T(8,128)S(1)}, f32[256,512]{1,0:T(8,128)}, u32[]{:S(2)}) copy-start(f32[256,512]{1,0:T(8,128)} %gate_ref.1) | copy-start | bytes 1572868
  82.4 3.9 %collective-permute-start = (bf16[1024,128]{1,0:T(8,128)(2,1)S(1)}, bf16[1024,128]{1,0:T(8,128)(2,1)S(1)}, u32[]{:S(2)}, u32[]{:S(2)}) collective-permute-start(bf16[1024,128]{1,0:T(8,128)(2,1)S(1)} %bitcast.6), channel_id=1, source_target_pairs={{0,4},{4,0},{1,5},{5,1},{2,6},{6,2},{3,7},{7,3},{8,12},{12,8},{9,1... | collective-permute-start | bytes 786440 | tf_op jit(solution)/shard_map/ppermute | solution.py:152
  89.6 6.1 %collective-permute-start.8 = (bf16[128,2048]{1,0:T(8,128)(2,1)S(1)}, bf16[128,2048]{1,0:T(8,128)(2,1)S(1)}, u32[]{:S(2)}, u32[]{:S(2)}) collective-permute-start(bf16[128,2048]{1,0:T(8,128)(2,1)S(1)} %get-tuple-element.18), channel_id=1, source_target_pairs={{0,4},{4,0},{1,5},{5,1},{2,6},{6,2},{3,7},{7,3},{8,12},{12,8},{9,1... | collective-permute-start | bytes 1572872 | tf_op jit(solution)/shard_map/ppermute | solution.py:152
  95.6 2.0 %collective-permute-start.9 = (bf16[128,2048]{1,0:T(8,128)(2,1)S(1)}, bf16[128,2048]{1,0:T(8,128)(2,1)S(1)}, u32[]{:S(2)}, u32[]{:S(2)}) collective-permute-start(bf16[128,2048]{1,0:T(8,128)(2,1)S(1)} %get-tuple-element.19), channel_id=1, source_target_pairs={{0,4},{4,0},{1,5},{5,1},{2,6},{6,2},{3,7},{7,3},{8,12},{12,8},{9,1... | collective-permute-start | bytes 1572872 | tf_op jit(solution)/shard_map/ppermute | solution.py:152

commit v11 on v10

--- a/solution.py
+++ b/solution.py
@@ -179,7 +179,7 @@
     mine = lax.dynamic_slice_in_dim(out_weight, start, QUARTER, 1)
     below = moved(mine, lambda y, x, z, c: (y, x, z + 1, c))
     above = moved(mine, lambda y, x, z, c: (y, x, z - 1, c))
-    far = moved(mine, lambda y, x, z, c: (y, x, z + 2 - 4 * c, c))
+    far = moved(above, lambda y, x, z, c: (y, x, z - 1, c))
     return below, above, far
 
 

time: 99.3 us -> 108 us (1.088)
  starting transfers between devices: 36.8 us -> 44.6 us
  waiting for transfers between devices: 26 us -> 28.5 us
  blocking collectives: 12 us -> 10.1 us
    ppermute x10, waiting for transfers between devices: 6.09 us -> 21.4 us  [moved(): return lax.ppermute(array, (*AXES, 'chan'), device_pairs(move))]
    all_to_all x1, waiting for transfers between devices: 14.4 us -> 0.01 us  [body(): lax.all_to_all(packed.reshape(SEQ_DEVICES, 32, LANES), AXES, split_axis=0...]
    all_to_all x1, starting transfers between devices: 4.18 us -> 13.1 us  [body(): lax.all_to_all(convolved.reshape(SEQ_DEVICES, 16, LANES), AXES, split_axi...]
    all_to_all x1, blocking collectives: 12 us -> 10.1 us  [body(): lax.all_to_all(rounded, 'chan', split_axis=0, concat_axis=0, tiled=True)]
    all_to_all x1, waiting for transfers between devices: 5.55 us -> 7.09 us  [body(): lax.all_to_all(convolved.reshape(SEQ_DEVICES, 16, LANES), AXES, split_axi...]
    ppermute x10, starting transfers between devices: 16.9 us -> 15.7 us  [moved(): return lax.ppermute(array, (*AXES, 'chan'), device_pairs(move))]
  transfers between devices with their start and end apart: 12 -> 12, of which waited for: 5 -> 4; matrix products, arithmetic and copies ran while one was open for 3% -> 2% of each run, Pallas kernels for 14% -> 13%
where the time goes in v11:
time: 108 us; the launch traced here: 107 us
  starting transfers between devices  44.6 us (41%)
  waiting for transfers between devices  28.5 us (26%)
  Pallas kernels  17.7 us (16%)
  blocking collectives  10.1 us (9%)
  local copies, waits for them, and re-layouts  5.36 us (5%)
    ppermute x10, waiting for transfers between devices, moved(): return lax.ppermute(array, (*AXES, 'chan'), device_pairs(move))  21.4 us
    all_to_all x1, starting transfers between devices, body(): lax.all_to_all(packed.reshape(SEQ_DEVICES, 32, LANES), AXES, split_axis=0...  15.7 us
    ppermute x10, starting transfers between devices, moved(): return lax.ppermute(array, (*AXES, 'chan'), device_pairs(move))  15.7 us
    all_to_all x1, starting transfers between devices, body(): lax.all_to_all(convolved.reshape(SEQ_DEVICES, 16, LANES), AXES, split_axi...  13.1 us
    all_to_all x1, blocking collectives, body(): lax.all_to_all(rounded, 'chan', split_axis=0, concat_axis=0, tiled=True)  10.1 us
    all_to_all x1, waiting for transfers between devices, body(): lax.all_to_all(convolved.reshape(SEQ_DEVICES, 16, LANES), AXES, split_axi...  7.09 us
    pallas_call x2, Pallas kernels, projected_quarters(): call(functools.partial(project_kernel, quarters, len(columns)), tuple(sha...  6.55 us
    pallas_call x1, Pallas kernels, body(): call(convolve_kernel, jax.ShapeDtypeStruct((SEQ_DEVICES * 16, LANES), jnp...  5.92 us
  transfers between devices with their start and end apart: 12, of which 4 were waited for; matrix products, arithmetic and copies ran while one was open for 2% of the time, Pallas kernels for 13%

profile of v11, /device:TPU:1, one launch (start us, length us, event | category | flops | bytes accessed | tf_op | source)
XLA Modules:
  0.0 107.1 jit_solution(11344925388713103845)
XLA Ops:
  0.6 3.1 %shard_map.86 = (bf16[2048,128]{1,0:T(8,128)(2,1)}, f32[8,128]{1,0:T(8,128)}) custom-call(f32[256,512]{1,0:T(8,128)} %signal_ref.3, f32[256,512]{1,0:T(8,128)} %filter_ref.1), custom_call_target="tpu_custom_call" | custom-call | flops 10000000000 | tf_op jit(solution)/shard_map/pallas_call | solution.py:327
  3.7 0.0 copy-start.4
  3.7 15.7 %all-to-all-start = ((bf16[64,32,128]{2,1,0:T(8,128)(2,1)}), bf16[64,32,128]{2,1,0:T(8,128)(2,1)S(1)}, u32[]{:S(2)}, u32[]{:S(2)}) async-start(bf16[64,32,128]{2,1,0:T(8,128)(2,1)} %bitcast.10), calls=%async_computation | async-start | bytes 1048576 | tf_op jit(solution)/shard_map/all_to_all | solution.py:336
  19.5 1.1 %constant_dynamic-slice_fusion = bf16[256,1024]{1,0:T(8,128)(2,1)S(1)} fusion(bf16[256,8192]{1,0:T(8,128)(2,1)} %refs_1_.1, s32[]{:T(128)S(6)} %select_n.15), kind=kLoop, calls=%fused_computation | loop fusion | bytes 1048580 | tf_op jit(solution)/shard_map/dynamic_slice | solution.py:179
  20.6 4.0 %collective-permute-start.2 = (bf16[256,1024]{1,0:T(8,128)(2,1)S(1)}, bf16[256,1024]{1,0:T(8,128)(2,1)S(1)}, u32[]{:S(2)}, u32[]{:S(2)}) collective-permute-start(bf16[256,1024]{1,0:T(8,128)(2,1)S(1)} %constant_dynamic-slice_fusion), channel_id=1, source_target_pairs={{0,11},{4,15},{1,0},{5,4},{2,1},{6,5},{3,2},{7,6},{8,3},{12,7},{9,... | collective-permute-start | bytes 1572872 | tf_op jit(solution)/shard_map/ppermute | solution.py:152
  24.6 0.0 collective-permute-start.1
  24.6 0.0 copy-done.4
  24.6 0.1 copy.11.skip_ref
  24.8 18.6 %collective-permute-done.2.above_ref = bf16[256,1024]{1,0:T(8,128)(2,1)S(1)} collective-permute-done((bf16[256,1024]{1,0:T(8,128)(2,1)S(1)}, bf16[256,1024]{1,0:T(8,128)(2,1)S(1)}, u32[]{:S(2)}, u32[]{:S(2)}) %collective-permute-start.2) | collective-permute-done | bytes 524320 | tf_op jit(solution)/shard_map/ppermute | solution.py:152
  43.4 2.7 %collective-permute-start.3 = (bf16[256,1024]{1,0:T(8,128)(2,1)S(1)}, bf16[256,1024]{1,0:T(8,128)(2,1)S(1)}, u32[]{:S(2)}, u32[]{:S(2)}) collective-permute-start(bf16[256,1024]{1,0:T(8,128)(2,1)S(1)} %collective-permute-done.2.above_ref), channel_id=1, source_target_pairs={{0,11},{4,15},{1,0},{5,4},{2,1},{6,5},{3,2},{7,6},{8,3},{12,7},{9,... | collective-permute-start | bytes 1572872 | tf_op jit(solution)/shard_map/ppermute | solution.py:152
  46.1 0.0 all-to-all-done
  46.1 0.0 copy-start.3
  46.1 0.8 copy-done.3
  46.9 0.0 copy-start.2
  46.9 5.9 %shard_map.87 = bf16[1024,128]{1,0:T(8,128)(2,1)} custom-call(bf16[2048,128]{1,0:T(8,128)(2,1)} %bitcast.9, bf16[1536,256]{1,0:T(8,128)(2,1)} %constant.41.clone.factors_ref, f32[512,128]{1,0:T(8,128)} %constant.42.clone.turn_ref), custom_call_target="tpu_custom_call" | custom-call | flops 99999997952 | tf_op jit(solution)/shard_map/pallas_call | solution.py:339
  52.8 13.1 %all-to-all-start.1 = ((bf16[64,16,128]{2,1,0:T(8,128)(2,1)}), bf16[64,16,128]{2,1,0:T(8,128)(2,1)S(1)}, u32[]{:S(2)}, u32[]{:S(2)}) async-start(bf16[64,16,128]{2,1,0:T(8,128)(2,1)} %bitcast.11), calls=%async_computation.1 | async-start | bytes 524288 | tf_op jit(solution)/shard_map/all_to_all | solution.py:349
  66.0 0.0 collective-permute-done.1.below_ref
  66.0 0.0 collective-permute-done.3.far_ref
  66.0 0.0 copy-done.2
  66.0 0.1 shard_map.89.refs_3_
  66.1 2.9 %collective-permute-start.6 = (bf16[768,1024]{1,0:T(8,128)(2,1)S(1)}, bf16[768,1024]{1,0:T(8,128)(2,1)S(1)}, u32[]{:S(2)}, u32[]{:S(2)}) collective-permute-start(bf16[768,1024]{1,0:T(8,128)(2,1)S(1)} %shard_map.89.refs_3_), channel_id=1, source_target_pairs={{0,48},{4,196},{1,49},{5,197},{2,50},{6,198},{3,51},{7,199},{8,56}... | collective-permute-start | bytes 4718600 | tf_op jit(solution)/shard_map/ppermute | solution.py:152
  69.0 0.0 collective-permute-start.7
  69.0 1.3 %fusion = (bf16[384,1024]{1,0:T(8,128)(2,1)}, bf16[384,1024]{1,0:T(8,128)(2,1)}) fusion(bf16[768,1024]{1,0:T(8,128)(2,1)S(1)} %shard_map.89.refs_3_), kind=kLoop, calls=%fused_computation.1 | loop fusion | bytes 3145728 | tf_op jit(solution)/shard_map/slice | solution.py:196
  70.3 2.5 %collective-permute-start.5 = (bf16[384,1024]{1,0:T(8,128)(2,1)}, bf16[384,1024]{1,0:T(8,128)(2,1)}, u32[]{:S(2)}, u32[]{:S(2)}) collective-permute-start(bf16[384,1024]{1,0:T(8,128)(2,1)} %get-tuple-element.20), channel_id=1, source_target_pairs={{0,192},{4,52},{1,193},{5,53},{2,194},{6,54},{3,195},{7,55},{8,200... | collective-permute-start | bytes 2359304 | tf_op jit(solution)/shard_map/ppermute | solution.py:152
  72.8 0.0 collective-permute-start.4
  72.8 7.1 %all-to-all-done.1 = bf16[64,16,128]{2,1,0:T(8,128)(2,1)S(1)} async-done(((bf16[64,16,128]{2,1,0:T(8,128)(2,1)}), bf16[64,16,128]{2,1,0:T(8,128)(2,1)S(1)}, u32[]{:S(2)}, u32[]{:S(2)}) %all-to-all-start.1) | async-done | bytes 262176 | tf_op jit(solution)/shard_map/all_to_all | solution.py:349
  79.8 0.0 copy-start
  79.8 1.0 copy-done
  80.9 0.0 copy-start.1
  80.9 1.0 copy-done.1
  81.9 1.0 shard_map.88
  83.0 10.1 %all_to_all.15 = bf16[4,256,128]{2,1,0:T(8,128)(2,1)S(1)} all-to-all(bf16[4,256,128]{2,1,0:T(8,128)(2,1)S(1)} %get-tuple-element.13), channel_id=1, replica_groups=mesh['y'=4,'x'=4,'zh'=2,'core'=2,'chan'=4] {'chan'}, dimensions={0} | all-to-all | bytes 524288 | tf_op jit(solution)/shard_map/all_to_all | solution.py:363
  93.1 2.7 %collective-permute-start = (bf16[1024,128]{1,0:T(8,128)(2,1)S(1)}, bf16[1024,128]{1,0:T(8,128)(2,1)S(1)}, u32[]{:S(2)}, u32[]{:S(2)}) collective-permute-start(bf16[1024,128]{1,0:T(8,128)(2,1)S(1)} %bitcast.6), channel_id=1, source_target_pairs={{0,4},{4,0},{1,5},{5,1},{2,6},{6,2},{3,7},{7,3},{8,12},{12,8},{9,1... | collective-permute-start | bytes 786440 | tf_op jit(solution)/shard_map/ppermute | solution.py:152
  95.8 0.0 collective-permute-done.5.refs_5_
  95.8 0.0 collective-permute-done.4.refs_4_
  95.8 1.2 %collective-permute-done.refs_1_ = bf16[1024,128]{1,0:T(8,128)(2,1)S(1)} collective-permute-done((bf16[1024,128]{1,0:T(8,128)(2,1)S(1)}, bf16[1024,128]{1,0:T(8,128)(2,1)S(1)}, u32[]{:S(2)}, u32[]{:S(2)}) %collective-permute-start) | collective-permute-done | bytes 262176 | tf_op jit(solution)/shard_map/ppermute | solution.py:152
  96.9 3.3 %shard_map.90 = (bf16[128,8192]{1,0:T(8,128)(2,1)}, bf16[128,2048]{1,0:T(8,128)(2,1)S(1)}, bf16[256,1024]{1,0:T(8,128)(2,1)S(1)}) custom-call(bf16[1024,128]{1,0:T(8,128)(2,1)S(1)} %bitcast.7, bf16[1024,128]{1,0:T(8,128)(2,1)S(1)} %collective-permute-done.refs_1_, bf16[256,8192]{1,0:T(8,128)(2,1)} %refs_1_.1, bf16[768,1024]{1,0:T(8,128)(2,1)S(1)} %shard_map.89.refs_3_, ...), custom_call_target="tpu_custom_call" | custom-call | tf_op jit(solution)/shard_map/pallas_call | solution.py:304
  100.2 0.5 collective-permute-start.8
  100.7 0.0 collective-permute-done.6.refs_2_
  100.7 0.0 collective-permute-done.7.refs_3_
  100.7 3.3 %shard_map.91 = (bf16[128,8192]{1,0:T(8,128)(2,1)}, bf16[128,2048]{1,0:T(8,128)(2,1)S(1)}) custom-call(bf16[256,1024]{1,0:T(8,128)(2,1)S(1)} %get-tuple-element.15.refs_0_, bf16[256,8192]{1,0:T(8,128)(2,1)} %refs_1_.1, bf16[768,1024]{1,0:T(8,128)(2,1)S(1)} %collective-permute-done.6.refs_2_, ...), custom_call_target="tpu_custom_call", output_to_operand_aliasing={{0}: (4, {})} | custom-call | tf_op jit(solution)/shard_map/pallas_call | solution.py:304
  104.0 0.4 collective-permute-start.9
  104.4 0.0 collective-permute-done.8.first_ref
  104.4 1.6 %collective-permute-done.9.second_ref = bf16[128,2048]{1,0:T(8,128)(2,1)S(1)} collective-permute-done((bf16[128,2048]{1,0:T(8,128)(2,1)S(1)}, bf16[128,2048]{1,0:T(8,128)(2,1)S(1)}, u32[]{:S(2)}, u32[]{:S(2)}) %collective-permute-start.9) | collective-permute-done | bytes 524320 | tf_op jit(solution)/shard_map/ppermute | solution.py:152
  106.0 1.0 shard_map.92
Async XLA Ops:
  3.7 20.9 %copy-start.4 = (f32[256]{0:T(256)S(1)}, f32[256]{0:T(256)}, u32[]{:S(2)}) copy-start(f32[256]{0:T(256)} %param.10) | copy-start | bytes 3076
  3.7 42.4 %all-to-all-start = ((bf16[64,32,128]{2,1,0:T(8,128)(2,1)}), bf16[64,32,128]{2,1,0:T(8,128)(2,1)S(1)}, u32[]{:S(2)}, u32[]{:S(2)}) async-start(bf16[64,32,128]{2,1,0:T(8,128)(2,1)} %bitcast.10), calls=%async_computation | async-start | bytes 1048576 | tf_op jit(solution)/shard_map/all_to_all | solution.py:336
  20.6 22.8 %collective-permute-start.2 = (bf16[256,1024]{1,0:T(8,128)(2,1)S(1)}, bf16[256,1024]{1,0:T(8,128)(2,1)S(1)}, u32[]{:S(2)}, u32[]{:S(2)}) collective-permute-start(bf16[256,1024]{1,0:T(8,128)(2,1)S(1)} %constant_dynamic-slice_fusion), channel_id=1, source_target_pairs={{0,11},{4,15},{1,0},{5,4},{2,1},{6,5},{3,2},{7,6},{8,3},{12,7},{9,... | collective-permute-start | bytes 1572872 | tf_op jit(solution)/shard_map/ppermute | solution.py:152
  24.6 41.3 %collective-permute-start.1 = (bf16[256,1024]{1,0:T(8,128)(2,1)S(1)}, bf16[256,1024]{1,0:T(8,128)(2,1)S(1)}, u32[]{:S(2)}, u32[]{:S(2)}) collective-permute-start(bf16[256,1024]{1,0:T(8,128)(2,1)S(1)} %constant_dynamic-slice_fusion), channel_id=1, source_target_pairs={{0,1},{4,5},{1,2},{5,6},{2,3},{6,7},{3,8},{7,12},{8,9},{12,13},{9,... | collective-permute-start | bytes 1572872 | tf_op jit(solution)/shard_map/ppermute | solution.py:152
  43.4 22.6 %collective-permute-start.3 = (bf16[256,1024]{1,0:T(8,128)(2,1)S(1)}, bf16[256,1024]{1,0:T(8,128)(2,1)S(1)}, u32[]{:S(2)}, u32[]{:S(2)}) collective-permute-start(bf16[256,1024]{1,0:T(8,128)(2,1)S(1)} %collective-permute-done.2.above_ref), channel_id=1, source_target_pairs={{0,11},{4,15},{1,0},{5,4},{2,1},{6,5},{3,2},{7,6},{8,3},{12,7},{9,... | collective-permute-start | bytes 1572872 | tf_op jit(solution)/shard_map/ppermute | solution.py:152
  46.1 0.8 copy-start.3
  46.9 19.1 %copy-start.2 = (f32[8,128]{1,0:T(8,128)S(1)}, f32[8,128]{1,0:T(8,128)}, u32[]{:S(2)}) copy-start(f32[8,128]{1,0:T(8,128)} %get-tuple-element.14.after_ref) | copy-start | bytes 12292
  52.8 27.0 %all-to-all-start.1 = ((bf16[64,16,128]{2,1,0:T(8,128)(2,1)}), bf16[64,16,128]{2,1,0:T(8,128)(2,1)S(1)}, u32[]{:S(2)}, u32[]{:S(2)}) async-start(bf16[64,16,128]{2,1,0:T(8,128)(2,1)} %bitcast.11), calls=%async_computation.1 | async-start | bytes 524288 | tf_op jit(solution)/shard_map/all_to_all | solution.py:349
  66.1 34.6 %collective-permute-start.6 = (bf16[768,1024]{1,0:T(8,128)(2,1)S(1)}, bf16[768,1024]{1,0:T(8,128)(2,1)S(1)}, u32[]{:S(2)}, u32[]{:S(2)}) collective-permute-start(bf16[768,1024]{1,0:T(8,128)(2,1)S(1)} %shard_map.89.refs_3_), channel_id=1, source_target_pairs={{0,48},{4,196},{1,49},{5,197},{2,50},{6,198},{3,51},{7,199},{8,56}... | collective-permute-start | bytes 4718600 | tf_op jit(solution)/shard_map/ppermute | solution.py:152
  69.0 31.7 %collective-permute-start.7 = (bf16[768,1024]{1,0:T(8,128)(2,1)S(1)}, bf16[768,1024]{1,0:T(8,128)(2,1)}, u32[]{:S(2)}, u32[]{:S(2)}) collective-permute-start(bf16[768,1024]{1,0:T(8,128)(2,1)S(1)} %shard_map.89.refs_3_), channel_id=1, source_target_pairs={{0,16},{4,68},{1,17},{5,69},{2,18},{6,70},{3,19},{7,71},{8,24},{12... | collective-permute-start | bytes 4718600 | tf_op jit(solution)/shard_map/ppermute | solution.py:152
  70.3 25.5 %collective-permute-start.5 = (bf16[384,1024]{1,0:T(8,128)(2,1)}, bf16[384,1024]{1,0:T(8,128)(2,1)}, u32[]{:S(2)}, u32[]{:S(2)}) collective-permute-start(bf16[384,1024]{1,0:T(8,128)(2,1)} %get-tuple-element.20), channel_id=1, source_target_pairs={{0,192},{4,52},{1,193},{5,53},{2,194},{6,54},{3,195},{7,55},{8,200... | collective-permute-start | bytes 2359304 | tf_op jit(solution)/shard_map/ppermute | solution.py:152
  72.8 23.0 %collective-permute-start.4 = (bf16[384,1024]{1,0:T(8,128)(2,1)}, bf16[384,1024]{1,0:T(8,128)(2,1)}, u32[]{:S(2)}, u32[]{:S(2)}) collective-permute-start(bf16[384,1024]{1,0:T(8,128)(2,1)} %get-tuple-element.21), channel_id=1, source_target_pairs={{0,64},{4,20},{1,65},{5,21},{2,66},{6,22},{3,67},{7,23},{8,72},{12... | collective-permute-start | bytes 2359304 | tf_op jit(solution)/shard_map/ppermute | solution.py:152
  79.8 1.0 copy-start
  80.9 1.0 copy-start.1
  93.1 3.9 %collective-permute-start = (bf16[1024,128]{1,0:T(8,128)(2,1)S(1)}, bf16[1024,128]{1,0:T(8,128)(2,1)S(1)}, u32[]{:S(2)}, u32[]{:S(2)}) collective-permute-start(bf16[1024,128]{1,0:T(8,128)(2,1)S(1)} %bitcast.6), channel_id=1, source_target_pairs={{0,4},{4,0},{1,5},{5,1},{2,6},{6,2},{3,7},{7,3},{8,12},{12,8},{9,1... | collective-permute-start | bytes 786440 | tf_op jit(solution)/shard_map/ppermute | solution.py:152
  100.2 4.2 %collective-permute-start.8 = (bf16[128,2048]{1,0:T(8,128)(2,1)S(1)}, bf16[128,2048]{1,0:T(8,128)(2,1)S(1)}, u32[]{:S(2)}, u32[]{:S(2)}) collective-permute-start(bf16[128,2048]{1,0:T(8,128)(2,1)S(1)} %get-tuple-element.18), channel_id=1, source_target_pairs={{0,4},{4,0},{1,5},{5,1},{2,6},{6,2},{3,7},{7,3},{8,12},{12,8},{9,1... | collective-permute-start | bytes 1572872 | tf_op jit(solution)/shard_map/ppermute | solution.py:152
  104.0 2.0 %collective-permute-start.9 = (bf16[128,2048]{1,0:T(8,128)(2,1)S(1)}, bf16[128,2048]{1,0:T(8,128)(2,1)S(1)}, u32[]{:S(2)}, u32[]{:S(2)}) collective-permute-start(bf16[128,2048]{1,0:T(8,128)(2,1)S(1)} %get-tuple-element.19), channel_id=1, source_target_pairs={{0,4},{4,0},{1,5},{5,1},{2,6},{6,2},{3,7},{7,3},{8,12},{12,8},{9,1... | collective-permute-start | bytes 1572872 | tf_op jit(solution)/shard_map/ppermute | solution.py:152

commit v12 on v10

--- a/solution.py
+++ b/solution.py
@@ -49,7 +49,10 @@
     return narrow(factors), np.concatenate([turn.real, turn.imag], 0).astype(np.float32)
 
 
-def pack_kernel(signal_ref, filter_ref, out_ref, token_ref, wide):
+def pack_kernel(signal_ref, filter_ref, own_ref, out_ref, token_ref, mine_ref, wide, sem):
+    core = lax.axis_index("core")
+    slice_copy = pltpu.make_async_copy(own_ref.at[:, pl.ds(place_of(core, 0), QUARTER)], mine_ref, sem)
+    slice_copy.start()
     for which, source in enumerate((signal_ref, filter_ref)):
         for own in range(OWN_CHANNELS):
             for piece in range(PIECES):
@@ -59,6 +62,7 @@
                     piece * LANES : (piece + 1) * LANES,
                 ]
     out_ref[...] = wide[...].astype(jnp.bfloat16)
+    slice_copy.wait()
 
 
 def matmul(left, right):
@@ -173,10 +177,7 @@
 TOKEN = jax.ShapeDtypeStruct((8, LANES), jnp.float32)
 
 
-def first_quarter(out_weight):
-    core = lax.axis_index("core")
-    start = core * HALF + colour(core) * QUARTER
-    mine = lax.dynamic_slice_in_dim(out_weight, start, QUARTER, 1)
+def first_quarter(mine):
     below = moved(mine, lambda y, x, z, c: (y, x, z + 1, c))
     above = moved(mine, lambda y, x, z, c: (y, x, z - 1, c))
     far = moved(mine, lambda y, x, z, c: (y, x, z + 2 - 4 * c, c))
@@ -322,16 +323,20 @@
 
 
 def body(signal, gate, filter_taps, skip_weight, out_weight):
-    parts = first_quarter(out_weight)
     tables = transform_tables()
-    packed, packed_token = call(
+    packed, packed_token, mine = call(
         pack_kernel,
-        (jax.ShapeDtypeStruct((SEQ_DEVICES * 32, LANES), jnp.bfloat16), TOKEN),
-        [pltpu.VMEM((SEQ_DEVICES * 32, LANES), jnp.float32)],
+        (
+            jax.ShapeDtypeStruct((SEQ_DEVICES * 32, LANES), jnp.bfloat16),
+            TOKEN,
+            jax.ShapeDtypeStruct((ROWS, QUARTER), jnp.bfloat16),
+        ),
+        [pltpu.VMEM((SEQ_DEVICES * 32, LANES), jnp.float32), pltpu.SemaphoreType.DMA(())],
         work=PACK_WORK,
-        in_specs=[INSIDE] * 2,
-        out_specs=(INSIDE, ANYWHERE),
-    )(signal, filter_taps)
+        in_specs=[INSIDE] * 2 + [ANYWHERE],
+        out_specs=(INSIDE, ANYWHERE, ANYWHERE),
+    )(signal, filter_taps, out_weight)
+    parts = first_quarter(mine)
     blocks = other_quarters(parts, packed_token)
     arrived = lax.all_to_all(
         packed.reshape(SEQ_DEVICES, 32, LANES), AXES, split_axis=0, concat_axis=0, tiled=True

time: 99.3 us -> 116 us (1.17)
  Pallas kernels: 17.7 us -> 33.6 us
    pallas_call x1, Pallas kernels: 3.09 us -> 19 us  [body(): call(pack_kernel, (jax.ShapeDtypeStruct((SEQ_DEVICES * 32, LANES), jnp.bf...]
    ppermute x10, waiting for transfers between devices: 6.09 us -> 8.73 us  [moved(): return lax.ppermute(array, (*AXES, 'chan'), device_pairs(move))]
  transfers between devices with their start and end apart: 12 -> 12, of which waited for: 5 -> 6; matrix products, arithmetic and copies ran while one was open for 3% -> 1% of each run, Pallas kernels for 14% -> 12%
where the time goes in v12:
time: 116 us; the launch traced here: 115 us
  starting transfers between devices  37.3 us (32%)
  Pallas kernels  33.6 us (29%)
  waiting for transfers between devices  27 us (23%)
  blocking collectives  12 us (10%)
  local copies, waits for them, and re-layouts  4.27 us (4%)
    pallas_call x1, Pallas kernels, body(): call(pack_kernel, (jax.ShapeDtypeStruct((SEQ_DEVICES * 32, LANES), jnp.bf...  19 us
    ppermute x10, starting transfers between devices, moved(): return lax.ppermute(array, (*AXES, 'chan'), device_pairs(move))  17.5 us
    all_to_all x1, starting transfers between devices, body(): lax.all_to_all(packed.reshape(SEQ_DEVICES, 32, LANES), AXES, split_axis=0...  15.6 us
    all_to_all x1, waiting for transfers between devices, body(): lax.all_to_all(packed.reshape(SEQ_DEVICES, 32, LANES), AXES, split_axis=0...  13.6 us
    all_to_all x1, blocking collectives, body(): lax.all_to_all(rounded, 'chan', split_axis=0, concat_axis=0, tiled=True)  12 us
    ppermute x10, waiting for transfers between devices, moved(): return lax.ppermute(array, (*AXES, 'chan'), device_pairs(move))  8.73 us
    pallas_call x2, Pallas kernels, projected_quarters(): call(functools.partial(project_kernel, quarters, len(columns)), tuple(sha...  6.55 us
    pallas_call x1, Pallas kernels, body(): call(convolve_kernel, jax.ShapeDtypeStruct((SEQ_DEVICES * 16, LANES), jnp...  5.91 us
  transfers between devices with their start and end apart: 12, of which 6 were waited for; matrix products, arithmetic and copies ran while one was open for 1% of the time, Pallas kernels for 12%

profile of v12, /device:TPU:1, one launch (start us, length us, event | category | flops | bytes accessed | tf_op | source)
XLA Modules:
  0.0 115.0 jit_solution(2855271164934436922)
XLA Ops:
  0.6 0.0 copy-start.4
  0.6 19.0 %shard_map.86 = (bf16[2048,128]{1,0:T(8,128)(2,1)}, f32[8,128]{1,0:T(8,128)}, bf16[256,1024]{1,0:T(8,128)(2,1)}) custom-call(f32[256,512]{1,0:T(8,128)} %signal_ref.3, f32[256,512]{1,0:T(8,128)} %filter_ref.1, bf16[256,8192]{1,0:T(8,128)(2,1)} %refs_1_.1), custom_call_target="tpu_custom_call" | custom-call | flops 10000000000 | tf_op jit(solution)/shard_map/pallas_call | solution.py:327
  19.6 15.6 %all-to-all-start = ((bf16[64,32,128]{2,1,0:T(8,128)(2,1)}), bf16[64,32,128]{2,1,0:T(8,128)(2,1)S(1)}, u32[]{:S(2)}, u32[]{:S(2)}) async-start(bf16[64,32,128]{2,1,0:T(8,128)(2,1)} %bitcast.10), calls=%async_computation | async-start | bytes 1048576 | tf_op jit(solution)/shard_map/all_to_all | solution.py:341
  35.3 4.5 %collective-permute-start.3 = (bf16[256,1024]{1,0:T(8,128)(2,1)}, bf16[256,1024]{1,0:T(8,128)(2,1)S(1)}, u32[]{:S(2)}, u32[]{:S(2)}) collective-permute-start(bf16[256,1024]{1,0:T(8,128)(2,1)} %get-tuple-element.15), channel_id=1, source_target_pairs={{0,2},{4,14},{1,3},{5,15},{2,8},{6,4},{3,9},{7,5},{8,10},{12,6},{9... | collective-permute-start | bytes 1572872 | tf_op jit(solution)/shard_map/ppermute | solution.py:156
  39.8 0.7 collective-permute-start.2
  40.5 0.7 collective-permute-start.1
  41.2 0.0 copy-done.4
  41.2 0.1 copy.11.skip_ref
  41.4 13.6 %all-to-all-done = bf16[64,32,128]{2,1,0:T(8,128)(2,1)S(1)} async-done(((bf16[64,32,128]{2,1,0:T(8,128)(2,1)}), bf16[64,32,128]{2,1,0:T(8,128)(2,1)S(1)}, u32[]{:S(2)}, u32[]{:S(2)}) %all-to-all-start) | async-done | bytes 524320 | tf_op jit(solution)/shard_map/all_to_all | solution.py:341
  55.0 0.0 copy-start.3
  55.0 0.8 copy-done.3
  55.7 0.0 copy-start.2
  55.8 5.9 %shard_map.87 = bf16[1024,128]{1,0:T(8,128)(2,1)} custom-call(bf16[2048,128]{1,0:T(8,128)(2,1)} %bitcast.9, bf16[1536,256]{1,0:T(8,128)(2,1)} %constant.4.clone.factors_ref, f32[512,128]{1,0:T(8,128)} %constant.5.clone.turn_ref), custom_call_target="tpu_custom_call" | custom-call | flops 99999997952 | tf_op jit(solution)/shard_map/pallas_call | solution.py:344
  61.7 4.2 %all-to-all-start.1 = ((bf16[64,16,128]{2,1,0:T(8,128)(2,1)}), bf16[64,16,128]{2,1,0:T(8,128)(2,1)S(1)}, u32[]{:S(2)}, u32[]{:S(2)}) async-start(bf16[64,16,128]{2,1,0:T(8,128)(2,1)} %bitcast.11), calls=%async_computation.1 | async-start | bytes 524288 | tf_op jit(solution)/shard_map/all_to_all | solution.py:354
  65.8 0.2 collective-permute-done.3.far_ref
  66.0 5.6 %collective-permute-done.2.above_ref = bf16[256,1024]{1,0:T(8,128)(2,1)S(1)} collective-permute-done((bf16[256,1024]{1,0:T(8,128)(2,1)}, bf16[256,1024]{1,0:T(8,128)(2,1)S(1)}, u32[]{:S(2)}, u32[]{:S(2)}) %collective-permute-start.2) | collective-permute-done | bytes 524320 | tf_op jit(solution)/shard_map/ppermute | solution.py:156
  71.6 0.0 collective-permute-done.1.below_ref
  71.6 0.0 copy-done.2
  71.6 0.1 shard_map.89.refs_3_
  71.7 3.0 %collective-permute-start.6 = (bf16[768,1024]{1,0:T(8,128)(2,1)S(1)}, bf16[768,1024]{1,0:T(8,128)(2,1)S(1)}, u32[]{:S(2)}, u32[]{:S(2)}) collective-permute-start(bf16[768,1024]{1,0:T(8,128)(2,1)S(1)} %shard_map.89.refs_3_), channel_id=1, source_target_pairs={{0,48},{4,196},{1,49},{5,197},{2,50},{6,198},{3,51},{7,199},{8,56}... | collective-permute-start | bytes 4718600 | tf_op jit(solution)/shard_map/ppermute | solution.py:156
  74.7 0.0 collective-permute-start.7
  74.7 1.3 %fusion = (bf16[384,1024]{1,0:T(8,128)(2,1)}, bf16[384,1024]{1,0:T(8,128)(2,1)}) fusion(bf16[768,1024]{1,0:T(8,128)(2,1)S(1)} %shard_map.89.refs_3_), kind=kLoop, calls=%fused_computation | loop fusion | bytes 3145728 | tf_op jit(solution)/shard_map/slice | solution.py:197
  75.9 2.5 %collective-permute-start.5 = (bf16[384,1024]{1,0:T(8,128)(2,1)}, bf16[384,1024]{1,0:T(8,128)(2,1)}, u32[]{:S(2)}, u32[]{:S(2)}) collective-permute-start(bf16[384,1024]{1,0:T(8,128)(2,1)} %get-tuple-element.22), channel_id=1, source_target_pairs={{0,192},{4,52},{1,193},{5,53},{2,194},{6,54},{3,195},{7,55},{8,200... | collective-permute-start | bytes 2359304 | tf_op jit(solution)/shard_map/ppermute | solution.py:156
  78.4 0.0 collective-permute-start.4
  78.4 4.7 %all-to-all-done.1 = bf16[64,16,128]{2,1,0:T(8,128)(2,1)S(1)} async-done(((bf16[64,16,128]{2,1,0:T(8,128)(2,1)}), bf16[64,16,128]{2,1,0:T(8,128)(2,1)S(1)}, u32[]{:S(2)}, u32[]{:S(2)}) %all-to-all-start.1) | async-done | bytes 262176 | tf_op jit(solution)/shard_map/all_to_all | solution.py:354
  83.1 0.0 copy-start
  83.1 1.0 copy-done
  84.2 0.0 copy-start.1
  84.2 1.0 copy-done.1
  85.2 1.0 shard_map.88
  86.2 12.0 %all_to_all.15 = bf16[4,256,128]{2,1,0:T(8,128)(2,1)S(1)} all-to-all(bf16[4,256,128]{2,1,0:T(8,128)(2,1)S(1)} %get-tuple-element.14), channel_id=1, replica_groups=mesh['y'=4,'x'=4,'zh'=2,'core'=2,'chan'=4] {'chan'}, dimensions={0} | all-to-all | bytes 524288 | tf_op jit(solution)/shard_map/all_to_all | solution.py:368
  98.2 2.7 %collective-permute-start = (bf16[1024,128]{1,0:T(8,128)(2,1)S(1)}, bf16[1024,128]{1,0:T(8,128)(2,1)S(1)}, u32[]{:S(2)}, u32[]{:S(2)}) collective-permute-start(bf16[1024,128]{1,0:T(8,128)(2,1)S(1)} %bitcast.6), channel_id=1, source_target_pairs={{0,4},{4,0},{1,5},{5,1},{2,6},{6,2},{3,7},{7,3},{8,12},{12,8},{9,1... | collective-permute-start | bytes 786440 | tf_op jit(solution)/shard_map/ppermute | solution.py:156
  100.9 0.0 collective-permute-done.5.refs_5_
  100.9 0.0 collective-permute-done.4.refs_4_
  100.9 1.2 %collective-permute-done.refs_1_ = bf16[1024,128]{1,0:T(8,128)(2,1)S(1)} collective-permute-done((bf16[1024,128]{1,0:T(8,128)(2,1)S(1)}, bf16[1024,128]{1,0:T(8,128)(2,1)S(1)}, u32[]{:S(2)}, u32[]{:S(2)}) %collective-permute-start) | collective-permute-done | bytes 262176 | tf_op jit(solution)/shard_map/ppermute | solution.py:156
  102.1 3.3 %shard_map.90 = (bf16[128,8192]{1,0:T(8,128)(2,1)}, bf16[128,2048]{1,0:T(8,128)(2,1)S(1)}, bf16[256,1024]{1,0:T(8,128)(2,1)S(1)}) custom-call(bf16[1024,128]{1,0:T(8,128)(2,1)S(1)} %bitcast.7, bf16[1024,128]{1,0:T(8,128)(2,1)S(1)} %collective-permute-done.refs_1_, bf16[256,8192]{1,0:T(8,128)(2,1)} %refs_1_.1, bf16[768,1024]{1,0:T(8,128)(2,1)S(1)} %shard_map.89.refs_3_, ...), custom_call_target="tpu_custom_call" | custom-call | tf_op jit(solution)/shard_map/pallas_call | solution.py:305
  105.4 3.2 %collective-permute-start.8 = (bf16[128,2048]{1,0:T(8,128)(2,1)S(1)}, bf16[128,2048]{1,0:T(8,128)(2,1)S(1)}, u32[]{:S(2)}, u32[]{:S(2)}) collective-permute-start(bf16[128,2048]{1,0:T(8,128)(2,1)S(1)} %get-tuple-element.20), channel_id=1, source_target_pairs={{0,4},{4,0},{1,5},{5,1},{2,6},{6,2},{3,7},{7,3},{8,12},{12,8},{9,1... | collective-permute-start | bytes 1572872 | tf_op jit(solution)/shard_map/ppermute | solution.py:156
  108.6 0.0 collective-permute-done.6.refs_2_
  108.6 0.0 collective-permute-done.7.refs_3_
  108.6 3.3 %shard_map.91 = (bf16[128,8192]{1,0:T(8,128)(2,1)}, bf16[128,2048]{1,0:T(8,128)(2,1)S(1)}) custom-call(bf16[256,1024]{1,0:T(8,128)(2,1)S(1)} %get-tuple-element.17.refs_0_, bf16[256,8192]{1,0:T(8,128)(2,1)} %refs_1_.1, bf16[768,1024]{1,0:T(8,128)(2,1)S(1)} %collective-permute-done.6.refs_2_, ...), custom_call_target="tpu_custom_call", output_to_operand_aliasing={{0}: (4, {})} | custom-call | tf_op jit(solution)/shard_map/pallas_call | solution.py:305
  111.9 0.1 collective-permute-start.9
  112.0 0.0 collective-permute-done.8.first_ref
  112.0 1.8 %collective-permute-done.9.second_ref = bf16[128,2048]{1,0:T(8,128)(2,1)S(1)} collective-permute-done((bf16[128,2048]{1,0:T(8,128)(2,1)S(1)}, bf16[128,2048]{1,0:T(8,128)(2,1)S(1)}, u32[]{:S(2)}, u32[]{:S(2)}) %collective-permute-start.9) | collective-permute-done | bytes 524320 | tf_op jit(solution)/shard_map/ppermute | solution.py:156
  113.9 1.0 shard_map.92
Async XLA Ops:
  0.6 40.6 %copy-start.4 = (f32[256]{0:T(256)S(1)}, f32[256]{0:T(256)}, u32[]{:S(2)}) copy-start(f32[256]{0:T(256)} %param.10) | copy-start | bytes 3076
  19.6 35.3 %all-to-all-start = ((bf16[64,32,128]{2,1,0:T(8,128)(2,1)}), bf16[64,32,128]{2,1,0:T(8,128)(2,1)S(1)}, u32[]{:S(2)}, u32[]{:S(2)}) async-start(bf16[64,32,128]{2,1,0:T(8,128)(2,1)} %bitcast.10), calls=%async_computation | async-start | bytes 1048576 | tf_op jit(solution)/shard_map/all_to_all | solution.py:341
  35.3 30.7 %collective-permute-start.3 = (bf16[256,1024]{1,0:T(8,128)(2,1)}, bf16[256,1024]{1,0:T(8,128)(2,1)S(1)}, u32[]{:S(2)}, u32[]{:S(2)}) collective-permute-start(bf16[256,1024]{1,0:T(8,128)(2,1)} %get-tuple-element.15), channel_id=1, source_target_pairs={{0,2},{4,14},{1,3},{5,15},{2,8},{6,4},{3,9},{7,5},{8,10},{12,6},{9... | collective-permute-start | bytes 1572872 | tf_op jit(solution)/shard_map/ppermute | solution.py:156
  39.8 31.8 %collective-permute-start.2 = (bf16[256,1024]{1,0:T(8,128)(2,1)}, bf16[256,1024]{1,0:T(8,128)(2,1)S(1)}, u32[]{:S(2)}, u32[]{:S(2)}) collective-permute-start(bf16[256,1024]{1,0:T(8,128)(2,1)} %get-tuple-element.15), channel_id=1, source_target_pairs={{0,11},{4,15},{1,0},{5,4},{2,1},{6,5},{3,2},{7,6},{8,3},{12,7},{9,... | collective-permute-start | bytes 1572872 | tf_op jit(solution)/shard_map/ppermute | solution.py:156
  40.5 31.1 %collective-permute-start.1 = (bf16[256,1024]{1,0:T(8,128)(2,1)}, bf16[256,1024]{1,0:T(8,128)(2,1)S(1)}, u32[]{:S(2)}, u32[]{:S(2)}) collective-permute-start(bf16[256,1024]{1,0:T(8,128)(2,1)} %get-tuple-element.15), channel_id=1, source_target_pairs={{0,1},{4,5},{1,2},{5,6},{2,3},{6,7},{3,8},{7,12},{8,9},{12,13},{9,... | collective-permute-start | bytes 1572872 | tf_op jit(solution)/shard_map/ppermute | solution.py:156
  55.0 0.8 copy-start.3
  55.7 15.8 %copy-start.2 = (f32[8,128]{1,0:T(8,128)S(1)}, f32[8,128]{1,0:T(8,128)}, u32[]{:S(2)}) copy-start(f32[8,128]{1,0:T(8,128)} %get-tuple-element.16.after_ref) | copy-start | bytes 12292
  61.7 21.5 %all-to-all-start.1 = ((bf16[64,16,128]{2,1,0:T(8,128)(2,1)}), bf16[64,16,128]{2,1,0:T(8,128)(2,1)S(1)}, u32[]{:S(2)}, u32[]{:S(2)}) async-start(bf16[64,16,128]{2,1,0:T(8,128)(2,1)} %bitcast.11), calls=%async_computation.1 | async-start | bytes 524288 | tf_op jit(solution)/shard_map/all_to_all | solution.py:354
  71.7 36.9 %collective-permute-start.6 = (bf16[768,1024]{1,0:T(8,128)(2,1)S(1)}, bf16[768,1024]{1,0:T(8,128)(2,1)S(1)}, u32[]{:S(2)}, u32[]{:S(2)}) collective-permute-start(bf16[768,1024]{1,0:T(8,128)(2,1)S(1)} %shard_map.89.refs_3_), channel_id=1, source_target_pairs={{0,48},{4,196},{1,49},{5,197},{2,50},{6,198},{3,51},{7,199},{8,56}... | collective-permute-start | bytes 4718600 | tf_op jit(solution)/shard_map/ppermute | solution.py:156
  74.7 33.9 %collective-permute-start.7 = (bf16[768,1024]{1,0:T(8,128)(2,1)S(1)}, bf16[768,1024]{1,0:T(8,128)(2,1)}, u32[]{:S(2)}, u32[]{:S(2)}) collective-permute-start(bf16[768,1024]{1,0:T(8,128)(2,1)S(1)} %shard_map.89.refs_3_), channel_id=1, source_target_pairs={{0,16},{4,68},{1,17},{5,69},{2,18},{6,70},{3,19},{7,71},{8,24},{12... | collective-permute-start | bytes 4718600 | tf_op jit(solution)/shard_map/ppermute | solution.py:156
  75.9 25.0 %collective-permute-start.5 = (bf16[384,1024]{1,0:T(8,128)(2,1)}, bf16[384,1024]{1,0:T(8,128)(2,1)}, u32[]{:S(2)}, u32[]{:S(2)}) collective-permute-start(bf16[384,1024]{1,0:T(8,128)(2,1)} %get-tuple-element.22), channel_id=1, source_target_pairs={{0,192},{4,52},{1,193},{5,53},{2,194},{6,54},{3,195},{7,55},{8,200... | collective-permute-start | bytes 2359304 | tf_op jit(solution)/shard_map/ppermute | solution.py:156
  78.4 22.5 %collective-permute-start.4 = (bf16[384,1024]{1,0:T(8,128)(2,1)}, bf16[384,1024]{1,0:T(8,128)(2,1)}, u32[]{:S(2)}, u32[]{:S(2)}) collective-permute-start(bf16[384,1024]{1,0:T(8,128)(2,1)} %get-tuple-element.23), channel_id=1, source_target_pairs={{0,64},{4,20},{1,65},{5,21},{2,66},{6,22},{3,67},{7,23},{8,72},{12... | collective-permute-start | bytes 2359304 | tf_op jit(solution)/shard_map/ppermute | solution.py:156
  83.1 1.0 copy-start
  84.2 1.0 copy-start.1
  98.2 3.9 %collective-permute-start = (bf16[1024,128]{1,0:T(8,128)(2,1)S(1)}, bf16[1024,128]{1,0:T(8,128)(2,1)S(1)}, u32[]{:S(2)}, u32[]{:S(2)}) collective-permute-start(bf16[1024,128]{1,0:T(8,128)(2,1)S(1)} %bitcast.6), channel_id=1, source_target_pairs={{0,4},{4,0},{1,5},{5,1},{2,6},{6,2},{3,7},{7,3},{8,12},{12,8},{9,1... | collective-permute-start | bytes 786440 | tf_op jit(solution)/shard_map/ppermute | solution.py:156
  105.4 6.7 %collective-permute-start.8 = (bf16[128,2048]{1,0:T(8,128)(2,1)S(1)}, bf16[128,2048]{1,0:T(8,128)(2,1)S(1)}, u32[]{:S(2)}, u32[]{:S(2)}) collective-permute-start(bf16[128,2048]{1,0:T(8,128)(2,1)S(1)} %get-tuple-element.20), channel_id=1, source_target_pairs={{0,4},{4,0},{1,5},{5,1},{2,6},{6,2},{3,7},{7,3},{8,12},{12,8},{9,1... | collective-permute-start | bytes 1572872 | tf_op jit(solution)/shard_map/ppermute | solution.py:156
  111.9 2.0 %collective-permute-start.9 = (bf16[128,2048]{1,0:T(8,128)(2,1)S(1)}, bf16[128,2048]{1,0:T(8,128)(2,1)S(1)}, u32[]{:S(2)}, u32[]{:S(2)}) collective-permute-start(bf16[128,2048]{1,0:T(8,128)(2,1)S(1)} %get-tuple-element.21), channel_id=1, source_target_pairs={{0,4},{4,0},{1,5},{5,1},{2,6},{6,2},{3,7},{7,3},{8,12},{12,8},{9,1... | collective-permute-start | bytes 1572872 | tf_op jit(solution)/shard_map/ppermute | solution.py:156
